TPU v7x, 32 devices: a whole 2x2x4 slice. The times are simulated.
32 devices in a mesh: ctx: 4 (over z), exp: 2 (over x), tp: 4 (over y, core).
Axes of the slice: x: 2, y: 2, z: 4, core: 2. Of those that a mesh axis runs over, the one named last changes fastest.
Arguments:
- queries: bfloat16 [4096, 4096], P(('ctx', 'exp'), 'tp'), may hold values from -6 to 6
- key_vectors: bfloat16 [4096, 4096], P(('ctx', 'exp'), 'tp'), may hold values from -6 to 6
- value_vectors: bfloat16 [4096, 4096], P(('ctx', 'exp'), 'tp'), may hold values from -6 to 6
- decay_rate: float32 [32], P('tp'), may hold values from 1e-07 to 0.05
- norm_gain: float32 [4096], P('tp'), may hold values from 0.5 to 1.5
Outputs:
- normed: bfloat16 [4096, 4096], P(('ctx', 'exp'), 'tp')
All inputs are finite; a program needn't handle non-finite values.
Results may differ from a plain program's by a relative error of at most 0.0052.
Values sent between devices are 32-bit elements; how exact they have to be, the bound alone decides.
No kernel may reach another device: no remote copies, remote signals or barrier semaphores. Data moves between devices by JAX's collectives and lax.ppermute only.
A program may use at most 128 MiB of HBM per device.

v0:
```python
import jax
import jax.numpy as jnp
from jax import lax
from jax.sharding import PartitionSpec as P

HEADS = 32
HEAD_DIM = 128
BLK = 256


def carried_in(value, axis, join, neutral):
    count, mine = (lax.axis_size(axis), lax.axis_index(axis))
    pieces = jax.tree.map(lambda part: lax.all_gather(part, axis), value)
    subtotal = jax.tree.map(
        lambda part, zero: jnp.full_like(part, 0) + jnp.asarray(zero, part.dtype), value, neutral
    )

    def hop(position, subtotal):
        longer = join(subtotal, jax.tree.map(lambda part: part[position], pieces))
        return jax.tree.map(lambda new, old: jnp.where(position < mine, new, old), longer, subtotal)

    return lax.fori_loop(0, count - 1, hop, subtotal)


def chain_step(earlier, later):
    decay_early, state_early = earlier
    decay_late, state_late = later
    return (decay_early * decay_late, decay_late[:, None, None] * state_early + state_late)


def local(queries, key_vectors, value_vectors, decay_rate, norm_gain):
    row_count = queries.shape[0]
    head_local = decay_rate.shape[0]
    block_count = row_count // BLK
    query_blocks = queries.reshape(block_count, BLK, head_local, HEAD_DIM)
    key_blocks = key_vectors.reshape(block_count, BLK, head_local, HEAD_DIM)
    value_blocks = value_vectors.reshape(block_count, BLK, head_local, HEAD_DIM)
    offsets = jnp.arange(BLK, dtype=jnp.float32)
    spread = offsets[:, None] - offsets[None, :]
    causal = spread >= 0
    rates = decay_rate[:, None, None]
    weight = jnp.where(causal[None], jnp.exp(-rates * jnp.maximum(spread, 0.0)[None]), 0.0)
    inner_decay = jnp.exp(-decay_rate[None, :] * offsets[:, None])
    tail_decay = jnp.exp(-decay_rate[None, :] * (BLK - offsets)[:, None])
    block_decay = jnp.exp(-decay_rate * BLK)[:, None, None]
    local_parts = []
    block_terms = []
    own_state = jnp.zeros((head_local, HEAD_DIM, HEAD_DIM), jnp.float32)
    for block_index in range(block_count):
        query_block = query_blocks[block_index]
        key_block = key_blocks[block_index]
        value_block = value_blocks[block_index]
        scores = jnp.einsum(
            "thd,shd->hts", query_block, key_block, preferred_element_type=jnp.float32
        )
        mixing = (scores * weight).astype(jnp.bfloat16)
        local_parts.append(
            jnp.einsum("hts,she->the", mixing, value_block, preferred_element_type=jnp.float32)
        )
        scaled_keys = (key_block.astype(jnp.float32) * tail_decay[:, :, None]).astype(jnp.bfloat16)
        block_term = jnp.einsum(
            "shd,she->hde", scaled_keys, value_block, preferred_element_type=jnp.float32
        )
        block_terms.append(block_term)
        own_state = block_decay * own_state + block_term
    span_decay = jnp.exp(-decay_rate * row_count)
    identity = (jnp.ones_like(span_decay), jnp.zeros_like(own_state))
    unused, before = carried_in((span_decay, own_state), ("ctx", "exp"), chain_step, identity)
    carry_state = before
    pieces = []
    for block_index in range(block_count):
        state_low = carry_state.astype(jnp.bfloat16)
        carried = jnp.einsum(
            "thd,hde->the", query_blocks[block_index], state_low, preferred_element_type=jnp.float32
        )
        pieces.append(local_parts[block_index] + carried * inner_decay[:, :, None])
        carry_state = block_decay * carry_state + block_terms[block_index]
    attended = jnp.concatenate(pieces, axis=0).reshape(row_count, head_local * HEAD_DIM)
    row_squares = jnp.sum(attended * attended, axis=1)
    row_total = lax.psum(row_squares, "tp")
    mean_square = row_total / (HEADS * HEAD_DIM)
    normed = attended * lax.rsqrt(mean_square + 1e-06)[:, None] * norm_gain[None, :]
    return normed.astype(jnp.bfloat16)


def solution(mesh):
    return jax.shard_map(
        local,
        mesh=mesh,
        in_specs=(
            P(("ctx", "exp"), "tp"),
            P(("ctx", "exp"), "tp"),
            P(("ctx", "exp"), "tp"),
            P("tp"),
            P("tp"),
        ),
        out_specs=P(("ctx", "exp"), "tp"),
        check_vma=False,
    )
```

profile of v0, /device:TPU:0, one launch (start us, length us, event | category | flops | bytes accessed | tf_op | source)
XLA Modules:
  0.0 127.2 jit_solution(11338182516695332099)
XLA Ops:
  6.5 0.0 all-gather.4.cloned.1.call-start
  6.5 1.3 fusion.29
  7.8 0.2 copy.87
  8.0 1.3 %fusion.30 = (bf16[256,1024]{1,0:T(8,128)(2,1)S(1)}, bf16[256,1024]{1,0:T(8,128)(2,1)S(1)}) fusion(bf16[512,1024]{1,0:T(8,128)(2,1)} %param.9), kind=kLoop, calls=%fused_computation.52 | loop fusion | bytes 2097152 | tf_op jit(solution)/shard_map/slice | solution.py:52
  9.3 0.0 copy-start.6
  9.3 0.0 copy-start.5
  9.3 0.2 copy.88
  9.5 0.2 copy.89
  9.7 0.2 copy.90
  10.0 0.0 copy-done.6
  10.0 0.6 dynamic-slice
  11.2 0.0 copy-done.5
  11.2 0.1 multiply_exponential_fusion.2
  11.3 0.1 multiply_exponential_fusion.1
  11.4 0.3 fusion.19
  11.7 1.1 convolution_add_fusion
  12.8 0.0 all-gather.4.cloned.1.call-update
  12.9 23.5 %all-reduce = f32[64]{0:T(128)S(1)} all-reduce(f32[64]{0:T(128)S(1)} %get-tuple-element.137), channel_id=2, replica_groups=mesh['ctx'=4,'exp'=2,'tp'=4] {'ctx','exp'}, use_global_device_ids=true, to_apply=%add | all-reduce | flops 64 | bytes 512
  36.4 0.1 reshape.97
  36.4 2.2 %fusion.28 = (bf16[256,1024]{1,0:T(8,128)(2,1)}, bf16[256,1024]{1,0:T(8,128)(2,1)}) fusion(bf16[512,1024]{1,0:T(8,128)(2,1)} %param.7), kind=kLoop, calls=%fused_computation.50 | loop fusion | bytes 2097152 | tf_op jit(solution)/shard_map/slice | solution.py:50
  38.7 2.1 %copy.91 = bf16[256,1024]{0,1:T(8,128)(2,1)} copy(bf16[256,1024]{1,0:T(8,128)(2,1)} %get-tuple-element.131) | data formatting | bytes 1048576
  40.7 2.0 %copy.86 = bf16[256,1024]{0,1:T(8,128)(2,1)} copy(bf16[256,1024]{1,0:T(8,128)(2,1)} %get-tuple-element.130) | data formatting | bytes 1048576
  42.8 0.1 fusion.25
  42.9 0.1 fusion.24
  42.9 46.3 %all-gather.4.cloned.1.call-done = f32[64,128,128]{2,1,0:T(8,128)} async-done(((f32[8,128,128]{2,1,0:T(8,128)}), f32[64,128,128]{2,1,0:T(8,128)}) %all-gather.4.cloned.1.call-update) | async-done | bytes 4194320 | tf_op jit(solution)/shard_map/all_gather | solution.py:13
  89.2 8.4 %while.14 = (s32[]{:T(128)}, f32[8,128,128]{2,1,0:T(8,128)S(1)}, s32[]{:T(128)}, f32[8,8]{1,0:T(8,128)S(1)}, f32[8,8,128,128]{3,2,1,0:T(8,128)}, /*index=5*/s32[]{:T(128)}, s32[]{:T(128)}) while((s32[]{:T(128)}, f32[8,128,128]{2,1,0:T(8,128)S(1)}, s32[]{:T(128)}, f32[8,8]{1,0:T(8,128)S(1)}, f32[8,8,128,128]{3,2,1,0:T(8,128)}, ...), condition=%wide.region_1.2_spmd.clone, body=%wide.region_0.1_spmd.clone.sunk | while | flops 524292 | bytes 1573065 | solution.py:22
  89.3 1.2 fusion.42
  90.5 1.2 fusion.42
  91.7 1.2 fusion.42
  92.9 1.2 fusion.42
  94.1 1.2 fusion.42
  95.3 1.2 fusion.42
  96.5 1.2 fusion.42
  97.7 0.0 copy-start
  97.7 2.6 %fusion.9 = f32[256,8,128]{2,0,1:T(8,128)} fusion(bf16[256,8,128]{0,2,1:T(8,128)(2,1)} %bitcast.60, f32[256,8]{0,1:T(8,128)S(1)} %get-tuple-element.141, f32[8,128,128]{2,1,0:T(8,128)S(1)} %fusion.19, f32[8,128,128]{2,1,0:T(8,128)S(1)} %get-tuple-element.99, f32[8]{0:T(128)S(1)} %get-tuple-element.136), kind=kOutput, calls=%fused_computation.18 | convolution fusion | flops 67764224 | bytes 2629664 | tf_op jit(solution)/shard_map/thd,hde->the/dot_general | solution.py:73
  100.3 0.0 copy-done
  100.3 1.5 %fusion.10 = f32[256,8,128]{2,0,1:T(8,128)} fusion(bf16[256,8,128]{0,2,1:T(8,128)(2,1)S(1)} %bitcast.58, f32[256,8]{0,1:T(8,128)S(1)} %get-tuple-element.141, f32[8,128,128]{2,1,0:T(8,128)S(1)} %get-tuple-element.99), kind=kOutput, calls=%fused_computation.20 | convolution fusion | flops 67502080 | bytes 2105344 | tf_op jit(solution)/shard_map/thd,hde->the/dot_general | solution.py:73
  101.8 0.0 copy-done.2
  101.8 3.2 %fusion.8 = f32[256,8,128]{2,0,1:T(8,128)} fusion(f32[256,8,128]{2,0,1:T(8,128)} %fusion.9, bf16[256,8,128]{0,2,1:T(8,128)(2,1)S(1)} %bitcast.57, bf16[256,8,128]{0,2,1:T(8,128)(2,1)S(1)} %bitcast.61, bf16[256,8,128]{0,2,1:T(8,128)(2,1)S(1)} %bitcast.55, f32[256,256]{1,0:T(8,128)S(1)} %fusion.24, f32[8]{0:T(128)S(1)} %get-tuple-element.139, ...), kind=kOutput, calls=%fused_computation.16 | convolution fusion | flops 270794752 | bytes 3997728 | tf_op jit(solution)/shard_map/hts,she->the/dot_general | solution.py:58
  105.0 0.0 copy-done.1
  105.0 3.2 %fusion.5 = f32[256,8,128]{2,0,1:T(8,128)} fusion(f32[256,8,128]{2,0,1:T(8,128)} %fusion.10, bf16[256,8,128]{0,2,1:T(8,128)(2,1)S(1)} %bitcast.53, bf16[256,8,128]{0,2,1:T(8,128)(2,1)S(1)} %bitcast.59, bf16[256,8,128]{0,2,1:T(8,128)(2,1)S(1)} %bitcast.51, f32[256,256]{1,0:T(8,128)S(1)} %fusion.24, f32[8]{0:T(128)S(1)} %get-tuple-element.139, ...), kind=kOutput, calls=%fused_computation.13 | convolution fusion | flops 270794752 | bytes 3997728 | tf_op jit(solution)/shard_map/hts,she->the/dot_general | solution.py:58
  108.3 0.0 copy-done.3
  108.3 2.8 %multiply_reduce_fusion = (f32[512]{0:T(512)S(1)}, f32[512,8,128]{2,0,1:T(8,128)}) fusion(f32[256,8,128]{2,0,1:T(8,128)S(1)} %copy-done.3, f32[256,8,128]{2,0,1:T(8,128)} %fusion.5), kind=kLoop, calls=%fused_computation.7 | loop fusion | flops 1572352 | bytes 4196352 | tf_op jit(solution)/shard_map/reduce_sum | solution.py:79
  111.1 1.9 %copy.70 = f32[512,8,128]{0,2,1:T(8,128)S(1)} copy(f32[512,8,128]{2,0,1:T(8,128)} %get-tuple-element.129) | data formatting | bytes 4194304 | tf_op jit(solution)/shard_map/concatenate | solution.py:78
  113.1 5.7 %psum.7 = f32[512]{0:T(512)S(1)} all-reduce(f32[512]{0:T(512)S(1)} %get-tuple-element.128), channel_id=1, replica_groups=mesh['ctx'=4,'exp'=2,'tp'=4] {'tp'}, use_global_device_ids=true, to_apply=%region_3.4 | all-reduce | flops 512 | bytes 4096 | tf_op jit(solution)/shard_map/psum | solution.py:80
  118.7 0.0 copy-done.4
  118.7 0.3 fusion.2
  119.0 1.3 %copy.71 = bf16[512,1024]{1,0:T(8,128)(2,1)} copy(bf16[512,1024]{0,1:T(8,128)(2,1)S(1)} %fusion.2) | data formatting | bytes 2097152 | tf_op jit(solution)/shard_map/convert_element_type | solution.py:83
  (15 shorter events, 0.1 us)
Async XLA Ops:
  6.5 82.7 %all-gather.4.cloned.1.call-start = ((), (), s32[]{:S(2)}) async-start(), calls=%async_computation | async-start | bytes 4718592 | tf_op jit(solution)/shard_map/all_gather | solution.py:13
  9.3 0.7 copy-start.6
  9.3 1.9 %copy-start.5 = (f32[8]{0:T(128)S(1)}, f32[8]{0:T(128)}, u32[]{:S(2)}) copy-start(f32[8]{0:T(128)} %param.10) | copy-start | bytes 100
  97.7 2.6 %copy-start = (bf16[256,1024]{0,1:T(8,128)(2,1)S(1)}, bf16[256,1024]{0,1:T(8,128)(2,1)}, u32[]{:S(2)}) copy-start(bf16[256,1024]{0,1:T(8,128)(2,1)} %copy.86) | copy-start | bytes 1572868
  100.3 1.5 %copy-start.2 = (bf16[256,1024]{0,1:T(8,128)(2,1)S(1)}, bf16[256,1024]{0,1:T(8,128)(2,1)}, u32[]{:S(2)}) copy-start(bf16[256,1024]{0,1:T(8,128)(2,1)} %copy.91) | copy-start | bytes 1572868
  101.8 3.2 %copy-start.1 = (bf16[256,1024]{0,1:T(8,128)(2,1)S(1)}, bf16[256,1024]{0,1:T(8,128)(2,1)}, u32[]{:S(2)}) copy-start(bf16[256,1024]{0,1:T(8,128)(2,1)} %copy.86) | copy-start | bytes 1572868
  105.0 3.3 %copy-start.3 = (f32[256,8,128]{2,0,1:T(8,128)S(1)}, f32[256,8,128]{2,0,1:T(8,128)}, u32[]{:S(2)}) copy-start(f32[256,8,128]{2,0,1:T(8,128)} %fusion.8) | copy-start | bytes 3145732
  111.1 7.6 %copy-start.4 = (f32[1024]{0:T(1024)S(1)}, f32[1024]{0:T(1024)}, u32[]{:S(2)}) copy-start(f32[1024]{0:T(1024)} %param.11) | copy-start | bytes 12292
Sparse Core Ops, SparseCore 0:
  13.0 76.2 all-gather.3
where the time goes:
time: 128 us; the launch traced here: 127 us
  waiting for transfers between devices  46.3 us (36%)
  blocking collectives  29.2 us (23%)
  between operations  14.2 us (11%)
  local copies, waits for them, and re-layouts  13.7 us (11%)
  matrix products  12 us (9%)
  other arithmetic  11.6 us (9%)
    all_gather x1, waiting for transfers between devices, carried_in(): pieces = jax.tree.map(lambda part: lax.all_gather(part, axis), value)  46.3 us
    unnamed x1, blocking collectives  23.5 us
    select_n x7, other arithmetic, hop(): jnp.where(position < mine, new, old)  8.2 us
    dot_general x2, matrix products, local(): jnp.einsum('hts,she->the', mixing, value_block, preferred_element_type=jn...  6.45 us
    psum x1, blocking collectives, local(): row_total = lax.psum(row_squares, 'tp')  5.67 us
    unnamed x22, local copies, waits for them, and re-layouts  5.54 us
    dot_general x2, matrix products, local(): jnp.einsum('thd,hde->the', query_blocks[block_index], state_low, preferre...  4.1 us
    reduce_sum x1, other arithmetic, local(): row_squares = jnp.sum(attended * attended, axis=1)  2.83 us
  transfers between devices with their start and end apart: 1, of which 1 were waited for; matrix products, arithmetic and copies ran while one was open for 5% of the time, Pallas kernels for 0%

commit v1 on v0

v1 whole, which is shorter than its diff:
```python
import functools
import jax
import jax.numpy as jnp
from jax import lax
from jax.experimental import pallas as pl
from jax.experimental.pallas import tpu as pltpu
from jax.sharding import PartitionSpec as P

HEAD_DIM = 128
BLK = 256
F32 = jnp.float32
BF16 = jnp.bfloat16


def dot(a, b, dims, precision=None):
    return lax.dot_general(a, b, (dims, ((), ())), precision=precision, preferred_element_type=F32)


def params(mib=32):
    return pltpu.CompilerParams(vmem_limit_bytes=mib << 20)


def spread_kernel(who, rate_ref, key_ref, value_ref, *outs, group, blocks, heads):
    states, terms = outs[:group], outs[group]
    d = pl.program_id(0)
    first = (who[0] ^ d) * heads
    left = (BLK - lax.broadcasted_iota(jnp.int32, (BLK, HEAD_DIM), 0)).astype(F32)
    results = []
    for h in range(heads):
        rate = rate_ref[first + h]
        cols = slice(h * HEAD_DIM, (h + 1) * HEAD_DIM)
        tail = jnp.exp(-rate * left)
        block_decay = jnp.exp(jnp.full((HEAD_DIM, HEAD_DIM), -rate * BLK, F32))
        own = None
        for b in range(blocks):
            rows = slice(b * BLK, (b + 1) * BLK)
            keys = (key_ref[rows, cols].astype(F32) * tail).astype(BF16)
            term = dot(keys, value_ref[rows, cols], ((0,), (0,)))
            if b < blocks - 1:
                terms[b, 0, cols, :] = term
            own = term if own is None else block_decay * own + term
        results.append(own)
    for i in range(group):
        @pl.when(d == i)
        def _():
            for h in range(heads):
                states[i][h * HEAD_DIM : (h + 1) * HEAD_DIM, :] = results[h]


def local_kernel(rate_ref, query_ref, key_ref, value_ref, out_ref, *, blocks):
    rate = rate_ref[pl.program_id(0)]
    t = lax.broadcasted_iota(jnp.int32, (BLK, BLK), 0)
    s = lax.broadcasted_iota(jnp.int32, (BLK, BLK), 1)
    apart = (t - s).astype(F32)
    weight = jnp.where(apart >= 0, jnp.exp(-rate * jnp.maximum(apart, 0.0)), 0.0)
    for b in range(blocks):
        rows = slice(b * BLK, (b + 1) * BLK)
        scores = dot(query_ref[rows, :], key_ref[rows, :], ((1,), (1,)))
        mixing = (scores * weight).astype(BF16)
        out_ref[rows, :] = dot(mixing, value_ref[rows, :], ((1,), (0,)))


def span_weight(rate, gap, span):
    wide = jnp.full((8, HEAD_DIM), jnp.maximum(gap, 0).astype(F32) * span, F32)
    return jnp.where(gap >= 0, jnp.exp(-rate * wide), 0.0)[:1, :]


def total_kernel(who, rate_ref, *refs, group, heads, span):
    slots, out = refs[:group], refs[group]
    me = who[0]
    for h in range(heads):
        rate = rate_ref[me * heads + h]
        rows = slice(h * HEAD_DIM, (h + 1) * HEAD_DIM)
        total = None
        for e in range(group):
            part = span_weight(rate, group - 1 - (me ^ e), span) * slots[e][rows, :]
            total = part if total is None else total + part
        out[rows, :] = total


def carry_kernel(who, rate_ref, before_ref, *refs, group, heads, span):
    slots, outs = refs[:group], refs[group:]
    me = who[0]
    for h in range(heads):
        rate = rate_ref[me * heads + h]
        rows = slice(h * HEAD_DIM, (h + 1) * HEAD_DIM)
        parts = [slots[e][rows, :] for e in range(group)]
        before = before_ref[rows, :]
        for d in range(group):
            carry = span_weight(rate, me ^ d, span) * before
            for e in range(group):
                if e != d:
                    carry = carry + span_weight(rate, (me ^ d) - (me ^ e) - 1, span) * parts[e]
            outs[d][rows, :] = carry


def carried_kernel(who, rate_ref, query_ref, local_ref, terms_ref, *refs, group, blocks, heads):
    carries, att_ref, squares_ref, acc_ref = refs[:group], refs[group], refs[group + 1], refs[group + 2]
    d = pl.program_id(0)
    first = (who[0] ^ d) * heads
    offset = lax.broadcasted_iota(jnp.int32, (BLK, HEAD_DIM), 0).astype(F32)

    @pl.when(d == 0)
    def _():
        acc_ref[...] = jnp.zeros_like(acc_ref)

    def work(carry_ref):
        for h in range(heads):
            rate = rate_ref[first + h]
            cols = slice(h * HEAD_DIM, (h + 1) * HEAD_DIM)
            inner = jnp.exp(-rate * offset)
            block_decay = jnp.exp(jnp.full((HEAD_DIM, HEAD_DIM), -rate * BLK, F32))
            state = carry_ref[cols, :]
            for b in range(blocks):
                rows = slice(b * BLK, (b + 1) * BLK)
                carried = dot(query_ref[rows, cols], state.astype(BF16), ((1,), (0,)))
                att = local_ref[rows, cols] + carried * inner
                att_ref[rows, cols] = att
                acc_ref[rows, :] += att * att
                if b < blocks - 1:
                    state = block_decay * state + terms_ref[b, 0, cols, :]

    for i in range(group):
        pl.when(d == i)(functools.partial(work, carries[i]))

    @pl.when(d == group - 1)
    def _():
        ones = jnp.ones((8, HEAD_DIM), F32)
        squares_ref[...] = dot(ones, acc_ref[...], ((1,), (1,)), lax.Precision.HIGHEST)


def norm_kernel(*refs, features, count):
    squares, gain_ref, att_ref, out_ref = refs[:count], refs[count], refs[count + 1], refs[count + 2]
    total = squares[0][...]
    for other in squares[1:]:
        total = total + other[...]
    inverse = lax.rsqrt(total / features + 1e-06)
    pick = (lax.broadcasted_iota(jnp.int32, (8, HEAD_DIM), 0) == 0).astype(F32)
    column = dot(inverse, pick, ((0,), (0,)), lax.Precision.HIGHEST)
    for c in range(att_ref.shape[1] // HEAD_DIM):
        cols = slice(c * HEAD_DIM, (c + 1) * HEAD_DIM)
        out_ref[:, cols] = (att_ref[:, cols] * column * gain_ref[:, cols]).astype(BF16)


def local(queries, key_vectors, value_vectors, decay_rate, norm_gain, *, zp, nc, ne, nt):
    rows, width = queries.shape
    heads_all = width // HEAD_DIM
    blocks = rows // BLK
    group = zp * ne
    heads = heads_all // group
    part = heads * HEAD_DIM
    z, x = lax.axis_index("ctx"), lax.axis_index("exp")
    who = jnp.reshape((z % zp) * ne + x, (1,)).astype(jnp.int32)
    smem = pl.BlockSpec(memory_space=pltpu.SMEM)
    vmem = pl.BlockSpec(memory_space=pltpu.VMEM)
    whole_state = pl.BlockSpec((part, HEAD_DIM), lambda d, w: (0, 0))
    mine = pl.BlockSpec((rows, part), lambda d, w: (0, w[0] ^ d))
    term_block = pl.BlockSpec((blocks - 1, 1, part, HEAD_DIM), lambda d, w: (0, d, 0, 0))
    state_type = jax.ShapeDtypeStruct((part, HEAD_DIM), F32)

    *slots, terms = pl.pallas_call(
        functools.partial(spread_kernel, group=group, blocks=blocks, heads=heads),
        grid_spec=pltpu.PrefetchScalarGridSpec(
            num_scalar_prefetch=1, grid=(group,),
            in_specs=[smem, mine, mine],
            out_specs=[whole_state] * group + [term_block],
        ),
        out_shape=[state_type] * group + [jax.ShapeDtypeStruct((blocks - 1, group, part, HEAD_DIM), F32)],
        compiler_params=params(),
        name="spread",
    )(who, decay_rate, key_vectors, value_vectors)

    def swap(value, d):
        pairs = []
        for zz in range(nc):
            for xx in range(ne):
                m = ((zz % zp) * ne + xx) ^ d
                pairs.append((zz * ne + xx, (zz // zp * zp + m // ne) * ne + m % ne))
        return lax.ppermute(value, ("ctx", "exp"), pairs)

    order = list(range(group - 1, 0, -1))
    got = {d: swap(slots[d], d) for d in order}
    slots = [slots[0]] + [got[d] for d in range(1, group)]

    one_head = pl.BlockSpec((rows, HEAD_DIM), lambda h: (0, h))
    local_part = pl.pallas_call(
        functools.partial(local_kernel, blocks=blocks),
        grid=(heads_all,),
        in_specs=[smem, one_head, one_head, one_head],
        out_specs=one_head,
        out_shape=jax.ShapeDtypeStruct((rows, width), F32),
        compiler_params=params(),
        cost_estimate=pl.CostEstimate(flops=4 * rows * BLK * width, bytes_accessed=10 * rows * width, transcendentals=0),
        name="local_part",
    )(decay_rate, queries, key_vectors, value_vectors)

    span = float(rows)
    total = pl.pallas_call(
        functools.partial(total_kernel, group=group, heads=heads, span=span),
        in_specs=[smem, smem] + [vmem] * group,
        out_specs=vmem,
        out_shape=state_type,
        compiler_params=params(),
        name="group_total",
    )(who, decay_rate, *slots)
    groups = nc // zp
    before = lax.ppermute(total, "ctx", [(zz, zz + zp) for zz in range(nc - zp)])
    step = 1
    while step < groups - 1:
        rates = lax.dynamic_slice_in_dim(decay_rate, who[0] * heads, heads)
        scale = jnp.repeat(jnp.exp(-rates * (span * group * step)), HEAD_DIM)[:, None]
        moved = lax.ppermute(before, "ctx", [(zz, zz + zp * step) for zz in range(nc - zp * step)])
        before = before + scale * moved
        step *= 2

    carries = pl.pallas_call(
        functools.partial(carry_kernel, group=group, heads=heads, span=span),
        in_specs=[smem, smem] + [vmem] * (group + 1),
        out_specs=[vmem] * group,
        out_shape=[state_type] * group,
        compiler_params=params(),
        name="carry",
    )(who, decay_rate, before, *slots)
    got = {d: swap(carries[d], d) for d in order}
    carries = [carries[0]] + [got[d] for d in range(1, group)]

    attended, squares = pl.pallas_call(
        functools.partial(carried_kernel, group=group, blocks=blocks, heads=heads),
        grid_spec=pltpu.PrefetchScalarGridSpec(
            num_scalar_prefetch=1, grid=(group,),
            in_specs=[smem, mine, mine, term_block] + [whole_state] * group,
            out_specs=[mine, pl.BlockSpec((8, rows), lambda d, w: (0, 0))],
            scratch_shapes=[pltpu.VMEM((rows, HEAD_DIM), F32)],
        ),
        out_shape=[jax.ShapeDtypeStruct((rows, width), F32), jax.ShapeDtypeStruct((8, rows), F32)],
        compiler_params=params(),
        name="carried",
    )(who, decay_rate, queries, local_part, terms, *carries)

    if nt & (nt - 1) == 0:
        swaps = [[(i, i ^ d) for i in range(nt)] for d in range(1, nt)]
    else:
        swaps = [[(i, (i + d) % nt) for i in range(nt)] for d in range(1, nt)]
    sums = [squares] + [lax.ppermute(squares, "tp", pairs) for pairs in swaps[::-1]]

    return pl.pallas_call(
        functools.partial(norm_kernel, features=float(width * nt), count=nt),
        in_specs=[vmem] * (nt + 2),
        out_specs=vmem,
        out_shape=jax.ShapeDtypeStruct((rows, width), BF16),
        compiler_params=params(),
        name="norm",
    )(*sums, norm_gain[None, :], attended)


def solution(mesh):
    nc, ne, nt = mesh.shape["ctx"], mesh.shape["exp"], mesh.shape["tp"]

    def whole(queries, key_vectors, value_vectors, decay_rate, norm_gain):
        heads_local = decay_rate.shape[0] // nt
        zp = 2 if nc % 2 == 0 and heads_local % (2 * ne) == 0 else 1
        return jax.shard_map(
            functools.partial(local, zp=zp, nc=nc, ne=ne, nt=nt),
            mesh=mesh,
            in_specs=(P(("ctx", "exp"), "tp"),) * 3 + (P("tp"), P("tp")),
            out_specs=P(("ctx", "exp"), "tp"),
            check_vma=False,
        )(queries, key_vectors, value_vectors, decay_rate, norm_gain)

    return whole
```

time: 128 us -> 44 us (0.34)
  waiting for transfers between devices: 46.3 us -> 11.4 us
  blocking collectives: 29.2 us -> 0 us
  starting transfers between devices: 0.01 us -> 15.8 us
  between operations: 14.2 us -> 0.1 us
  Pallas kernels: 0 us -> 13.2 us
  matrix products: 12 us -> 0 us
  other arithmetic: 11.6 us -> 0 us
  local copies, waits for them, and re-layouts: 13.7 us -> 3.21 us
    all_gather x1 -> x0, waiting for transfers between devices: 46.3 us -> none  [carried_in(): pieces = jax.tree.map(lambda part: lax.all_gather(part, axis), value)]
    unnamed x1 -> x0, blocking collectives: 23.5 us -> none
    ppermute x0 -> x10, starting transfers between devices: none -> 15.8 us  [the longest x6 9.23 us: swap(): return lax.ppermute(value, ('ctx', 'exp'), pairs)]
    pallas_call x0 -> x6, Pallas kernels: none -> 13.2 us  [the longest x1 5.75 us: local(): pl.pallas_call(functools.partial(local_kernel, blocks=blocks), grid=(head...]
    dot_general x6 -> x0, matrix products: 12 us -> none  [the longest x2 6.45 us: local(): jnp.einsum('hts,she->the', mixing, value_block, preferred_element_type=jn...]
    ppermute x0 -> x10, waiting for transfers between devices: none -> 11.4 us  [the longest x6 6 us: swap(): return lax.ppermute(value, ('ctx', 'exp'), pairs)]
    select_n x7 -> x0, other arithmetic: 8.2 us -> none  [hop(): jnp.where(position < mine, new, old)]
    psum x1 -> x0, blocking collectives: 5.67 us -> none  [local(): row_total = lax.psum(row_squares, 'tp')]
  transfers between devices with their start and end apart: 1 -> 10, of which waited for: 1 -> 6; matrix products, arithmetic and copies ran while one was open for 5% -> 0% of each run, Pallas kernels for 0% -> 13%
where the time goes in v1:
time: 44 us; the launch traced here: 43.7 us
  starting transfers between devices  15.8 us (36%)
  Pallas kernels  13.2 us (30%)
  waiting for transfers between devices  11.4 us (26%)
  local copies, waits for them, and re-layouts  3.21 us (7%)
    ppermute x6, starting transfers between devices, swap(): return lax.ppermute(value, ('ctx', 'exp'), pairs)  9.23 us
    ppermute x6, waiting for transfers between devices, swap(): return lax.ppermute(value, ('ctx', 'exp'), pairs)  6 us
    pallas_call x1, Pallas kernels, local(): pl.pallas_call(functools.partial(local_kernel, blocks=blocks), grid=(head...  5.75 us
    ppermute x1, starting transfers between devices, local(): lax.ppermute(total, 'ctx', [(zz, zz + zp) for zz in range(nc - zp)])  4.68 us
    unnamed x14, local copies, waits for them, and re-layouts  3.21 us
    ppermute x3, waiting for transfers between devices, local(): lax.ppermute(squares, 'tp', pairs)  2.88 us
    ppermute x1, waiting for transfers between devices, local(): lax.ppermute(total, 'ctx', [(zz, zz + zp) for zz in range(nc - zp)])  2.51 us
    pallas_call x1, Pallas kernels, local(): pl.pallas_call(functools.partial(carried_kernel, group=group, blocks=bloc...  2.44 us
  transfers between devices with their start and end apart: 10, of which 6 were waited for; matrix products, arithmetic and copies ran while one was open for 0% of the time, Pallas kernels for 13%

profile of v1, /device:TPU:0, one launch (start us, length us, event | category | flops | bytes accessed | tf_op | source)
XLA Modules:
  0.0 43.7 jit_solution(12744734123423118204)
XLA Ops:
  0.0 0.0 copy-start
  0.0 0.0 copy-start.1
  0.0 1.3 %copy-done.1 = bf16[512,1024]{1,0:T(8,128)(2,1)S(1)} copy-done((bf16[512,1024]{1,0:T(8,128)(2,1)S(1)}, bf16[512,1024]{1,0:T(8,128)(2,1)}, u32[]{:S(2)}) %copy-start.1) | copy-done | bytes 1048600
  1.3 0.0 copy-start.3
  1.3 1.2 %copy-done.3 = bf16[512,1024]{1,0:T(8,128)(2,1)S(1)} copy-done((bf16[512,1024]{1,0:T(8,128)(2,1)S(1)}, bf16[512,1024]{1,0:T(8,128)(2,1)}, u32[]{:S(2)}) %copy-start.3) | copy-done | bytes 1048600
  2.5 0.0 copy-start.5
  2.5 0.7 %copy-done.5 = f32[8]{0:T(128)S(1)} copy-done((f32[8]{0:T(128)S(1)}, f32[8]{0:T(128)}, u32[]{:S(2)}) %copy-start.5) | copy-done | bytes 56
  3.2 0.0 copy-start.2
  3.2 0.0 copy-start.4
  3.2 2.1 %spread.1 = (f32[256,128]{1,0:T(8,128)S(1)}, f32[256,128]{1,0:T(8,128)S(1)}, f32[256,128]{1,0:T(8,128)S(1)}, f32[256,128]{1,0:T(8,128)S(1)}, f32[1,4,256,128]{3,2,1,0:T(8,128)S(1)}) custom-call(s32[1]{0:T(128)} %bitcast.who, f32[8]{0:T(128)S(1)} %copy-done.5, bf16[512,1024]{1,0:T(8,128)(2,1)S(1)} %copy-done.1, bf16[512,1024]{1,0:T(8,128)(2,1)S(1)} %copy-done.3), custom_call_target="tpu_custom_call" | custom-call | tf_op jit(solution)/shard_map/spread/pallas_call | solution.py:161
  5.3 3.0 %collective-permute-start = (f32[256,128]{1,0:T(8,128)S(1)}, f32[256,128]{1,0:T(8,128)S(1)}, u32[]{:S(2)}, u32[]{:S(2)}) collective-permute-start(f32[256,128]{1,0:T(8,128)S(1)} %get-tuple-element.18), channel_id=1, source_target_pairs={{0,4},{4,0},{8,12},{12,8},{16,20},{20,16},{24,28},{28,24},{1,5},{5... | collective-permute-start | bytes 393224 | tf_op jit(solution)/shard_map/ppermute | solution.py:179
  8.3 1.6 %collective-permute-start.1 = (f32[256,128]{1,0:T(8,128)S(1)}, f32[256,128]{1,0:T(8,128)S(1)}, u32[]{:S(2)}, u32[]{:S(2)}) collective-permute-start(f32[256,128]{1,0:T(8,128)S(1)} %get-tuple-element.19), channel_id=1, source_target_pairs={{0,8},{4,12},{8,0},{12,4},{16,24},{20,28},{24,16},{28,20},{1,9},{5... | collective-permute-start | bytes 393224 | tf_op jit(solution)/shard_map/ppermute | solution.py:179
  9.9 0.0 collective-permute-start.2
  9.9 1.9 %collective-permute-done.refs_1_ = f32[256,128]{1,0:T(8,128)S(1)} collective-permute-done((f32[256,128]{1,0:T(8,128)S(1)}, f32[256,128]{1,0:T(8,128)S(1)}, u32[]{:S(2)}, u32[]{:S(2)}) %collective-permute-start) | collective-permute-done | bytes 131104 | tf_op jit(solution)/shard_map/ppermute | solution.py:179
  11.8 2.9 %collective-permute-done.1.refs_2_ = f32[256,128]{1,0:T(8,128)S(1)} collective-permute-done((f32[256,128]{1,0:T(8,128)S(1)}, f32[256,128]{1,0:T(8,128)S(1)}, u32[]{:S(2)}, u32[]{:S(2)}) %collective-permute-start.1) | collective-permute-done | bytes 131104 | tf_op jit(solution)/shard_map/ppermute | solution.py:179
  14.7 1.2 %collective-permute-done.2.refs_3_ = f32[256,128]{1,0:T(8,128)S(1)} collective-permute-done((f32[256,128]{1,0:T(8,128)S(1)}, f32[256,128]{1,0:T(8,128)S(1)}, u32[]{:S(2)}, u32[]{:S(2)}) %collective-permute-start.2) | collective-permute-done | bytes 131104 | tf_op jit(solution)/shard_map/ppermute | solution.py:179
  15.9 0.6 %group_total.1 = f32[256,128]{1,0:T(8,128)S(1)} custom-call(s32[1]{0:T(128)} %bitcast.who, f32[8]{0:T(128)S(1)} %copy-done.5, f32[256,128]{1,0:T(8,128)S(1)} %get-tuple-element.17.refs_0_, f32[256,128]{1,0:T(8,128)S(1)} %collective-permute-done.refs_1_, f32[256,128]{1,0:T(8,128)S(1)} %collective-permute-done.1.refs_2_, ...), custom_call_target="tpu_custom_call" | custom-call | tf_op jit(solution)/shard_map/group_total/pallas_call | solution.py:198
  16.5 4.7 %collective-permute-start.3 = (f32[256,128]{1,0:T(8,128)S(1)}, f32[256,128]{1,0:T(8,128)S(1)}, u32[]{:S(2)}, u32[]{:S(2)}) collective-permute-start(f32[256,128]{1,0:T(8,128)S(1)} %group_total.1), channel_id=1, source_target_pairs={{0,16},{8,24},{1,17},{9,25},{2,18},{10,26},{3,19},{11,27},{4,20},{... | collective-permute-start | bytes 393224 | tf_op jit(solution)/shard_map/ppermute | solution.py:207
  21.2 2.5 %collective-permute-done.3.before_ref = f32[256,128]{1,0:T(8,128)S(1)} collective-permute-done((f32[256,128]{1,0:T(8,128)S(1)}, f32[256,128]{1,0:T(8,128)S(1)}, u32[]{:S(2)}, u32[]{:S(2)}) %collective-permute-start.3) | collective-permute-done | bytes 131104 | tf_op jit(solution)/shard_map/ppermute | solution.py:207
  23.7 0.7 %carry.1 = (f32[256,128]{1,0:T(8,128)S(1)}, f32[256,128]{1,0:T(8,128)S(1)}, f32[256,128]{1,0:T(8,128)S(1)}, f32[256,128]{1,0:T(8,128)S(1)}) custom-call(s32[1]{0:T(128)} %bitcast.who, f32[8]{0:T(128)S(1)} %copy-done.5, f32[256,128]{1,0:T(8,128)S(1)} %collective-permute-done.3.before_ref, f32[256,128]{1,0:T(8,128)S(1)} %get-tuple-element.17.refs_0_, ...), custom_call_target="tpu_custom_call" | custom-call | tf_op jit(solution)/shard_map/carry/pallas_call | solution.py:216
  24.4 1.5 %collective-permute-start.4 = (f32[256,128]{1,0:T(8,128)S(1)}, f32[256,128]{1,0:T(8,128)S(1)}, u32[]{:S(2)}, u32[]{:S(2)}) collective-permute-start(f32[256,128]{1,0:T(8,128)S(1)} %get-tuple-element.22), channel_id=1, source_target_pairs={{0,4},{4,0},{8,12},{12,8},{16,20},{20,16},{24,28},{28,24},{1,5},{5... | collective-permute-start | bytes 393224 | tf_op jit(solution)/shard_map/ppermute | solution.py:179
  26.0 3.0 %collective-permute-start.5 = (f32[256,128]{1,0:T(8,128)S(1)}, f32[256,128]{1,0:T(8,128)S(1)}, u32[]{:S(2)}, u32[]{:S(2)}) collective-permute-start(f32[256,128]{1,0:T(8,128)S(1)} %get-tuple-element.23), channel_id=1, source_target_pairs={{0,8},{4,12},{8,0},{12,4},{16,24},{20,28},{24,16},{28,20},{1,9},{5... | collective-permute-start | bytes 393224 | tf_op jit(solution)/shard_map/ppermute | solution.py:179
  29.0 0.1 collective-permute-start.6
  29.1 0.0 copy-done
  29.1 0.0 copy-done.2
  29.1 0.0 copy-done.4
  29.1 5.7 %local_part.1.local_ref = f32[512,1024]{1,0:T(8,128)S(1)} custom-call(f32[8]{0:T(128)S(1)} %copy-done.5, bf16[512,1024]{1,0:T(8,128)(2,1)S(1)} %copy-done, bf16[512,1024]{1,0:T(8,128)(2,1)S(1)} %copy-done.2, bf16[512,1024]{1,0:T(8,128)(2,1)S(1)} %copy-done.4), custom_call_target="tpu_custom_call" | custom-call | flops 536870912 | bytes 5242880 | tf_op jit(solution)/shard_map/local_part/pallas_call | solution.py:186
  34.8 0.0 collective-permute-done.4.refs_1_
  34.8 0.0 collective-permute-done.5.refs_2_
  34.8 0.0 collective-permute-done.6.refs_3_
  34.9 0.0 copy-start.6
  34.9 2.4 %carried.1 = (f32[512,1024]{1,0:T(8,128)S(1)}, f32[8,512]{1,0:T(8,128)S(1)}) custom-call(s32[1]{0:T(128)} %bitcast.who, f32[8]{0:T(128)S(1)} %copy-done.5, bf16[512,1024]{1,0:T(8,128)(2,1)S(1)} %copy-done, f32[512,1024]{1,0:T(8,128)S(1)} %local_part.1.local_ref, f32[1,4,256,128]{3,2,1,0:T(8,128)S(1)} %get-tuple-element.16.terms_ref, ...), custom_call_target="tpu_custom_call" | custom-call | tf_op jit(solution)/shard_map/carried/pallas_call | solution.py:227
  37.3 0.1 collective-permute-start.9
  37.4 1.6 %collective-permute-start.8 = (f32[8,512]{1,0:T(8,128)S(1)}, f32[8,512]{1,0:T(8,128)S(1)}, u32[]{:S(2)}, u32[]{:S(2)}) collective-permute-start(f32[8,512]{1,0:T(8,128)S(1)} %get-tuple-element.25.refs_0_), channel_id=1, source_target_pairs={{0,2},{1,3},{2,0},{3,1},{4,6},{5,7},{6,4},{7,5},{8,10},{9,11},{10,... | collective-permute-start | bytes 49160 | tf_op jit(solution)/shard_map/ppermute | solution.py:244
  39.0 0.3 collective-permute-start.7
  39.3 0.0 collective-permute-done.9.refs_3_
  39.3 1.9 %collective-permute-done.8.refs_2_ = f32[8,512]{1,0:T(8,128)S(1)} collective-permute-done((f32[8,512]{1,0:T(8,128)S(1)}, f32[8,512]{1,0:T(8,128)S(1)}, u32[]{:S(2)}, u32[]{:S(2)}) %collective-permute-start.8) | collective-permute-done | bytes 16416 | tf_op jit(solution)/shard_map/ppermute | solution.py:244
  41.2 0.9 %collective-permute-done.7.refs_1_ = f32[8,512]{1,0:T(8,128)S(1)} collective-permute-done((f32[8,512]{1,0:T(8,128)S(1)}, f32[8,512]{1,0:T(8,128)S(1)}, u32[]{:S(2)}, u32[]{:S(2)}) %collective-permute-start.7) | collective-permute-done | bytes 16416 | tf_op jit(solution)/shard_map/ppermute | solution.py:244
  42.1 0.0 copy-done.6
  42.1 1.6 %norm.1 = bf16[512,1024]{1,0:T(8,128)(2,1)} custom-call(f32[8,512]{1,0:T(8,128)S(1)} %get-tuple-element.25.refs_0_, f32[8,512]{1,0:T(8,128)S(1)} %collective-permute-done.7.refs_1_, f32[8,512]{1,0:T(8,128)S(1)} %collective-permute-done.8.refs_2_, f32[8,512]{1,0:T(8,128)S(1)} %collective-permute-done.9.refs_3_, f32[1,1024]{1,0:T(1,128)S(1)} %bitcast.2, ...), custom_call_target="tpu_custom_call" | custom-call | tf_op jit(solution)/shard_map/norm/pallas_call | solution.py:246
Async XLA Ops:
  0.0 29.1 %copy-start = (bf16[512,1024]{1,0:T(8,128)(2,1)S(1)}, bf16[512,1024]{1,0:T(8,128)(2,1)}, u32[]{:S(2)}) copy-start(bf16[512,1024]{1,0:T(8,128)(2,1)} %query_ref.3) | copy-start | bytes 3145732
  0.0 1.3 %copy-start.1 = (bf16[512,1024]{1,0:T(8,128)(2,1)S(1)}, bf16[512,1024]{1,0:T(8,128)(2,1)}, u32[]{:S(2)}) copy-start(bf16[512,1024]{1,0:T(8,128)(2,1)} %key_ref.3) | copy-start | bytes 3145732
  1.3 1.2 %copy-start.3 = (bf16[512,1024]{1,0:T(8,128)(2,1)S(1)}, bf16[512,1024]{1,0:T(8,128)(2,1)}, u32[]{:S(2)}) copy-start(bf16[512,1024]{1,0:T(8,128)(2,1)} %value_ref.3) | copy-start | bytes 3145732
  2.5 0.7 %copy-start.5 = (f32[8]{0:T(128)S(1)}, f32[8]{0:T(128)}, u32[]{:S(2)}) copy-start(f32[8]{0:T(128)} %rate_ref.9) | copy-start | bytes 100
  3.2 25.9 %copy-start.2 = (bf16[512,1024]{1,0:T(8,128)(2,1)S(1)}, bf16[512,1024]{1,0:T(8,128)(2,1)}, u32[]{:S(2)}) copy-start(bf16[512,1024]{1,0:T(8,128)(2,1)} %key_ref.3) | copy-start | bytes 3145732
  3.2 25.9 %copy-start.4 = (bf16[512,1024]{1,0:T(8,128)(2,1)S(1)}, bf16[512,1024]{1,0:T(8,128)(2,1)}, u32[]{:S(2)}) copy-start(bf16[512,1024]{1,0:T(8,128)(2,1)} %value_ref.3) | copy-start | bytes 3145732
  5.3 6.5 %collective-permute-start = (f32[256,128]{1,0:T(8,128)S(1)}, f32[256,128]{1,0:T(8,128)S(1)}, u32[]{:S(2)}, u32[]{:S(2)}) collective-permute-start(f32[256,128]{1,0:T(8,128)S(1)} %get-tuple-element.18), channel_id=1, source_target_pairs={{0,4},{4,0},{8,12},{12,8},{16,20},{20,16},{24,28},{28,24},{1,5},{5... | collective-permute-start | bytes 393224 | tf_op jit(solution)/shard_map/ppermute | solution.py:179
  8.3 6.4 %collective-permute-start.1 = (f32[256,128]{1,0:T(8,128)S(1)}, f32[256,128]{1,0:T(8,128)S(1)}, u32[]{:S(2)}, u32[]{:S(2)}) collective-permute-start(f32[256,128]{1,0:T(8,128)S(1)} %get-tuple-element.19), channel_id=1, source_target_pairs={{0,8},{4,12},{8,0},{12,4},{16,24},{20,28},{24,16},{28,20},{1,9},{5... | collective-permute-start | bytes 393224 | tf_op jit(solution)/shard_map/ppermute | solution.py:179
  9.9 6.0 %collective-permute-start.2 = (f32[256,128]{1,0:T(8,128)S(1)}, f32[256,128]{1,0:T(8,128)S(1)}, u32[]{:S(2)}, u32[]{:S(2)}) collective-permute-start(f32[256,128]{1,0:T(8,128)S(1)} %get-tuple-element.20), channel_id=1, source_target_pairs={{0,12},{4,8},{8,4},{12,0},{16,28},{20,24},{24,20},{28,16},{1,13},{... | collective-permute-start | bytes 393224 | tf_op jit(solution)/shard_map/ppermute | solution.py:179
  16.5 7.2 %collective-permute-start.3 = (f32[256,128]{1,0:T(8,128)S(1)}, f32[256,128]{1,0:T(8,128)S(1)}, u32[]{:S(2)}, u32[]{:S(2)}) collective-permute-start(f32[256,128]{1,0:T(8,128)S(1)} %group_total.1), channel_id=1, source_target_pairs={{0,16},{8,24},{1,17},{9,25},{2,18},{10,26},{3,19},{11,27},{4,20},{... | collective-permute-start | bytes 393224 | tf_op jit(solution)/shard_map/ppermute | solution.py:207
  24.4 10.4 %collective-permute-start.4 = (f32[256,128]{1,0:T(8,128)S(1)}, f32[256,128]{1,0:T(8,128)S(1)}, u32[]{:S(2)}, u32[]{:S(2)}) collective-permute-start(f32[256,128]{1,0:T(8,128)S(1)} %get-tuple-element.22), channel_id=1, source_target_pairs={{0,4},{4,0},{8,12},{12,8},{16,20},{20,16},{24,28},{28,24},{1,5},{5... | collective-permute-start | bytes 393224 | tf_op jit(solution)/shard_map/ppermute | solution.py:179
  26.0 8.9 %collective-permute-start.5 = (f32[256,128]{1,0:T(8,128)S(1)}, f32[256,128]{1,0:T(8,128)S(1)}, u32[]{:S(2)}, u32[]{:S(2)}) collective-permute-start(f32[256,128]{1,0:T(8,128)S(1)} %get-tuple-element.23), channel_id=1, source_target_pairs={{0,8},{4,12},{8,0},{12,4},{16,24},{20,28},{24,16},{28,20},{1,9},{5... | collective-permute-start | bytes 393224 | tf_op jit(solution)/shard_map/ppermute | solution.py:179
  29.0 5.9 %collective-permute-start.6 = (f32[256,128]{1,0:T(8,128)S(1)}, f32[256,128]{1,0:T(8,128)S(1)}, u32[]{:S(2)}, u32[]{:S(2)}) collective-permute-start(f32[256,128]{1,0:T(8,128)S(1)} %get-tuple-element.24), channel_id=1, source_target_pairs={{0,12},{4,8},{8,4},{12,0},{16,28},{20,24},{24,20},{28,16},{1,13},{... | collective-permute-start | bytes 393224 | tf_op jit(solution)/shard_map/ppermute | solution.py:179
  34.9 7.3 %copy-start.6 = (f32[1024]{0:T(1024)S(1)}, f32[1024]{0:T(1024)}, u32[]{:S(2)}) copy-start(f32[1024]{0:T(1024)} %param.9) | copy-start | bytes 12292
  37.3 1.9 %collective-permute-start.9 = (f32[8,512]{1,0:T(8,128)S(1)}, f32[8,512]{1,0:T(8,128)S(1)}, u32[]{:S(2)}, u32[]{:S(2)}) collective-permute-start(f32[8,512]{1,0:T(8,128)S(1)} %get-tuple-element.25.refs_0_), channel_id=1, source_target_pairs={{0,1},{1,0},{2,3},{3,2},{4,5},{5,4},{6,7},{7,6},{8,9},{9,8},{10,11... | collective-permute-start | bytes 49160 | tf_op jit(solution)/shard_map/ppermute | solution.py:244
  37.4 3.8 %collective-permute-start.8 = (f32[8,512]{1,0:T(8,128)S(1)}, f32[8,512]{1,0:T(8,128)S(1)}, u32[]{:S(2)}, u32[]{:S(2)}) collective-permute-start(f32[8,512]{1,0:T(8,128)S(1)} %get-tuple-element.25.refs_0_), channel_id=1, source_target_pairs={{0,2},{1,3},{2,0},{3,1},{4,6},{5,7},{6,4},{7,5},{8,10},{9,11},{10,... | collective-permute-start | bytes 49160 | tf_op jit(solution)/shard_map/ppermute | solution.py:244
  39.0 3.2 %collective-permute-start.7 = (f32[8,512]{1,0:T(8,128)S(1)}, f32[8,512]{1,0:T(8,128)S(1)}, u32[]{:S(2)}, u32[]{:S(2)}) collective-permute-start(f32[8,512]{1,0:T(8,128)S(1)} %get-tuple-element.25.refs_0_), channel_id=1, source_target_pairs={{0,3},{1,2},{2,1},{3,0},{4,7},{5,6},{6,5},{7,4},{8,11},{9,10},{10,... | collective-permute-start | bytes 49160 | tf_op jit(solution)/shard_map/ppermute | solution.py:244

commit v2 on v1

v2 whole, which is shorter than its diff:
```python
import functools
import jax
import jax.numpy as jnp
from jax import lax
from jax.experimental import pallas as pl
from jax.experimental.pallas import tpu as pltpu
from jax.sharding import PartitionSpec as P

HEAD_DIM = 128
BLK = 256
F32 = jnp.float32
BF16 = jnp.bfloat16


def dot(a, b, dims, precision=None):
    return lax.dot_general(a, b, (dims, ((), ())), precision=precision, preferred_element_type=F32)


def params(mib=32):
    return pltpu.CompilerParams(vmem_limit_bytes=mib << 20)


def spread_kernel(who, rate_hbm, key_hbm, value_hbm, *refs, group, blocks, heads, order):
    states, terms = refs[:group], refs[group]
    rate_ref, key_ref, value_ref, sems, rate_sem = refs[group + 1 :]
    part = heads * HEAD_DIM

    def copies(d):
        cols = pl.ds(pl.multiple_of((who[0] ^ d) * part, part), part)
        return (
            pltpu.make_async_copy(key_hbm.at[:, cols], key_ref.at[d], sems.at[0, d]),
            pltpu.make_async_copy(value_hbm.at[:, cols], value_ref.at[d], sems.at[1, d]),
        )

    rate_copy = pltpu.make_async_copy(rate_hbm, rate_ref, rate_sem)
    rate_copy.start()
    for d in order:
        for copy in copies(d):
            copy.start()
    left = (BLK - lax.broadcasted_iota(jnp.int32, (BLK, HEAD_DIM), 0)).astype(F32)
    rate_copy.wait()
    for d in order:
        rates = [rate_ref[(who[0] ^ d) * heads + h] for h in range(heads)]
        tails = [jnp.exp(-rate * left) for rate in rates]
        for copy in copies(d):
            copy.wait()
        for h in range(heads):
            cols = slice(h * HEAD_DIM, (h + 1) * HEAD_DIM)
            block_decay = jnp.exp(jnp.full((8, HEAD_DIM), -rates[h] * BLK, F32))[:1, :]
            own = None
            for b in range(blocks):
                rows = slice(b * BLK, (b + 1) * BLK)
                keys = (key_ref[d, rows, cols].astype(F32) * tails[h]).astype(BF16)
                term = dot(keys, value_ref[d, rows, cols], ((0,), (0,)))
                if b < blocks - 1:
                    terms[b, d, cols, :] = term
                own = term if own is None else block_decay * own + term
            states[d][cols, :] = own


def local_kernel(rate_ref, query_ref, key_ref, value_ref, out_ref, inner_ref, *, blocks):
    rate = rate_ref[pl.program_id(0)]
    t = lax.broadcasted_iota(jnp.int32, (BLK, BLK), 0)
    s = lax.broadcasted_iota(jnp.int32, (BLK, BLK), 1)
    apart = (t - s).astype(F32)
    weight = jnp.where(apart >= 0, jnp.exp(-rate * jnp.maximum(apart, 0.0)), 0.0)
    inner_ref[0] = jnp.exp(-rate * lax.broadcasted_iota(jnp.int32, (BLK, HEAD_DIM), 0).astype(F32))
    for b in range(blocks):
        rows = slice(b * BLK, (b + 1) * BLK)
        scores = dot(query_ref[rows, :], key_ref[rows, :], ((1,), (1,)))
        mixing = (scores * weight).astype(BF16)
        out_ref[rows, :] = dot(mixing, value_ref[rows, :], ((1,), (0,)))


def span_weight(rate, gap, span):
    wide = jnp.full((8, HEAD_DIM), jnp.maximum(gap, 0).astype(F32) * span, F32)
    return jnp.where(gap >= 0, jnp.exp(-rate * wide), 0.0)[:1, :]


def total_kernel(who, rate_ref, after_ref, *refs, group, heads, span):
    slots, out = refs[:group], refs[group]
    me = who[0]
    for h in range(heads):
        rate = rate_ref[me * heads + h]
        rows = slice(h * HEAD_DIM, (h + 1) * HEAD_DIM)
        total = None
        for e in range(group):
            part = span_weight(rate, group - 1 - (me ^ e), span) * slots[e][rows, :]
            total = part if total is None else total + part
        out[rows, :] = total


def carry_kernel(who, rate_ref, before_ref, *refs, group, heads, span):
    slots, outs = refs[:group], refs[group:]
    me = who[0]
    for h in range(heads):
        rate = rate_ref[me * heads + h]
        rows = slice(h * HEAD_DIM, (h + 1) * HEAD_DIM)
        parts = [slots[e][rows, :] for e in range(group)]
        before = before_ref[rows, :]
        for d in range(group):
            carry = span_weight(rate, me ^ d, span) * before
            for e in range(group):
                if e != d:
                    carry = carry + span_weight(rate, (me ^ d) - (me ^ e) - 1, span) * parts[e]
            outs[d][rows, :] = carry


def split_bf16(value):
    high = value.astype(BF16)
    rest = value - high.astype(F32)
    middle = rest.astype(BF16)
    return high, middle, (rest - middle.astype(F32)).astype(BF16)


def carried_kernel(who, rate_ref, query_ref, local_ref, terms_ref, inner_ref, *refs, group, blocks, heads):
    carries, att_ref, squares_ref, acc_ref = refs[:group], refs[group], refs[group + 1], refs[group + 2]
    for d in range(group):
        owner = who[0] ^ d
        part = heads * HEAD_DIM
        for h in range(heads):
            head = owner * heads + h
            rate = rate_ref[head]
            here = slice(h * HEAD_DIM, (h + 1) * HEAD_DIM)
            cols = pl.ds(pl.multiple_of(owner * part + h * HEAD_DIM, HEAD_DIM), HEAD_DIM)
            block_decay = jnp.exp(jnp.full((8, HEAD_DIM), -rate * BLK, F32))[:1, :]
            state = carries[d][here, :]
            for b in range(blocks):
                rows = slice(b * BLK, (b + 1) * BLK)
                carried = dot(query_ref[rows, cols], state.astype(BF16), ((1,), (0,)))
                att = local_ref[rows, cols] + carried * inner_ref[head]
                att_ref[rows, cols] = att
                if d == 0 and h == 0:
                    acc_ref[rows, :] = att * att
                else:
                    acc_ref[rows, :] += att * att
                if b < blocks - 1:
                    state = block_decay * state + terms_ref[b, d, here, :]
    ones = jnp.ones((8, HEAD_DIM), BF16)
    total = None
    for piece in split_bf16(acc_ref[...]):
        add = dot(ones, piece, ((1,), (1,)))
        total = add if total is None else total + add
    squares_ref[...] = total[:1, :]


def norm_kernel(*refs, features, count):
    squares, gain_ref, att_ref, out_ref, column_ref = refs[:count], *refs[count:]
    step = pl.program_id(0)

    @pl.when(step == 0)
    def _():
        total = squares[0][...]
        for other in squares[1:]:
            total = total + other[...]
        inverse = lax.rsqrt(total / features + 1e-06)
        row = lax.broadcasted_iota(jnp.int32, (16, inverse.shape[1]), 0)
        pieces = jnp.zeros(row.shape, F32)
        for i, piece in enumerate(split_bf16(inverse)):
            pieces = jnp.where(row == i, piece.astype(F32), pieces)
        column_ref[...] = dot(pieces.astype(BF16), jnp.ones((16, HEAD_DIM), BF16), ((0,), (0,)))

    height = out_ref.shape[0]
    rows = pl.ds(pl.multiple_of(step * height, height), height)
    column = column_ref[rows, :]
    for c in range(out_ref.shape[1] // HEAD_DIM):
        cols = slice(c * HEAD_DIM, (c + 1) * HEAD_DIM)
        out_ref[:, cols] = (att_ref[rows, cols] * column * gain_ref[:, cols]).astype(BF16)


def local(queries, key_vectors, value_vectors, decay_rate, norm_gain, *, zp, nc, ne, nt):
    rows, width = queries.shape
    heads_all = width // HEAD_DIM
    blocks = rows // BLK
    group = zp * ne
    heads = heads_all // group
    part = heads * HEAD_DIM
    z, x = lax.axis_index("ctx"), lax.axis_index("exp")
    who = jnp.reshape((z % zp) * ne + x, (1,)).astype(jnp.int32)
    smem = pl.BlockSpec(memory_space=pltpu.SMEM)
    vmem = pl.BlockSpec(memory_space=pltpu.VMEM)
    hbm = pl.BlockSpec(memory_space=pltpu.HBM)
    state_type = jax.ShapeDtypeStruct((part, HEAD_DIM), F32)
    order = list(range(1, group))

    *slots, terms = pl.pallas_call(
        functools.partial(spread_kernel, group=group, blocks=blocks, heads=heads, order=order + [0]),
        in_specs=[smem, hbm, hbm, hbm],
        out_specs=[vmem] * (group + 1),
        out_shape=[state_type] * group + [jax.ShapeDtypeStruct((max(blocks - 1, 1), group, part, HEAD_DIM), F32)],
        scratch_shapes=[
            pltpu.SMEM((heads_all,), F32),
            pltpu.VMEM((group, rows, part), BF16),
            pltpu.VMEM((group, rows, part), BF16),
            pltpu.SemaphoreType.DMA((2, group)),
            pltpu.SemaphoreType.DMA,
        ],
        compiler_params=params(),
        name="spread",
    )(who, *(pltpu.with_memory_space_constraint(a, pltpu.HBM) for a in (decay_rate, key_vectors, value_vectors)))

    def swap(value, d):
        pairs = []
        for zz in range(nc):
            for xx in range(ne):
                m = ((zz % zp) * ne + xx) ^ d
                pairs.append((zz * ne + xx, (zz // zp * zp + m // ne) * ne + m % ne))
        return lax.ppermute(value, ("ctx", "exp"), pairs)

    got = {d: swap(slots[d], d) for d in order}
    slots = [slots[0]] + [got[d] for d in range(1, group)]

    one_head = pl.BlockSpec((rows, HEAD_DIM), lambda h: (0, h))
    local_part, inner = pl.pallas_call(
        functools.partial(local_kernel, blocks=blocks),
        grid=(heads_all,),
        in_specs=[smem, one_head, one_head, one_head],
        out_specs=[one_head, pl.BlockSpec((1, BLK, HEAD_DIM), lambda h: (h, 0, 0))],
        out_shape=[jax.ShapeDtypeStruct((rows, width), F32), jax.ShapeDtypeStruct((heads_all, BLK, HEAD_DIM), F32)],
        compiler_params=params(),
        cost_estimate=pl.CostEstimate(flops=4 * rows * BLK * width, bytes_accessed=10 * rows * width, transcendentals=0),
        name="local_part",
    )(decay_rate, queries, key_vectors, value_vectors)

    span = float(rows)
    total = pl.pallas_call(
        functools.partial(total_kernel, group=group, heads=heads, span=span),
        in_specs=[smem, smem, pl.BlockSpec(memory_space=pl.ANY)] + [vmem] * group,
        out_specs=vmem,
        out_shape=state_type,
        compiler_params=params(),
        name="group_total",
    )(who, decay_rate, inner, *slots)
    groups = nc // zp
    before = lax.ppermute(total, "ctx", [(zz, zz + zp) for zz in range(nc - zp)])
    step = 1
    while step < groups - 1:
        rates = lax.dynamic_slice_in_dim(decay_rate, who[0] * heads, heads)
        scale = jnp.repeat(jnp.exp(-rates * (span * group * step)), HEAD_DIM)[:, None]
        moved = lax.ppermute(before, "ctx", [(zz, zz + zp * step) for zz in range(nc - zp * step)])
        before = before + scale * moved
        step *= 2

    carries = pl.pallas_call(
        functools.partial(carry_kernel, group=group, heads=heads, span=span),
        in_specs=[smem, smem] + [vmem] * (group + 1),
        out_specs=[vmem] * group,
        out_shape=[state_type] * group,
        compiler_params=params(),
        name="carry",
    )(who, decay_rate, before, *slots)
    got = {d: swap(carries[d], d) for d in order}
    carries = [carries[0]] + [got[d] for d in range(1, group)]

    attended, squares = pl.pallas_call(
        functools.partial(carried_kernel, group=group, blocks=blocks, heads=heads),
        in_specs=[smem, smem] + [vmem] * (4 + group),
        out_specs=[vmem, vmem],
        out_shape=[jax.ShapeDtypeStruct((rows, width), F32), jax.ShapeDtypeStruct((1, rows), F32)],
        scratch_shapes=[pltpu.VMEM((rows, HEAD_DIM), F32)],
        compiler_params=params(),
        name="carried",
    )(who, decay_rate, queries, local_part, terms, inner, *carries)

    if nt & (nt - 1) == 0:
        swaps = [[(i, i ^ d) for i in range(nt)] for d in range(1, nt)]
    else:
        swaps = [[(i, (i + d) % nt) for i in range(nt)] for d in range(1, nt)]
    sums = [squares] + [lax.ppermute(squares, "tp", pairs) for pairs in swaps[::-1]]

    height = rows // 4
    return pl.pallas_call(
        functools.partial(norm_kernel, features=float(width * nt), count=nt),
        grid=(rows // height,),
        in_specs=[vmem] * (nt + 2),
        out_specs=pl.BlockSpec((height, width), lambda i: (i, 0)),
        out_shape=jax.ShapeDtypeStruct((rows, width), BF16),
        scratch_shapes=[pltpu.VMEM((rows, HEAD_DIM), F32)],
        compiler_params=params(),
        name="norm",
    )(*sums, norm_gain[None, :], attended)


def solution(mesh):
    nc, ne, nt = mesh.shape["ctx"], mesh.shape["exp"], mesh.shape["tp"]

    def whole(queries, key_vectors, value_vectors, decay_rate, norm_gain):
        heads_local = decay_rate.shape[0] // nt
        zp = 2 if nc % 2 == 0 and heads_local % (2 * ne) == 0 else 1
        return jax.shard_map(
            functools.partial(local, zp=zp, nc=nc, ne=ne, nt=nt),
            mesh=mesh,
            in_specs=(P(("ctx", "exp"), "tp"),) * 3 + (P("tp"), P("tp")),
            out_specs=P(("ctx", "exp"), "tp"),
            check_vma=False,
        )(queries, key_vectors, value_vectors, decay_rate, norm_gain)

    return whole
```

time: 44 us -> 42.3 us (0.961)
  local copies, waits for them, and re-layouts: 3.21 us -> 1.24 us
  starting transfers between devices: 15.8 us -> 16.6 us
    unnamed x14 -> x12, local copies, waits for them, and re-layouts: 3.21 us -> 1.24 us
    pallas_call x1, Pallas kernels: 2.44 us -> 1.67 us  [local(): pl.pallas_call(functools.partial(carried_kernel, group=group, blocks=bloc...]
    ppermute x6, starting transfers between devices: 9.23 us -> 9.81 us  [swap(): return lax.ppermute(value, ('ctx', 'exp'), pairs)]
  transfers between devices with their start and end apart: 10 -> 10, of which waited for: 6 -> 5; matrix products, arithmetic and copies ran while one was open for 0% -> 0% of each run, Pallas kernels for 13% -> 14%
where the time goes in v2:
time: 42.3 us; the launch traced here: 42.2 us
  starting transfers between devices  16.6 us (39%)
  Pallas kernels  13.1 us (31%)
  waiting for transfers between devices  11.1 us (26%)
  local copies, waits for them, and re-layouts  1.24 us (3%)
    ppermute x6, starting transfers between devices, swap(): return lax.ppermute(value, ('ctx', 'exp'), pairs)  9.81 us
    ppermute x6, waiting for transfers between devices, swap(): return lax.ppermute(value, ('ctx', 'exp'), pairs)  5.87 us
    pallas_call x1, Pallas kernels, local(): pl.pallas_call(functools.partial(local_kernel, blocks=blocks), grid=(head...  5.79 us
    ppermute x1, starting transfers between devices, local(): lax.ppermute(total, 'ctx', [(zz, zz + zp) for zz in range(nc - zp)])  4.91 us
    ppermute x3, waiting for transfers between devices, local(): lax.ppermute(squares, 'tp', pairs)  2.73 us
    ppermute x1, waiting for transfers between devices, local(): lax.ppermute(total, 'ctx', [(zz, zz + zp) for zz in range(nc - zp)])  2.51 us
    pallas_call x1, Pallas kernels, local(): pl.pallas_call(functools.partial(spread_kernel, group=group, blocks=block...  2.43 us
    pallas_call x1, Pallas kernels, local(): pl.pallas_call(functools.partial(norm_kernel, features=float(width * nt),...  1.92 us
  transfers between devices with their start and end apart: 10, of which 5 were waited for; matrix products, arithmetic and copies ran while one was open for 0% of the time, Pallas kernels for 14%

profile of v2, /device:TPU:0, one launch (start us, length us, event | category | flops | bytes accessed | tf_op | source)
XLA Modules:
  0.0 42.2 jit_solution(12053996046643926216)
XLA Ops:
  0.0 0.0 copy-start.4
  0.0 0.0 copy-start.1
  0.0 0.0 copy-start
  0.0 2.4 %spread.1 = (f32[256,128]{1,0:T(8,128)S(1)}, f32[256,128]{1,0:T(8,128)S(1)}, f32[256,128]{1,0:T(8,128)S(1)}, f32[256,128]{1,0:T(8,128)S(1)}, f32[1,4,256,128]{3,2,1,0:T(8,128)S(1)}) custom-call(s32[1]{0:T(128)} %bitcast.who, f32[8]{0:T(128)} %rate_ref.7, bf16[512,1024]{1,0:T(8,128)(2,1)} %key_hbm.1, bf16[512,1024]{1,0:T(8,128)(2,1)} %value_hbm.1), custom_call_target="tpu_custom_call" | custom-call | tf_op jit(solution)/shard_map/spread/pallas_call | solution.py:186
  2.4 3.0 %collective-permute-start = (f32[256,128]{1,0:T(8,128)S(1)}, f32[256,128]{1,0:T(8,128)S(1)}, u32[]{:S(2)}, u32[]{:S(2)}) collective-permute-start(f32[256,128]{1,0:T(8,128)S(1)} %get-tuple-element.22), channel_id=1, source_target_pairs={{0,4},{4,0},{8,12},{12,8},{16,20},{20,16},{24,28},{28,24},{1,5},{5... | collective-permute-start | bytes 393224 | tf_op jit(solution)/shard_map/ppermute | solution.py:208
  5.5 1.6 %collective-permute-start.1 = (f32[256,128]{1,0:T(8,128)S(1)}, f32[256,128]{1,0:T(8,128)S(1)}, u32[]{:S(2)}, u32[]{:S(2)}) collective-permute-start(f32[256,128]{1,0:T(8,128)S(1)} %get-tuple-element.23), channel_id=1, source_target_pairs={{0,8},{4,12},{8,0},{12,4},{16,24},{20,28},{24,16},{28,20},{1,9},{5... | collective-permute-start | bytes 393224 | tf_op jit(solution)/shard_map/ppermute | solution.py:208
  7.0 0.0 collective-permute-start.2
  7.0 0.0 copy-done.4
  7.0 0.0 copy-done.1
  7.1 0.0 copy-done
  7.1 0.0 copy-start.2
  7.1 1.2 %copy-done.2 = bf16[512,1024]{1,0:T(8,128)(2,1)S(1)} copy-done((bf16[512,1024]{1,0:T(8,128)(2,1)S(1)}, bf16[512,1024]{1,0:T(8,128)(2,1)}, u32[]{:S(2)}) %copy-start.2) | copy-done | bytes 1048600
  8.3 0.0 copy-start.3
  8.3 5.8 %local_part.1 = (f32[512,1024]{1,0:T(8,128)S(1)}, f32[8,256,128]{2,1,0:T(8,128)S(1)}) custom-call(f32[8]{0:T(128)S(1)} %copy-done.4, bf16[512,1024]{1,0:T(8,128)(2,1)S(1)} %copy-done.2, bf16[512,1024]{1,0:T(8,128)(2,1)S(1)} %copy-done, bf16[512,1024]{1,0:T(8,128)(2,1)S(1)} %copy-done.1), custom_call_target="tpu_custom_call" | custom-call | flops 536870912 | bytes 5242880 | tf_op jit(solution)/shard_map/local_part/pallas_call | solution.py:214
  14.1 0.0 collective-permute-done.refs_1_
  14.1 0.0 collective-permute-done.1.refs_2_
  14.1 0.0 collective-permute-done.2.refs_3_
  14.1 0.6 %group_total.1 = f32[256,128]{1,0:T(8,128)S(1)} custom-call(s32[1]{0:T(128)} %bitcast.who, f32[8]{0:T(128)S(1)} %copy-done.4, f32[8,256,128]{2,1,0:T(8,128)S(1)} %get-tuple-element.20.after_ref.inner_ref, f32[256,128]{1,0:T(8,128)S(1)} %get-tuple-element.21.refs_0_, f32[256,128]{1,0:T(8,128)S(1)} %collective-permute-done.refs_1_, ...), custom_call_target="tpu_custom_call" | custom-call | tf_op jit(solution)/shard_map/group_total/pallas_call | solution.py:226
  14.7 4.9 %collective-permute-start.3 = (f32[256,128]{1,0:T(8,128)S(1)}, f32[256,128]{1,0:T(8,128)S(1)}, u32[]{:S(2)}, u32[]{:S(2)}) collective-permute-start(f32[256,128]{1,0:T(8,128)S(1)} %group_total.1), channel_id=1, source_target_pairs={{0,16},{8,24},{1,17},{9,25},{2,18},{10,26},{3,19},{11,27},{4,20},{... | collective-permute-start | bytes 393224 | tf_op jit(solution)/shard_map/ppermute | solution.py:235
  19.6 2.5 %collective-permute-done.3.before_ref = f32[256,128]{1,0:T(8,128)S(1)} collective-permute-done((f32[256,128]{1,0:T(8,128)S(1)}, f32[256,128]{1,0:T(8,128)S(1)}, u32[]{:S(2)}, u32[]{:S(2)}) %collective-permute-start.3) | collective-permute-done | bytes 131104 | tf_op jit(solution)/shard_map/ppermute | solution.py:235
  22.1 0.7 %carry.1 = (f32[256,128]{1,0:T(8,128)S(1)}, f32[256,128]{1,0:T(8,128)S(1)}, f32[256,128]{1,0:T(8,128)S(1)}, f32[256,128]{1,0:T(8,128)S(1)}) custom-call(s32[1]{0:T(128)} %bitcast.who, f32[8]{0:T(128)S(1)} %copy-done.4, f32[256,128]{1,0:T(8,128)S(1)} %collective-permute-done.3.before_ref, f32[256,128]{1,0:T(8,128)S(1)} %get-tuple-element.21.refs_0_, ...), custom_call_target="tpu_custom_call" | custom-call | tf_op jit(solution)/shard_map/carry/pallas_call | solution.py:244
  22.9 1.6 %collective-permute-start.4 = (f32[256,128]{1,0:T(8,128)S(1)}, f32[256,128]{1,0:T(8,128)S(1)}, u32[]{:S(2)}, u32[]{:S(2)}) collective-permute-start(f32[256,128]{1,0:T(8,128)S(1)} %get-tuple-element.26), channel_id=1, source_target_pairs={{0,4},{4,0},{8,12},{12,8},{16,20},{20,16},{24,28},{28,24},{1,5},{5... | collective-permute-start | bytes 393224 | tf_op jit(solution)/shard_map/ppermute | solution.py:208
  24.4 3.7 %collective-permute-start.5 = (f32[256,128]{1,0:T(8,128)S(1)}, f32[256,128]{1,0:T(8,128)S(1)}, u32[]{:S(2)}, u32[]{:S(2)}) collective-permute-start(f32[256,128]{1,0:T(8,128)S(1)} %get-tuple-element.27), channel_id=1, source_target_pairs={{0,8},{4,12},{8,0},{12,4},{16,24},{20,28},{24,16},{28,20},{1,9},{5... | collective-permute-start | bytes 393224 | tf_op jit(solution)/shard_map/ppermute | solution.py:208
  28.1 0.0 collective-permute-start.6
  28.1 0.0 collective-permute-done.4.refs_1_
  28.1 4.2 %collective-permute-done.5.refs_2_ = f32[256,128]{1,0:T(8,128)S(1)} collective-permute-done((f32[256,128]{1,0:T(8,128)S(1)}, f32[256,128]{1,0:T(8,128)S(1)}, u32[]{:S(2)}, u32[]{:S(2)}) %collective-permute-start.5) | collective-permute-done | bytes 131104 | tf_op jit(solution)/shard_map/ppermute | solution.py:208
  32.3 1.7 %collective-permute-done.6.refs_3_ = f32[256,128]{1,0:T(8,128)S(1)} collective-permute-done((f32[256,128]{1,0:T(8,128)S(1)}, f32[256,128]{1,0:T(8,128)S(1)}, u32[]{:S(2)}, u32[]{:S(2)}) %collective-permute-start.6) | collective-permute-done | bytes 131104 | tf_op jit(solution)/shard_map/ppermute | solution.py:208
  34.0 0.0 copy-done.3
  34.0 0.0 copy-start.5
  34.0 1.7 %carried.1 = (f32[512,1024]{1,0:T(8,128)S(1)}, f32[1,512]{1,0:T(1,128)S(1)}) custom-call(s32[1]{0:T(128)} %bitcast.who, f32[8]{0:T(128)S(1)} %copy-done.4, bf16[512,1024]{1,0:T(8,128)(2,1)S(1)} %copy-done.3, f32[512,1024]{1,0:T(8,128)S(1)} %get-tuple-element.18.local_ref, f32[1,4,256,128]{3,2,1,0:T(8,128)S(1)} %get-tuple-element.19.terms_ref, ...), custom_call_target="tpu_custom_call" | custom-call | tf_op jit(solution)/shard_map/carried/pallas_call | solution.py:255
  35.6 0.0 collective-permute-start.9
  35.6 1.6 %collective-permute-start.8 = (f32[1,512]{1,0:T(1,128)S(1)}, f32[1,512]{1,0:T(1,128)S(1)}, u32[]{:S(2)}, u32[]{:S(2)}) collective-permute-start(f32[1,512]{1,0:T(1,128)S(1)} %get-tuple-element.29.refs_0_), channel_id=1, source_target_pairs={{0,2},{1,3},{2,0},{3,1},{4,6},{5,7},{6,4},{7,5},{8,10},{9,11},{10,... | collective-permute-start | bytes 6152 | tf_op jit(solution)/shard_map/ppermute | solution.py:269
  37.2 0.3 collective-permute-start.7
  37.5 0.0 collective-permute-done.9.refs_3_
  37.5 1.8 %collective-permute-done.8.refs_2_ = f32[1,512]{1,0:T(1,128)S(1)} collective-permute-done((f32[1,512]{1,0:T(1,128)S(1)}, f32[1,512]{1,0:T(1,128)S(1)}, u32[]{:S(2)}, u32[]{:S(2)}) %collective-permute-start.8) | collective-permute-done | bytes 2080 | tf_op jit(solution)/shard_map/ppermute | solution.py:269
  39.3 0.9 %collective-permute-done.7.refs_1_ = f32[1,512]{1,0:T(1,128)S(1)} collective-permute-done((f32[1,512]{1,0:T(1,128)S(1)}, f32[1,512]{1,0:T(1,128)S(1)}, u32[]{:S(2)}, u32[]{:S(2)}) %collective-permute-start.7) | collective-permute-done | bytes 2080 | tf_op jit(solution)/shard_map/ppermute | solution.py:269
  40.2 0.0 copy-done.5
  40.2 1.9 %norm.1 = bf16[512,1024]{1,0:T(8,128)(2,1)} custom-call(f32[1,512]{1,0:T(1,128)S(1)} %get-tuple-element.29.refs_0_, f32[1,512]{1,0:T(1,128)S(1)} %collective-permute-done.7.refs_1_, f32[1,512]{1,0:T(1,128)S(1)} %collective-permute-done.8.refs_2_, f32[1,512]{1,0:T(1,128)S(1)} %collective-permute-done.9.refs_3_, f32[1,1024]{1,0:T(1,128)S(1)} %bitcast.2, ...), custom_call_target="tpu_custom_call" | custom-call | tf_op jit(solution)/shard_map/norm/pallas_call | solution.py:272
Async XLA Ops:
  0.0 7.0 %copy-start.4 = (f32[8]{0:T(128)S(1)}, f32[8]{0:T(128)}, u32[]{:S(2)}) copy-start(f32[8]{0:T(128)} %rate_ref.7) | copy-start | bytes 100
  0.0 7.0 %copy-start.1 = (bf16[512,1024]{1,0:T(8,128)(2,1)S(1)}, bf16[512,1024]{1,0:T(8,128)(2,1)}, u32[]{:S(2)}) copy-start(bf16[512,1024]{1,0:T(8,128)(2,1)} %value_hbm.1) | copy-start | bytes 3145732
  0.0 7.0 %copy-start = (bf16[512,1024]{1,0:T(8,128)(2,1)S(1)}, bf16[512,1024]{1,0:T(8,128)(2,1)}, u32[]{:S(2)}) copy-start(bf16[512,1024]{1,0:T(8,128)(2,1)} %key_hbm.1) | copy-start | bytes 3145732
  2.4 11.6 %collective-permute-start = (f32[256,128]{1,0:T(8,128)S(1)}, f32[256,128]{1,0:T(8,128)S(1)}, u32[]{:S(2)}, u32[]{:S(2)}) collective-permute-start(f32[256,128]{1,0:T(8,128)S(1)} %get-tuple-element.22), channel_id=1, source_target_pairs={{0,4},{4,0},{8,12},{12,8},{16,20},{20,16},{24,28},{28,24},{1,5},{5... | collective-permute-start | bytes 393224 | tf_op jit(solution)/shard_map/ppermute | solution.py:208
  5.5 8.6 %collective-permute-start.1 = (f32[256,128]{1,0:T(8,128)S(1)}, f32[256,128]{1,0:T(8,128)S(1)}, u32[]{:S(2)}, u32[]{:S(2)}) collective-permute-start(f32[256,128]{1,0:T(8,128)S(1)} %get-tuple-element.23), channel_id=1, source_target_pairs={{0,8},{4,12},{8,0},{12,4},{16,24},{20,28},{24,16},{28,20},{1,9},{5... | collective-permute-start | bytes 393224 | tf_op jit(solution)/shard_map/ppermute | solution.py:208
  7.0 7.1 %collective-permute-start.2 = (f32[256,128]{1,0:T(8,128)S(1)}, f32[256,128]{1,0:T(8,128)S(1)}, u32[]{:S(2)}, u32[]{:S(2)}) collective-permute-start(f32[256,128]{1,0:T(8,128)S(1)} %get-tuple-element.24), channel_id=1, source_target_pairs={{0,12},{4,8},{8,4},{12,0},{16,28},{20,24},{24,20},{28,16},{1,13},{... | collective-permute-start | bytes 393224 | tf_op jit(solution)/shard_map/ppermute | solution.py:208
  7.1 1.2 %copy-start.2 = (bf16[512,1024]{1,0:T(8,128)(2,1)S(1)}, bf16[512,1024]{1,0:T(8,128)(2,1)}, u32[]{:S(2)}) copy-start(bf16[512,1024]{1,0:T(8,128)(2,1)} %query_ref.3) | copy-start | bytes 3145732
  8.3 25.7 %copy-start.3 = (bf16[512,1024]{1,0:T(8,128)(2,1)S(1)}, bf16[512,1024]{1,0:T(8,128)(2,1)}, u32[]{:S(2)}) copy-start(bf16[512,1024]{1,0:T(8,128)(2,1)} %query_ref.3) | copy-start | bytes 3145732
  14.7 7.4 %collective-permute-start.3 = (f32[256,128]{1,0:T(8,128)S(1)}, f32[256,128]{1,0:T(8,128)S(1)}, u32[]{:S(2)}, u32[]{:S(2)}) collective-permute-start(f32[256,128]{1,0:T(8,128)S(1)} %group_total.1), channel_id=1, source_target_pairs={{0,16},{8,24},{1,17},{9,25},{2,18},{10,26},{3,19},{11,27},{4,20},{... | collective-permute-start | bytes 393224 | tf_op jit(solution)/shard_map/ppermute | solution.py:235
  22.9 5.2 %collective-permute-start.4 = (f32[256,128]{1,0:T(8,128)S(1)}, f32[256,128]{1,0:T(8,128)S(1)}, u32[]{:S(2)}, u32[]{:S(2)}) collective-permute-start(f32[256,128]{1,0:T(8,128)S(1)} %get-tuple-element.26), channel_id=1, source_target_pairs={{0,4},{4,0},{8,12},{12,8},{16,20},{20,16},{24,28},{28,24},{1,5},{5... | collective-permute-start | bytes 393224 | tf_op jit(solution)/shard_map/ppermute | solution.py:208
  24.4 7.8 %collective-permute-start.5 = (f32[256,128]{1,0:T(8,128)S(1)}, f32[256,128]{1,0:T(8,128)S(1)}, u32[]{:S(2)}, u32[]{:S(2)}) collective-permute-start(f32[256,128]{1,0:T(8,128)S(1)} %get-tuple-element.27), channel_id=1, source_target_pairs={{0,8},{4,12},{8,0},{12,4},{16,24},{20,28},{24,16},{28,20},{1,9},{5... | collective-permute-start | bytes 393224 | tf_op jit(solution)/shard_map/ppermute | solution.py:208
  28.1 5.9 %collective-permute-start.6 = (f32[256,128]{1,0:T(8,128)S(1)}, f32[256,128]{1,0:T(8,128)S(1)}, u32[]{:S(2)}, u32[]{:S(2)}) collective-permute-start(f32[256,128]{1,0:T(8,128)S(1)} %get-tuple-element.28), channel_id=1, source_target_pairs={{0,12},{4,8},{8,4},{12,0},{16,28},{20,24},{24,20},{28,16},{1,13},{... | collective-permute-start | bytes 393224 | tf_op jit(solution)/shard_map/ppermute | solution.py:208
  34.0 6.3 %copy-start.5 = (f32[1024]{0:T(1024)S(1)}, f32[1024]{0:T(1024)}, u32[]{:S(2)}) copy-start(f32[1024]{0:T(1024)} %param.9) | copy-start | bytes 12292
  35.6 1.9 %collective-permute-start.9 = (f32[1,512]{1,0:T(1,128)S(1)}, f32[1,512]{1,0:T(1,128)S(1)}, u32[]{:S(2)}, u32[]{:S(2)}) collective-permute-start(f32[1,512]{1,0:T(1,128)S(1)} %get-tuple-element.29.refs_0_), channel_id=1, source_target_pairs={{0,1},{1,0},{2,3},{3,2},{4,5},{5,4},{6,7},{7,6},{8,9},{9,8},{10,11... | collective-permute-start | bytes 6152 | tf_op jit(solution)/shard_map/ppermute | solution.py:269
  35.6 3.7 %collective-permute-start.8 = (f32[1,512]{1,0:T(1,128)S(1)}, f32[1,512]{1,0:T(1,128)S(1)}, u32[]{:S(2)}, u32[]{:S(2)}) collective-permute-start(f32[1,512]{1,0:T(1,128)S(1)} %get-tuple-element.29.refs_0_), channel_id=1, source_target_pairs={{0,2},{1,3},{2,0},{3,1},{4,6},{5,7},{6,4},{7,5},{8,10},{9,11},{10,... | collective-permute-start | bytes 6152 | tf_op jit(solution)/shard_map/ppermute | solution.py:269
  37.2 3.0 %collective-permute-start.7 = (f32[1,512]{1,0:T(1,128)S(1)}, f32[1,512]{1,0:T(1,128)S(1)}, u32[]{:S(2)}, u32[]{:S(2)}) collective-permute-start(f32[1,512]{1,0:T(1,128)S(1)} %get-tuple-element.29.refs_0_), channel_id=1, source_target_pairs={{0,3},{1,2},{2,1},{3,0},{4,7},{5,6},{6,5},{7,4},{8,11},{9,10},{10,... | collective-permute-start | bytes 6152 | tf_op jit(solution)/shard_map/ppermute | solution.py:269

commit v3 on v0

v3 whole, which is shorter than its diff:
```python
import functools
import jax
import jax.numpy as jnp
from jax import lax
from jax.experimental import pallas as pl
from jax.experimental.pallas import tpu as pltpu
from jax.sharding import PartitionSpec as P

HEAD_DIM = 128
BLK = 256
F32 = jnp.float32
BF16 = jnp.bfloat16


def dot(a, b, dims):
    return lax.dot_general(a, b, (dims, ((), ())), preferred_element_type=F32)


def params(mib=32):
    return pltpu.CompilerParams(vmem_limit_bytes=mib << 20)


def head_rows(h):
    return slice(h * HEAD_DIM, (h + 1) * HEAD_DIM)


def split_bf16(value):
    high = value.astype(BF16)
    rest = value - high.astype(F32)
    middle = rest.astype(BF16)
    return high, middle, (rest - middle.astype(F32)).astype(BF16)


def member(zp, ne):
    return (lax.axis_index("ctx") % zp) * ne + lax.axis_index("exp")


def load_kernel(rate_hbm, query_hbm, key_hbm, value_hbm, rates_ref, query_ref, key_ref, value_ref, rate_smem, sems, *, zp, ne, heads, order):
    me = member(zp, ne)
    part = heads * HEAD_DIM
    copies = []
    for n, (source, held) in enumerate(((key_hbm, key_ref), (value_hbm, value_ref), (query_hbm, query_ref))):
        for d in order:
            cols = pl.ds(pl.multiple_of((me ^ d) * part, part), part)
            copies.append(pltpu.make_async_copy(source.at[:, cols], held.at[d], sems.at[n, d]))
    rate_copy = pltpu.make_async_copy(rate_hbm, rate_smem, sems.at[3, 0])
    rate_copy.start()
    for copy in copies:
        copy.start()
    rate_copy.wait()
    for d in order:
        for h in range(heads):
            rates_ref[d, h] = jnp.full((8, HEAD_DIM), rate_smem[(me ^ d) * heads + h], F32)
    for copy in copies:
        copy.wait()


def spread_kernel(rates_ref, key_ref, value_ref, state_ref, terms_ref, *, d, blocks, heads):
    left = (BLK - lax.broadcasted_iota(jnp.int32, (BLK, HEAD_DIM), 0)).astype(F32)
    for h in range(heads):
        here = head_rows(h)
        rate = rates_ref[d, h][:1, :]
        tail = jnp.exp(-rate * left)
        block_decay = jnp.exp(-rate * BLK)
        own = None
        for b in range(blocks):
            rows = slice(b * BLK, (b + 1) * BLK)
            keys = (key_ref[d, rows, here].astype(F32) * tail).astype(BF16)
            term = dot(keys, value_ref[d, rows, here], ((0,), (0,)))
            if b < blocks - 1:
                terms_ref[b, here, :] = term
            own = term if own is None else block_decay * own + term
        state_ref[here, :] = own


def local_kernel(rates_ref, query_ref, key_ref, value_ref, out_ref, inner_ref, *, blocks, heads, group):
    sub = HEAD_DIM
    count = BLK // sub
    i = lax.broadcasted_iota(jnp.int32, (sub, sub), 0)
    j = lax.broadcasted_iota(jnp.int32, (sub, sub), 1)
    apart = (i - j).astype(F32)
    offset = lax.broadcasted_iota(jnp.int32, (BLK, HEAD_DIM), 0).astype(F32)
    for d in range(group):
        for h in range(heads):
            rate = rates_ref[d, h][:1, :]
            weights = [jnp.where(apart >= 0, jnp.exp(-rate * jnp.maximum(apart, 0.0)), 0.0)]
            weights += [jnp.exp(-rate * (apart + float(sub * n))) for n in range(1, count)]
            inner_ref[d, h] = jnp.exp(-rate * offset)
            cols = head_rows(h)
            for b in range(blocks):
                for n in range(count):
                    rows = slice(b * BLK + n * sub, b * BLK + (n + 1) * sub)
                    seen = slice(b * BLK, b * BLK + (n + 1) * sub)
                    scores = dot(query_ref[d, rows, cols], key_ref[d, seen, cols], ((1,), (1,)))
                    weight = weights[0] if n == 0 else jnp.concatenate(weights[n::-1], axis=1)
                    mixing = (scores * weight).astype(BF16)
                    out_ref[d, rows, cols] = dot(mixing, value_ref[d, seen, cols], ((1,), (0,)))


def span_weight(rate, gap, span):
    return jnp.where(gap >= 0, jnp.exp(-rate * (jnp.maximum(gap, 0).astype(F32) * span)), 0.0)


def total_kernel(rates_ref, after_ref, *refs, ring, heads, span, zp, ne):
    group = len(ring)
    slots, out = refs[:group], refs[group]
    me = member(zp, ne)
    for h in range(heads):
        rate = rates_ref[0, h][:1, :]
        total = None
        for e, slot in zip(ring, slots):
            part = span_weight(rate, group - 1 - (me ^ e), span) * slot[head_rows(h), :]
            total = part if total is None else total + part
        out[head_rows(h), :] = total


def carry_kernel(rates_ref, before_ref, *refs, ring, heads, span, zp, ne):
    group = len(ring)
    slots, outs = refs[:group], refs[group:]
    me = member(zp, ne)
    has_before = lax.axis_index("ctx") >= zp
    for h in range(heads):
        rate = rates_ref[0, h][:1, :]
        parts = [slot[head_rows(h), :] for slot in slots]
        before = jnp.where(has_before, before_ref[head_rows(h), :], 0.0)
        for d, out in zip(ring, outs):
            carry = span_weight(rate, me ^ d, span) * before
            for e, part in zip(ring, parts):
                if e != d:
                    carry = carry + span_weight(rate, (me ^ d) - (me ^ e) - 1, span) * part
            out[head_rows(h), :] = carry


def carried_kernel(rates_ref, query_ref, local_ref, inner_ref, *refs, ds, blocks, heads):
    count = len(ds)
    terms, carries, (att_ref, acc_ref) = refs[:count], refs[count : 2 * count], refs[2 * count :]
    for i, d in enumerate(ds):
        for h in range(heads):
            here = head_rows(h)
            block_decay = jnp.exp(-rates_ref[d, h][:1, :] * BLK)
            state = carries[i][here, :]
            for b in range(blocks):
                rows = slice(b * BLK, (b + 1) * BLK)
                carried = dot(query_ref[d, rows, here], state.astype(BF16), ((1,), (0,)))
                att = local_ref[d, rows, here] + carried * inner_ref[d, h]
                att_ref[i, rows, here] = att
                if i == 0 and h == 0:
                    acc_ref[rows, :] = att * att
                else:
                    acc_ref[rows, :] += att * att
                if b < blocks - 1:
                    state = block_decay * state + terms[i][b, here, :]


def squares_kernel(*refs):
    parts, out_ref = refs[:-1], refs[-1]
    squares = parts[0][...]
    for other in parts[1:]:
        squares = squares + other[...]
    ones = jnp.ones((8, HEAD_DIM), BF16)
    total = None
    for piece in split_bf16(squares):
        add = dot(ones, piece, ((1,), (1,)))
        total = add if total is None else total + add
    out_ref[...] = total[:1, :]


def norm_kernel(*refs, features, count, steps, parts, zp, ne, heads):
    squares, gain_ref, refs = refs[:count], refs[count], refs[count + 1 :]
    atts, (out_hbm, out_ref, column_ref, sems) = refs[: len(parts)], refs[len(parts) :]
    me = member(zp, ne)
    total = squares[0][...]
    for other in squares[1:]:
        total = total + other[...]
    inverse = lax.rsqrt(total / features + 1e-06)
    row = lax.broadcasted_iota(jnp.int32, (16, inverse.shape[1]), 0)
    pieces = jnp.zeros(row.shape, F32)
    for i, piece in enumerate(split_bf16(inverse)):
        pieces = jnp.where(row == i, piece.astype(F32), pieces)
    column_ref[...] = dot(pieces.astype(BF16), jnp.ones((16, HEAD_DIM), BF16), ((0,), (0,)))
    height = out_ref.shape[0] // steps
    copies = []
    for step in range(steps):
        rows = slice(step * height, (step + 1) * height)
        column = column_ref[rows, :]
        for att, ds in zip(atts, parts):
            for i, d in enumerate(ds):
                for h in range(heads):
                    cols = pl.ds(pl.multiple_of(((me ^ d) * heads + h) * HEAD_DIM, HEAD_DIM), HEAD_DIM)
                    out_ref[rows, cols] = (att[i, rows, head_rows(h)] * column * gain_ref[:, cols]).astype(BF16)
        copies.append(pltpu.make_async_copy(out_ref.at[rows, :], out_hbm.at[rows, :], sems.at[step]))
        copies[-1].start()
    for copy in copies:
        copy.wait()


def local(queries, key_vectors, value_vectors, decay_rate, norm_gain, *, zp, nc, ne, nt):
    rows, width = queries.shape
    heads_all = width // HEAD_DIM
    blocks = rows // BLK
    group = zp * ne
    groups = nc // zp
    heads = heads_all // group
    part = heads * HEAD_DIM
    span = float(rows)
    vmem = pl.BlockSpec(memory_space=pltpu.VMEM)
    hbm = pl.BlockSpec(memory_space=pltpu.HBM)
    anywhere = pl.BlockSpec(memory_space=pl.ANY)
    ring = (0, 3, 2, 1) if group == 4 else tuple(range(group))
    state_type = jax.ShapeDtypeStruct((part, HEAD_DIM), F32)
    term_type = jax.ShapeDtypeStruct((max(blocks - 1, 1), part, HEAD_DIM), F32)
    held_type = jax.ShapeDtypeStruct((group, rows, part), BF16)
    where = dict(zp=zp, ne=ne)

    def call(kernel, count, outs, name, **more):
        more = {"in_specs": [vmem] * count, "out_specs": [vmem] * len(outs), "out_shape": outs, "name": name, **more}
        return pl.pallas_call(kernel, compiler_params=params(), **more)

    pinned = [pltpu.with_memory_space_constraint(a, pltpu.HBM) for a in (decay_rate, queries, key_vectors, value_vectors)]
    order = ring[1:] + ring[:1]
    rates, query, key, value = call(
        functools.partial(load_kernel, heads=heads, order=order, **where),
        4,
        [jax.ShapeDtypeStruct((group, heads, 8, HEAD_DIM), F32), held_type, held_type, held_type],
        "load",
        in_specs=[hbm] * 4,
        scratch_shapes=[pltpu.SMEM((heads_all,), F32), pltpu.SemaphoreType.DMA((4, group))],
    )(*pinned)

    slots, terms = {}, {}
    for d in order:
        spread = functools.partial(spread_kernel, d=d, blocks=blocks, heads=heads)
        slots[d], terms[d] = call(spread, 3, [state_type, term_type], "spread")(rates, key, value)

    def swap(value, d):
        pairs = []
        for zz in range(nc):
            for xx in range(ne):
                m = ((zz % zp) * ne + xx) ^ d
                pairs.append((zz * ne + xx, (zz // zp * zp + m // ne) * ne + m % ne))
        return lax.ppermute(value, ("ctx", "exp"), pairs)

    slots = [slots[0]] + [swap(slots[d], d) for d in ring[1:]]

    local_part, inner = call(
        functools.partial(local_kernel, blocks=blocks, heads=heads, group=group),
        4,
        [jax.ShapeDtypeStruct((group, rows, part), F32), jax.ShapeDtypeStruct((group, heads, BLK, HEAD_DIM), F32)],
        "local_part",
        cost_estimate=pl.CostEstimate(flops=4 * rows * BLK * width, bytes_accessed=10 * rows * width, transcendentals=0),
    )(rates, query, key, value)

    (total,) = call(
        functools.partial(total_kernel, ring=ring, heads=heads, span=span, **where),
        group + 2,
        [state_type],
        "group_total",
        in_specs=[vmem, anywhere] + [vmem] * group,
    )(rates, inner, *slots)

    if groups == 2:
        before = lax.ppermute(total, "ctx", [(zz, (zz + zp) % nc) for zz in range(nc)])
    else:
        before = lax.ppermute(total, "ctx", [(zz, zz + zp) for zz in range(nc - zp)])
    step = 1
    while step < groups - 1:
        scale = jnp.exp(-rates[0, :, :1, :] * (span * group * step))
        moved = lax.ppermute(before, "ctx", [(zz, zz + zp * step) for zz in range(nc - zp * step)])
        before = before + (scale * moved.reshape(heads, HEAD_DIM, HEAD_DIM)).reshape(part, HEAD_DIM)
        step *= 2

    carries = call(
        functools.partial(carry_kernel, ring=ring, heads=heads, span=span, **where), group + 2, [state_type] * group, "carry"
    )(rates, before, *slots)
    carries = [carries[0]] + [swap(carry, d) for carry, d in zip(carries[1:], ring[1:])]

    parts = [(d,) for d in ring]
    attended, squares, at = [], [], 0
    for ds in parts:
        att, acc = call(
            functools.partial(carried_kernel, ds=ds, blocks=blocks, heads=heads),
            4 + 2 * len(ds),
            [jax.ShapeDtypeStruct((len(ds), rows, part), F32), jax.ShapeDtypeStruct((rows, HEAD_DIM), F32)],
            "carried",
        )(rates, query, local_part, inner, *(terms[d] for d in ds), *carries[at : at + len(ds)])
        attended.append(att)
        squares.append(acc)
        at += len(ds)
    (row_sum,) = call(squares_kernel, len(parts), [jax.ShapeDtypeStruct((1, rows), F32)], "row_squares")(*squares)

    if nt & (nt - 1) == 0:
        swaps = [[(i, i ^ d) for i in range(nt)] for d in range(1, nt)]
    else:
        swaps = [[(i, (i + d) % nt) for i in range(nt)] for d in range(1, nt)]
    row_sums = [row_sum] + [lax.ppermute(row_sum, "tp", pairs) for pairs in swaps[::-1]]

    steps = 4
    norm = functools.partial(norm_kernel, features=float(width * nt), count=nt, steps=steps, parts=parts, heads=heads, **where)
    (out,) = call(
        norm,
        nt + 1 + len(parts),
        [jax.ShapeDtypeStruct((rows, width), BF16)],
        "norm",
        out_specs=[hbm],
        scratch_shapes=[
            pltpu.VMEM((rows, width), BF16),
            pltpu.VMEM((rows, HEAD_DIM), F32),
            pltpu.SemaphoreType.DMA((steps,)),
        ],
    )(*row_sums, norm_gain[None, :], *attended)
    return out


def solution(mesh):
    nc, ne, nt = mesh.shape["ctx"], mesh.shape["exp"], mesh.shape["tp"]

    def whole(queries, key_vectors, value_vectors, decay_rate, norm_gain):
        heads_local = decay_rate.shape[0] // nt
        zp = 2 if nc % 2 == 0 and heads_local % (2 * ne) == 0 else 1
        return jax.shard_map(
            functools.partial(local, zp=zp, nc=nc, ne=ne, nt=nt),
            mesh=mesh,
            in_specs=(P(("ctx", "exp"), "tp"),) * 3 + (P("tp"), P("tp")),
            out_specs=P(("ctx", "exp"), "tp"),
            check_vma=False,
        )(queries, key_vectors, value_vectors, decay_rate, norm_gain)

    return whole
```

time: 128 us -> 37.1 us (0.29)
  waiting for transfers between devices: 46.3 us -> 14.6 us
  blocking collectives: 29.2 us -> 0 us
  between operations: 14.2 us -> 0.11 us
  local copies, waits for them, and re-layouts: 13.7 us -> 0.01 us
  starting transfers between devices: 0.01 us -> 12.9 us
  matrix products: 12 us -> 0 us
  other arithmetic: 11.6 us -> 0 us
  Pallas kernels: 0 us -> 9.25 us
    all_gather x1 -> x0, waiting for transfers between devices: 46.3 us -> none  [carried_in(): pieces = jax.tree.map(lambda part: lax.all_gather(part, axis), value)]
    unnamed x1 -> x0, blocking collectives: 23.5 us -> none
    ppermute x0 -> x10, waiting for transfers between devices: none -> 14.6 us  [the longest x6 7.06 us: swap(): return lax.ppermute(value, ('ctx', 'exp'), pairs)]
    ppermute x0 -> x10, starting transfers between devices: none -> 12.9 us  [the longest x6 8.37 us: swap(): return lax.ppermute(value, ('ctx', 'exp'), pairs)]
    dot_general x6 -> x0, matrix products: 12 us -> none  [the longest x2 6.45 us: local(): jnp.einsum('hts,she->the', mixing, value_block, preferred_element_type=jn...]
    pallas_call x0 -> x14, Pallas kernels: none -> 9.25 us  [the longest x1 3.36 us: local(): call(functools.partial(local_kernel, blocks=blocks, heads=heads, group=gr...]
    select_n x7 -> x0, other arithmetic: 8.2 us -> none  [hop(): jnp.where(position < mine, new, old)]
    psum x1 -> x0, blocking collectives: 5.67 us -> none  [local(): row_total = lax.psum(row_squares, 'tp')]
  transfers between devices with their start and end apart: 1 -> 10, of which waited for: 1 -> 8; matrix products, arithmetic and copies ran while one was open for 5% -> 0% of each run, Pallas kernels for 0% -> 13%
where the time goes in v3:
time: 37.1 us; the launch traced here: 36.9 us
  waiting for transfers between devices  14.6 us (39%)
  starting transfers between devices  12.9 us (35%)
  Pallas kernels  9.25 us (25%)
    ppermute x6, starting transfers between devices, swap(): return lax.ppermute(value, ('ctx', 'exp'), pairs)  8.37 us
    ppermute x6, waiting for transfers between devices, swap(): return lax.ppermute(value, ('ctx', 'exp'), pairs)  7.06 us
    ppermute x1, waiting for transfers between devices, local(): lax.ppermute(total, 'ctx', [(zz, (zz + zp) % nc) for zz in range(nc)])  4.83 us
    pallas_call x1, Pallas kernels, local(): call(functools.partial(local_kernel, blocks=blocks, heads=heads, group=gr...  3.36 us
    ppermute x3, waiting for transfers between devices, local(): lax.ppermute(row_sum, 'tp', pairs)  2.73 us
    ppermute x1, starting transfers between devices, local(): lax.ppermute(total, 'ctx', [(zz, (zz + zp) % nc) for zz in range(nc)])  2.65 us
    pallas_call x1, Pallas kernels, local(): call(functools.partial(load_kernel, heads=heads, order=order, **where), 4...  2 us
    ppermute x3, starting transfers between devices, local(): lax.ppermute(row_sum, 'tp', pairs)  1.88 us
  transfers between devices with their start and end apart: 10, of which 8 were waited for; matrix products, arithmetic and copies ran while one was open for 0% of the time, Pallas kernels for 13%

profile of v3, /device:TPU:0, one launch (start us, length us, event | category | flops | bytes accessed | tf_op | source)
XLA Modules:
  0.0 36.9 jit_solution(8071761052661453455)
XLA Ops:
  0.0 2.0 %load.1 = (f32[4,2,8,128]{3,2,1,0:T(8,128)S(1)}, bf16[4,512,256]{2,1,0:T(8,128)(2,1)S(1)}, bf16[4,512,256]{2,1,0:T(8,128)(2,1)S(1)}, bf16[4,512,256]{2,1,0:T(8,128)(2,1)S(1)}) custom-call(f32[8]{0:T(128)} %rate_hbm.1, bf16[512,1024]{1,0:T(8,128)(2,1)} %query_hbm.1, bf16[512,1024]{1,0:T(8,128)(2,1)} %key_hbm.1, bf16[512,1024]{1,0:T(8,128)(2,1)} %value_hbm.1), custom_call_target="tpu_custom_call" | custom-call | tf_op jit(solution)/shard_map/load/pallas_call | solution.py:221
  2.0 0.3 spread.7
  2.3 3.0 %collective-permute-start.2 = (f32[256,128]{1,0:T(8,128)S(1)}, f32[256,128]{1,0:T(8,128)S(1)}, u32[]{:S(2)}, u32[]{:S(2)}) collective-permute-start(f32[256,128]{1,0:T(8,128)S(1)} %get-tuple-element.41), channel_id=1, source_target_pairs={{0,4},{4,0},{8,12},{12,8},{16,20},{20,16},{24,28},{28,24},{1,5},{5... | collective-permute-start | bytes 393224 | tf_op jit(solution)/shard_map/ppermute | solution.py:241
  5.3 0.3 spread.6
  5.6 1.6 %collective-permute-start.1 = (f32[256,128]{1,0:T(8,128)S(1)}, f32[256,128]{1,0:T(8,128)S(1)}, u32[]{:S(2)}, u32[]{:S(2)}) collective-permute-start(f32[256,128]{1,0:T(8,128)S(1)} %get-tuple-element.40), channel_id=1, source_target_pairs={{0,8},{4,12},{8,0},{12,4},{16,24},{20,28},{24,16},{28,20},{1,9},{5... | collective-permute-start | bytes 393224 | tf_op jit(solution)/shard_map/ppermute | solution.py:241
  7.3 0.3 spread.5
  7.5 0.1 collective-permute-start
  7.6 0.3 spread.4
  7.9 3.4 %local_part.1 = (f32[4,512,256]{2,1,0:T(8,128)S(1)}, f32[4,2,256,128]{3,2,1,0:T(8,128)S(1)}) custom-call(f32[4,2,8,128]{3,2,1,0:T(8,128)S(1)} %get-tuple-element.31.rates_ref, bf16[4,512,256]{2,1,0:T(8,128)(2,1)S(1)} %get-tuple-element.32.query_ref, bf16[4,512,256]{2,1,0:T(8,128)(2,1)S(1)} %get-tuple-element.33.key_ref, ...), custom_call_target="tpu_custom_call" | custom-call | flops 536870912 | bytes 5242880 | tf_op jit(solution)/shard_map/local_part/pallas_call | solution.py:245
  11.3 0.0 collective-permute-done.2.refs_3_
  11.3 0.5 %collective-permute-done.1.refs_2_ = f32[256,128]{1,0:T(8,128)S(1)} collective-permute-done((f32[256,128]{1,0:T(8,128)S(1)}, f32[256,128]{1,0:T(8,128)S(1)}, u32[]{:S(2)}, u32[]{:S(2)}) %collective-permute-start.1) | collective-permute-done | bytes 131104 | tf_op jit(solution)/shard_map/ppermute | solution.py:241
  11.8 1.7 %collective-permute-done.refs_1_ = f32[256,128]{1,0:T(8,128)S(1)} collective-permute-done((f32[256,128]{1,0:T(8,128)S(1)}, f32[256,128]{1,0:T(8,128)S(1)}, u32[]{:S(2)}, u32[]{:S(2)}) %collective-permute-start) | collective-permute-done | bytes 131104 | tf_op jit(solution)/shard_map/ppermute | solution.py:241
  13.5 0.1 group_total.1
  13.5 2.7 %collective-permute-start.3 = (f32[256,128]{1,0:T(8,128)S(1)}, f32[256,128]{1,0:T(8,128)S(1)}, u32[]{:S(2)}, u32[]{:S(2)}) collective-permute-start(f32[256,128]{1,0:T(8,128)S(1)} %group_total.1), channel_id=1, source_target_pairs={{0,16},{8,24},{16,0},{24,8},{1,17},{9,25},{17,1},{25,9},{2,18},{10... | collective-permute-start | bytes 393224 | tf_op jit(solution)/shard_map/ppermute | solution.py:262
  16.2 4.8 %collective-permute-done.3.before_ref = f32[256,128]{1,0:T(8,128)S(1)} collective-permute-done((f32[256,128]{1,0:T(8,128)S(1)}, f32[256,128]{1,0:T(8,128)S(1)}, u32[]{:S(2)}, u32[]{:S(2)}) %collective-permute-start.3) | collective-permute-done | bytes 131104 | tf_op jit(solution)/shard_map/ppermute | solution.py:262
  21.0 0.2 carry.1
  21.2 2.1 %collective-permute-start.6 = (f32[256,128]{1,0:T(8,128)S(1)}, f32[256,128]{1,0:T(8,128)S(1)}, u32[]{:S(2)}, u32[]{:S(2)}) collective-permute-start(f32[256,128]{1,0:T(8,128)S(1)} %get-tuple-element.51), channel_id=1, source_target_pairs={{0,4},{4,0},{8,12},{12,8},{16,20},{20,16},{24,28},{28,24},{1,5},{5... | collective-permute-start | bytes 393224 | tf_op jit(solution)/shard_map/ppermute | solution.py:241
  23.3 0.2 collective-permute-start.5
  23.5 1.3 %collective-permute-start.4 = (f32[256,128]{1,0:T(8,128)S(1)}, f32[256,128]{1,0:T(8,128)S(1)}, u32[]{:S(2)}, u32[]{:S(2)}) collective-permute-start(f32[256,128]{1,0:T(8,128)S(1)} %get-tuple-element.45), channel_id=1, source_target_pairs={{0,12},{4,8},{8,4},{12,0},{16,28},{20,24},{24,20},{28,16},{1,13},{... | collective-permute-start | bytes 393224 | tf_op jit(solution)/shard_map/ppermute | solution.py:241
  24.9 0.2 carried.4
  25.1 1.7 %collective-permute-done.6.refs_1_ = f32[256,128]{1,0:T(8,128)S(1)} collective-permute-done((f32[256,128]{1,0:T(8,128)S(1)}, f32[256,128]{1,0:T(8,128)S(1)}, u32[]{:S(2)}, u32[]{:S(2)}) %collective-permute-start.6) | collective-permute-done | bytes 131104 | tf_op jit(solution)/shard_map/ppermute | solution.py:241
  26.8 0.2 carried.7
  27.0 2.3 %collective-permute-done.5.refs_1_ = f32[256,128]{1,0:T(8,128)S(1)} collective-permute-done((f32[256,128]{1,0:T(8,128)S(1)}, f32[256,128]{1,0:T(8,128)S(1)}, u32[]{:S(2)}, u32[]{:S(2)}) %collective-permute-start.5) | collective-permute-done | bytes 131104 | tf_op jit(solution)/shard_map/ppermute | solution.py:241
  29.3 0.2 carried.6
  29.5 1.0 %collective-permute-done.4.refs_1_ = f32[256,128]{1,0:T(8,128)S(1)} collective-permute-done((f32[256,128]{1,0:T(8,128)S(1)}, f32[256,128]{1,0:T(8,128)S(1)}, u32[]{:S(2)}, u32[]{:S(2)}) %collective-permute-start.4) | collective-permute-done | bytes 131104 | tf_op jit(solution)/shard_map/ppermute | solution.py:241
  30.5 0.0 copy-start
  30.5 0.2 carried.5
  30.7 0.2 row_squares.1.refs_0_
  30.9 0.0 collective-permute-start.9
  30.9 1.6 %collective-permute-start.8 = (f32[1,512]{1,0:T(1,128)S(1)}, f32[1,512]{1,0:T(1,128)S(1)}, u32[]{:S(2)}, u32[]{:S(2)}) collective-permute-start(f32[1,512]{1,0:T(1,128)S(1)} %row_squares.1.refs_0_), channel_id=1, source_target_pairs={{0,2},{1,3},{2,0},{3,1},{4,6},{5,7},{6,4},{7,5},{8,10},{9,11},{10,... | collective-permute-start | bytes 6152 | tf_op jit(solution)/shard_map/ppermute | solution.py:295
  32.5 0.3 collective-permute-start.7
  32.8 0.0 collective-permute-done.9.refs_3_
  32.8 1.8 %collective-permute-done.8.refs_2_ = f32[1,512]{1,0:T(1,128)S(1)} collective-permute-done((f32[1,512]{1,0:T(1,128)S(1)}, f32[1,512]{1,0:T(1,128)S(1)}, u32[]{:S(2)}, u32[]{:S(2)}) %collective-permute-start.8) | collective-permute-done | bytes 2080 | tf_op jit(solution)/shard_map/ppermute | solution.py:295
  34.6 0.9 %collective-permute-done.7.refs_1_ = f32[1,512]{1,0:T(1,128)S(1)} collective-permute-done((f32[1,512]{1,0:T(1,128)S(1)}, f32[1,512]{1,0:T(1,128)S(1)}, u32[]{:S(2)}, u32[]{:S(2)}) %collective-permute-start.7) | collective-permute-done | bytes 2080 | tf_op jit(solution)/shard_map/ppermute | solution.py:295
  35.5 0.0 copy-done
  35.5 1.4 %norm.1 = bf16[512,1024]{1,0:T(8,128)(2,1)} custom-call(f32[1,512]{1,0:T(1,128)S(1)} %row_squares.1.refs_0_, f32[1,512]{1,0:T(1,128)S(1)} %collective-permute-done.7.refs_1_, f32[1,512]{1,0:T(1,128)S(1)} %collective-permute-done.8.refs_2_, f32[1,512]{1,0:T(1,128)S(1)} %collective-permute-done.9.refs_3_, f32[1,1024]{1,0:T(1,128)S(1)} %bitcast.1, ...), custom_call_target="tpu_custom_call" | custom-call | tf_op jit(solution)/shard_map/norm/pallas_call | solution.py:299
Async XLA Ops:
  2.3 9.0 %collective-permute-start.2 = (f32[256,128]{1,0:T(8,128)S(1)}, f32[256,128]{1,0:T(8,128)S(1)}, u32[]{:S(2)}, u32[]{:S(2)}) collective-permute-start(f32[256,128]{1,0:T(8,128)S(1)} %get-tuple-element.41), channel_id=1, source_target_pairs={{0,4},{4,0},{8,12},{12,8},{16,20},{20,16},{24,28},{28,24},{1,5},{5... | collective-permute-start | bytes 393224 | tf_op jit(solution)/shard_map/ppermute | solution.py:241
  5.6 6.2 %collective-permute-start.1 = (f32[256,128]{1,0:T(8,128)S(1)}, f32[256,128]{1,0:T(8,128)S(1)}, u32[]{:S(2)}, u32[]{:S(2)}) collective-permute-start(f32[256,128]{1,0:T(8,128)S(1)} %get-tuple-element.40), channel_id=1, source_target_pairs={{0,8},{4,12},{8,0},{12,4},{16,24},{20,28},{24,16},{28,20},{1,9},{5... | collective-permute-start | bytes 393224 | tf_op jit(solution)/shard_map/ppermute | solution.py:241
  7.5 5.9 %collective-permute-start = (f32[256,128]{1,0:T(8,128)S(1)}, f32[256,128]{1,0:T(8,128)S(1)}, u32[]{:S(2)}, u32[]{:S(2)}) collective-permute-start(f32[256,128]{1,0:T(8,128)S(1)} %get-tuple-element.39), channel_id=1, source_target_pairs={{0,12},{4,8},{8,4},{12,0},{16,28},{20,24},{24,20},{28,16},{1,13},{... | collective-permute-start | bytes 393224 | tf_op jit(solution)/shard_map/ppermute | solution.py:241
  13.5 7.5 %collective-permute-start.3 = (f32[256,128]{1,0:T(8,128)S(1)}, f32[256,128]{1,0:T(8,128)S(1)}, u32[]{:S(2)}, u32[]{:S(2)}) collective-permute-start(f32[256,128]{1,0:T(8,128)S(1)} %group_total.1), channel_id=1, source_target_pairs={{0,16},{8,24},{16,0},{24,8},{1,17},{9,25},{17,1},{25,9},{2,18},{10... | collective-permute-start | bytes 393224 | tf_op jit(solution)/shard_map/ppermute | solution.py:262
  21.2 5.6 %collective-permute-start.6 = (f32[256,128]{1,0:T(8,128)S(1)}, f32[256,128]{1,0:T(8,128)S(1)}, u32[]{:S(2)}, u32[]{:S(2)}) collective-permute-start(f32[256,128]{1,0:T(8,128)S(1)} %get-tuple-element.51), channel_id=1, source_target_pairs={{0,4},{4,0},{8,12},{12,8},{16,20},{20,16},{24,28},{28,24},{1,5},{5... | collective-permute-start | bytes 393224 | tf_op jit(solution)/shard_map/ppermute | solution.py:241
  23.3 5.9 %collective-permute-start.5 = (f32[256,128]{1,0:T(8,128)S(1)}, f32[256,128]{1,0:T(8,128)S(1)}, u32[]{:S(2)}, u32[]{:S(2)}) collective-permute-start(f32[256,128]{1,0:T(8,128)S(1)} %get-tuple-element.48), channel_id=1, source_target_pairs={{0,8},{4,12},{8,0},{12,4},{16,24},{20,28},{24,16},{28,20},{1,9},{5... | collective-permute-start | bytes 393224 | tf_op jit(solution)/shard_map/ppermute | solution.py:241
  23.5 6.9 %collective-permute-start.4 = (f32[256,128]{1,0:T(8,128)S(1)}, f32[256,128]{1,0:T(8,128)S(1)}, u32[]{:S(2)}, u32[]{:S(2)}) collective-permute-start(f32[256,128]{1,0:T(8,128)S(1)} %get-tuple-element.45), channel_id=1, source_target_pairs={{0,12},{4,8},{8,4},{12,0},{16,28},{20,24},{24,20},{28,16},{1,13},{... | collective-permute-start | bytes 393224 | tf_op jit(solution)/shard_map/ppermute | solution.py:241
  30.5 5.1 %copy-start = (f32[1024]{0:T(1024)S(1)}, f32[1024]{0:T(1024)}, u32[]{:S(2)}) copy-start(f32[1024]{0:T(1024)} %param.9) | copy-start | bytes 12292
  30.9 1.9 %collective-permute-start.9 = (f32[1,512]{1,0:T(1,128)S(1)}, f32[1,512]{1,0:T(1,128)S(1)}, u32[]{:S(2)}, u32[]{:S(2)}) collective-permute-start(f32[1,512]{1,0:T(1,128)S(1)} %row_squares.1.refs_0_), channel_id=1, source_target_pairs={{0,1},{1,0},{2,3},{3,2},{4,5},{5,4},{6,7},{7,6},{8,9},{9,8},{10,11... | collective-permute-start | bytes 6152 | tf_op jit(solution)/shard_map/ppermute | solution.py:295
  30.9 3.7 %collective-permute-start.8 = (f32[1,512]{1,0:T(1,128)S(1)}, f32[1,512]{1,0:T(1,128)S(1)}, u32[]{:S(2)}, u32[]{:S(2)}) collective-permute-start(f32[1,512]{1,0:T(1,128)S(1)} %row_squares.1.refs_0_), channel_id=1, source_target_pairs={{0,2},{1,3},{2,0},{3,1},{4,6},{5,7},{6,4},{7,5},{8,10},{9,11},{10,... | collective-permute-start | bytes 6152 | tf_op jit(solution)/shard_map/ppermute | solution.py:295
  32.5 3.0 %collective-permute-start.7 = (f32[1,512]{1,0:T(1,128)S(1)}, f32[1,512]{1,0:T(1,128)S(1)}, u32[]{:S(2)}, u32[]{:S(2)}) collective-permute-start(f32[1,512]{1,0:T(1,128)S(1)} %row_squares.1.refs_0_), channel_id=1, source_target_pairs={{0,3},{1,2},{2,1},{3,0},{4,7},{5,6},{6,5},{7,4},{8,11},{9,10},{10,... | collective-permute-start | bytes 6152 | tf_op jit(solution)/shard_map/ppermute | solution.py:295

commit v4 on v3

--- a/solution.py
+++ b/solution.py
@@ -35,8 +35,13 @@
     return (lax.axis_index("ctx") % zp) * ne + lax.axis_index("exp")
 
 
-def load_kernel(rate_hbm, query_hbm, key_hbm, value_hbm, rates_ref, query_ref, key_ref, value_ref, rate_smem, sems, *, zp, ne, heads, order):
+def owned(zp, ne, mirror):
     me = member(zp, ne)
+    return me ^ (lax.axis_index("ctx") // zp % 2 * ne) if mirror else me
+
+
+def load_kernel(rate_hbm, query_hbm, key_hbm, value_hbm, rates_ref, query_ref, key_ref, value_ref, rate_smem, sems, *, zp, ne, mirror, heads, order):
+    me = owned(zp, ne, mirror)
     part = heads * HEAD_DIM
     copies = []
     for n, (source, held) in enumerate(((key_hbm, key_ref), (value_hbm, value_ref), (query_hbm, query_ref))):
@@ -114,7 +119,7 @@
         out[head_rows(h), :] = total
 
 
-def carry_kernel(rates_ref, before_ref, *refs, ring, heads, span, zp, ne):
+def carry_kernel(rates_ref, before_ref, *refs, ring, ring_out, heads, span, zp, ne):
     group = len(ring)
     slots, outs = refs[:group], refs[group:]
     me = member(zp, ne)
@@ -123,7 +128,7 @@
         rate = rates_ref[0, h][:1, :]
         parts = [slot[head_rows(h), :] for slot in slots]
         before = jnp.where(has_before, before_ref[head_rows(h), :], 0.0)
-        for d, out in zip(ring, outs):
+        for d, out in zip(ring_out, outs):
             carry = span_weight(rate, me ^ d, span) * before
             for e, part in zip(ring, parts):
                 if e != d:
@@ -131,44 +136,45 @@
             out[head_rows(h), :] = carry
 
 
-def carried_kernel(rates_ref, query_ref, local_ref, inner_ref, *refs, ds, blocks, heads):
-    count = len(ds)
-    terms, carries, (att_ref, acc_ref) = refs[:count], refs[count : 2 * count], refs[2 * count :]
-    for i, d in enumerate(ds):
-        for h in range(heads):
-            here = head_rows(h)
-            block_decay = jnp.exp(-rates_ref[d, h][:1, :] * BLK)
-            state = carries[i][here, :]
-            for b in range(blocks):
-                rows = slice(b * BLK, (b + 1) * BLK)
-                carried = dot(query_ref[d, rows, here], state.astype(BF16), ((1,), (0,)))
-                att = local_ref[d, rows, here] + carried * inner_ref[d, h]
-                att_ref[i, rows, here] = att
-                if i == 0 and h == 0:
-                    acc_ref[rows, :] = att * att
-                else:
-                    acc_ref[rows, :] += att * att
-                if b < blocks - 1:
-                    state = block_decay * state + terms[i][b, here, :]
-
-
-def squares_kernel(*refs):
-    parts, out_ref = refs[:-1], refs[-1]
-    squares = parts[0][...]
-    for other in parts[1:]:
-        squares = squares + other[...]
-    ones = jnp.ones((8, HEAD_DIM), BF16)
-    total = None
-    for piece in split_bf16(squares):
-        add = dot(ones, piece, ((1,), (1,)))
-        total = add if total is None else total + add
-    out_ref[...] = total[:1, :]
-
-
-def norm_kernel(*refs, features, count, steps, parts, zp, ne, heads):
+def carried_kernel(rates_ref, query_ref, local_ref, inner_ref, terms_ref, carry_ref, *refs, d, blocks, heads, first, last):
+    earlier_ref = None if first else refs[0]
+    att_ref, acc_ref = refs[0 if first else 1 :][:2]
+    sums = []
+    for h in range(heads):
+        here = head_rows(h)
+        block_decay = jnp.exp(-rates_ref[d, h][:1, :] * BLK)
+        state = carry_ref[here, :]
+        for b in range(blocks):
+            rows = slice(b * BLK, (b + 1) * BLK)
+            carried = dot(query_ref[d, rows, here], state.astype(BF16), ((1,), (0,)))
+            att = local_ref[d, rows, here] + carried * inner_ref[d, h]
+            att_ref[rows, here] = att
+            square = att * att
+            if h > 0:
+                square = square + sums[b]
+                sums[b] = square
+            else:
+                sums.append(square)
+            if b < blocks - 1:
+                state = block_decay * state + terms_ref[b, here, :]
+    for b in range(blocks):
+        rows = slice(b * BLK, (b + 1) * BLK)
+        square = sums[b] if first else sums[b] + earlier_ref[rows, :]
+        if last:
+            ones = jnp.ones((8, HEAD_DIM), BF16)
+            total = None
+            for piece in split_bf16(square)[:2]:
+                add = dot(ones, piece, ((1,), (1,)))
+                total = add if total is None else total + add
+            acc_ref[:, rows] = total[:1, :]
+        else:
+            acc_ref[rows, :] = square
+
+
+def norm_kernel(*refs, features, count, steps, ring, zp, ne, mirror, heads):
     squares, gain_ref, refs = refs[:count], refs[count], refs[count + 1 :]
-    atts, (out_hbm, out_ref, column_ref, sems) = refs[: len(parts)], refs[len(parts) :]
-    me = member(zp, ne)
+    atts, (out_hbm, out_ref, column_ref, sems) = refs[: len(ring)], refs[len(ring) :]
+    me = owned(zp, ne, mirror)
     total = squares[0][...]
     for other in squares[1:]:
         total = total + other[...]
@@ -183,11 +189,10 @@
     for step in range(steps):
         rows = slice(step * height, (step + 1) * height)
         column = column_ref[rows, :]
-        for att, ds in zip(atts, parts):
-            for i, d in enumerate(ds):
-                for h in range(heads):
-                    cols = pl.ds(pl.multiple_of(((me ^ d) * heads + h) * HEAD_DIM, HEAD_DIM), HEAD_DIM)
-                    out_ref[rows, cols] = (att[i, rows, head_rows(h)] * column * gain_ref[:, cols]).astype(BF16)
+        for att, d in zip(atts, ring):
+            for h in range(heads):
+                cols = pl.ds(pl.multiple_of(((me ^ d) * heads + h) * HEAD_DIM, HEAD_DIM), HEAD_DIM)
+                out_ref[rows, cols] = (att[rows, head_rows(h)] * column * gain_ref[:, cols]).astype(BF16)
         copies.append(pltpu.make_async_copy(out_ref.at[rows, :], out_hbm.at[rows, :], sems.at[step]))
         copies[-1].start()
     for copy in copies:
@@ -206,11 +211,13 @@
     vmem = pl.BlockSpec(memory_space=pltpu.VMEM)
     hbm = pl.BlockSpec(memory_space=pltpu.HBM)
     anywhere = pl.BlockSpec(memory_space=pl.ANY)
-    ring = (0, 3, 2, 1) if group == 4 else tuple(range(group))
+    ring = (0, 1, 2, 3) if group == 4 else tuple(range(group))
+    ring3 = (0, 2, 1, 3) if group == 4 else tuple(range(group))
     state_type = jax.ShapeDtypeStruct((part, HEAD_DIM), F32)
     term_type = jax.ShapeDtypeStruct((max(blocks - 1, 1), part, HEAD_DIM), F32)
     held_type = jax.ShapeDtypeStruct((group, rows, part), BF16)
     where = dict(zp=zp, ne=ne)
+    mirror = groups == 2 and zp == 2
 
     def call(kernel, count, outs, name, **more):
         more = {"in_specs": [vmem] * count, "out_specs": [vmem] * len(outs), "out_shape": outs, "name": name, **more}
@@ -219,7 +226,7 @@
     pinned = [pltpu.with_memory_space_constraint(a, pltpu.HBM) for a in (decay_rate, queries, key_vectors, value_vectors)]
     order = ring[1:] + ring[:1]
     rates, query, key, value = call(
-        functools.partial(load_kernel, heads=heads, order=order, **where),
+        functools.partial(load_kernel, heads=heads, order=order, mirror=mirror, **where),
         4,
         [jax.ShapeDtypeStruct((group, heads, 8, HEAD_DIM), F32), held_type, held_type, held_type],
         "load",
@@ -259,7 +266,7 @@
     )(rates, inner, *slots)
 
     if groups == 2:
-        before = lax.ppermute(total, "ctx", [(zz, (zz + zp) % nc) for zz in range(nc)])
+        before = lax.ppermute(total, "ctx", [(zz, nc - 1 - zz if mirror else (zz + zp) % nc) for zz in range(nc)])
     else:
         before = lax.ppermute(total, "ctx", [(zz, zz + zp) for zz in range(nc - zp)])
     step = 1
@@ -270,35 +277,32 @@
         step *= 2
 
     carries = call(
-        functools.partial(carry_kernel, ring=ring, heads=heads, span=span, **where), group + 2, [state_type] * group, "carry"
+        functools.partial(carry_kernel, ring=ring, ring_out=ring3, heads=heads, span=span, **where), group + 2, [state_type] * group, "carry"
     )(rates, before, *slots)
-    carries = [carries[0]] + [swap(carry, d) for carry, d in zip(carries[1:], ring[1:])]
-
-    parts = [(d,) for d in ring]
-    attended, squares, at = [], [], 0
-    for ds in parts:
-        att, acc = call(
-            functools.partial(carried_kernel, ds=ds, blocks=blocks, heads=heads),
-            4 + 2 * len(ds),
-            [jax.ShapeDtypeStruct((len(ds), rows, part), F32), jax.ShapeDtypeStruct((rows, HEAD_DIM), F32)],
+    carries = [carries[0]] + [swap(carry, d) for carry, d in zip(carries[1:], ring3[1:])]
+
+    attended, row_sum = [], None
+    for i, d in enumerate(ring3):
+        first, last = i == 0, i == group - 1
+        att, row_sum = call(
+            functools.partial(carried_kernel, d=d, blocks=blocks, heads=heads, first=first, last=last),
+            6 if first else 7,
+            [jax.ShapeDtypeStruct((rows, part), F32), jax.ShapeDtypeStruct((1, rows) if last else (rows, HEAD_DIM), F32)],
             "carried",
-        )(rates, query, local_part, inner, *(terms[d] for d in ds), *carries[at : at + len(ds)])
+        )(rates, query, local_part, inner, terms[d], carries[i], *([] if first else [row_sum]))
         attended.append(att)
-        squares.append(acc)
-        at += len(ds)
-    (row_sum,) = call(squares_kernel, len(parts), [jax.ShapeDtypeStruct((1, rows), F32)], "row_squares")(*squares)
 
     if nt & (nt - 1) == 0:
         swaps = [[(i, i ^ d) for i in range(nt)] for d in range(1, nt)]
     else:
         swaps = [[(i, (i + d) % nt) for i in range(nt)] for d in range(1, nt)]
-    row_sums = [row_sum] + [lax.ppermute(row_sum, "tp", pairs) for pairs in swaps[::-1]]
+    row_sums = [row_sum] + [lax.ppermute(row_sum, "tp", pairs) for pairs in swaps]
 
     steps = 4
-    norm = functools.partial(norm_kernel, features=float(width * nt), count=nt, steps=steps, parts=parts, heads=heads, **where)
+    norm = functools.partial(norm_kernel, features=float(width * nt), count=nt, steps=steps, ring=ring3, heads=heads, mirror=mirror, **where)
     (out,) = call(
         norm,
-        nt + 1 + len(parts),
+        nt + 1 + group,
         [jax.ShapeDtypeStruct((rows, width), BF16)],
         "norm",
         out_specs=[hbm],

time: 37.1 us -> 34.4 us (0.927)
  waiting for transfers between devices: 14.6 us -> 11.8 us
    ppermute x6, waiting for transfers between devices: 7.06 us -> 6.03 us  [swap(): return lax.ppermute(value, ('ctx', 'exp'), pairs)]
    ppermute x3, waiting for transfers between devices: 2.73 us -> 1.79 us  [local(): lax.ppermute(row_sum, 'tp', pairs)]
    ppermute x1, waiting for transfers between devices: 4.83 us -> 4.02 us  [local(): lax.ppermute(total, 'ctx', [(zz, nc - 1 - zz if mirror else (zz + zp) % n...]
    pallas_call x8 -> x7, Pallas kernels: 4.68 us -> 4.62 us  [the longest x1 2 us: local(): call(functools.partial(load_kernel, heads=heads, order=order, mirror=mirr...]
  transfers between devices with their start and end apart: 10 -> 10, of which waited for: 8 -> 7; matrix products, arithmetic and copies ran while one was open for 0% -> 0% of each run, Pallas kernels for 13% -> 14%
where the time goes in v4:
time: 34.4 us; the launch traced here: 34.2 us
  starting transfers between devices  13.1 us (38%)
  waiting for transfers between devices  11.8 us (34%)
  Pallas kernels  9.2 us (27%)
    ppermute x6, starting transfers between devices, swap(): return lax.ppermute(value, ('ctx', 'exp'), pairs)  8.27 us
    ppermute x6, waiting for transfers between devices, swap(): return lax.ppermute(value, ('ctx', 'exp'), pairs)  6.03 us
    ppermute x1, waiting for transfers between devices, local(): lax.ppermute(total, 'ctx', [(zz, nc - 1 - zz if mirror else (zz + zp) % n...  4.02 us
    pallas_call x1, Pallas kernels, local(): call(functools.partial(local_kernel, blocks=blocks, heads=heads, group=gr...  3.36 us
    ppermute x1, starting transfers between devices, local(): lax.ppermute(total, 'ctx', [(zz, nc - 1 - zz if mirror else (zz + zp) % n...  2.91 us
    pallas_call x1, Pallas kernels, local(): call(functools.partial(load_kernel, heads=heads, order=order, mirror=mirr...  2 us
    ppermute x3, starting transfers between devices, local(): lax.ppermute(row_sum, 'tp', pairs)  1.88 us
    ppermute x3, waiting for transfers between devices, local(): lax.ppermute(row_sum, 'tp', pairs)  1.79 us
  transfers between devices with their start and end apart: 10, of which 7 were waited for; matrix products, arithmetic and copies ran while one was open for 0% of the time, Pallas kernels for 14%

profile of v4, /device:TPU:0, one launch (start us, length us, event | category | flops | bytes accessed | tf_op | source)
XLA Modules:
  0.0 34.2 jit_solution(3133587810782833901)
XLA Ops:
  0.0 2.0 %load.1 = (f32[4,2,8,128]{3,2,1,0:T(8,128)S(1)}, bf16[4,512,256]{2,1,0:T(8,128)(2,1)S(1)}, bf16[4,512,256]{2,1,0:T(8,128)(2,1)S(1)}, bf16[4,512,256]{2,1,0:T(8,128)(2,1)S(1)}) custom-call(f32[8]{0:T(128)} %rate_hbm.1, bf16[512,1024]{1,0:T(8,128)(2,1)} %query_hbm.1, bf16[512,1024]{1,0:T(8,128)(2,1)} %key_hbm.1, bf16[512,1024]{1,0:T(8,128)(2,1)} %value_hbm.1), custom_call_target="tpu_custom_call" | custom-call | tf_op jit(solution)/shard_map/load/pallas_call | solution.py:228
  2.0 0.3 spread.7
  2.3 3.1 %collective-permute-start.1 = (f32[256,128]{1,0:T(8,128)S(1)}, f32[256,128]{1,0:T(8,128)S(1)}, u32[]{:S(2)}, u32[]{:S(2)}) collective-permute-start(f32[256,128]{1,0:T(8,128)S(1)} %get-tuple-element.40), channel_id=1, source_target_pairs={{0,8},{4,12},{8,0},{12,4},{16,24},{20,28},{24,16},{28,20},{1,9},{5... | collective-permute-start | bytes 393224 | tf_op jit(solution)/shard_map/ppermute | solution.py:248
  5.4 0.3 spread.6
  5.7 1.6 %collective-permute-start = (f32[256,128]{1,0:T(8,128)S(1)}, f32[256,128]{1,0:T(8,128)S(1)}, u32[]{:S(2)}, u32[]{:S(2)}) collective-permute-start(f32[256,128]{1,0:T(8,128)S(1)} %get-tuple-element.39), channel_id=1, source_target_pairs={{0,4},{4,0},{8,12},{12,8},{16,20},{20,16},{24,28},{28,24},{1,5},{5... | collective-permute-start | bytes 393224 | tf_op jit(solution)/shard_map/ppermute | solution.py:248
  7.3 0.3 spread.4
  7.5 0.1 collective-permute-start.2
  7.6 0.3 spread.5
  7.9 3.4 %local_part.1 = (f32[4,512,256]{2,1,0:T(8,128)S(1)}, f32[4,2,256,128]{3,2,1,0:T(8,128)S(1)}) custom-call(f32[4,2,8,128]{3,2,1,0:T(8,128)S(1)} %get-tuple-element.31.rates_ref, bf16[4,512,256]{2,1,0:T(8,128)(2,1)S(1)} %get-tuple-element.32.query_ref, bf16[4,512,256]{2,1,0:T(8,128)(2,1)S(1)} %get-tuple-element.33.key_ref, ...), custom_call_target="tpu_custom_call" | custom-call | flops 536870912 | bytes 5242880 | tf_op jit(solution)/shard_map/local_part/pallas_call | solution.py:252
  11.3 0.0 collective-permute-done.1.refs_2_
  11.3 2.2 %collective-permute-done.refs_1_ = f32[256,128]{1,0:T(8,128)S(1)} collective-permute-done((f32[256,128]{1,0:T(8,128)S(1)}, f32[256,128]{1,0:T(8,128)S(1)}, u32[]{:S(2)}, u32[]{:S(2)}) %collective-permute-start) | collective-permute-done | bytes 131104 | tf_op jit(solution)/shard_map/ppermute | solution.py:248
  13.5 0.0 collective-permute-done.2.refs_3_
  13.5 0.1 group_total.1
  13.6 2.9 %collective-permute-start.3 = (f32[256,128]{1,0:T(8,128)S(1)}, f32[256,128]{1,0:T(8,128)S(1)}, u32[]{:S(2)}, u32[]{:S(2)}) collective-permute-start(f32[256,128]{1,0:T(8,128)S(1)} %group_total.1), channel_id=1, source_target_pairs={{0,24},{8,16},{16,8},{24,0},{1,25},{9,17},{17,9},{25,1},{2,26},{10... | collective-permute-start | bytes 393224 | tf_op jit(solution)/shard_map/ppermute | solution.py:269
  16.5 4.0 %collective-permute-done.3.before_ref = f32[256,128]{1,0:T(8,128)S(1)} collective-permute-done((f32[256,128]{1,0:T(8,128)S(1)}, f32[256,128]{1,0:T(8,128)S(1)}, u32[]{:S(2)}, u32[]{:S(2)}) %collective-permute-start.3) | collective-permute-done | bytes 131104 | tf_op jit(solution)/shard_map/ppermute | solution.py:269
  20.5 0.2 carry.1
  20.7 1.3 %collective-permute-start.6 = (f32[256,128]{1,0:T(8,128)S(1)}, f32[256,128]{1,0:T(8,128)S(1)}, u32[]{:S(2)}, u32[]{:S(2)}) collective-permute-start(f32[256,128]{1,0:T(8,128)S(1)} %get-tuple-element.46), channel_id=1, source_target_pairs={{0,8},{4,12},{8,0},{12,4},{16,24},{20,28},{24,16},{28,20},{1,9},{5... | collective-permute-start | bytes 393224 | tf_op jit(solution)/shard_map/ppermute | solution.py:248
  22.0 0.9 %collective-permute-start.5 = (f32[256,128]{1,0:T(8,128)S(1)}, f32[256,128]{1,0:T(8,128)S(1)}, u32[]{:S(2)}, u32[]{:S(2)}) collective-permute-start(f32[256,128]{1,0:T(8,128)S(1)} %get-tuple-element.44), channel_id=1, source_target_pairs={{0,4},{4,0},{8,12},{12,8},{16,20},{20,16},{24,28},{28,24},{1,5},{5... | collective-permute-start | bytes 393224 | tf_op jit(solution)/shard_map/ppermute | solution.py:248
  22.9 1.4 %collective-permute-start.4 = (f32[256,128]{1,0:T(8,128)S(1)}, f32[256,128]{1,0:T(8,128)S(1)}, u32[]{:S(2)}, u32[]{:S(2)}) collective-permute-start(f32[256,128]{1,0:T(8,128)S(1)} %get-tuple-element.42), channel_id=1, source_target_pairs={{0,12},{4,8},{8,4},{12,0},{16,28},{20,24},{24,20},{28,16},{1,13},{... | collective-permute-start | bytes 393224 | tf_op jit(solution)/shard_map/ppermute | solution.py:248
  24.3 0.2 carried.4
  24.5 1.5 %collective-permute-done.6.carry_ref = f32[256,128]{1,0:T(8,128)S(1)} collective-permute-done((f32[256,128]{1,0:T(8,128)S(1)}, f32[256,128]{1,0:T(8,128)S(1)}, u32[]{:S(2)}, u32[]{:S(2)}) %collective-permute-start.6) | collective-permute-done | bytes 131104 | tf_op jit(solution)/shard_map/ppermute | solution.py:248
  26.0 0.2 carried.5
  26.3 0.7 %collective-permute-done.5.carry_ref = f32[256,128]{1,0:T(8,128)S(1)} collective-permute-done((f32[256,128]{1,0:T(8,128)S(1)}, f32[256,128]{1,0:T(8,128)S(1)}, u32[]{:S(2)}, u32[]{:S(2)}) %collective-permute-start.5) | collective-permute-done | bytes 131104 | tf_op jit(solution)/shard_map/ppermute | solution.py:248
  27.0 0.2 carried.6
  27.2 1.5 %collective-permute-done.4.carry_ref = f32[256,128]{1,0:T(8,128)S(1)} collective-permute-done((f32[256,128]{1,0:T(8,128)S(1)}, f32[256,128]{1,0:T(8,128)S(1)}, u32[]{:S(2)}, u32[]{:S(2)}) %collective-permute-start.4) | collective-permute-done | bytes 131104 | tf_op jit(solution)/shard_map/ppermute | solution.py:248
  28.8 0.0 copy-start
  28.8 0.4 %carried.7 = (f32[512,256]{1,0:T(8,128)S(1)}, f32[1,512]{1,0:T(1,128)S(1)}) custom-call(f32[4,2,8,128]{3,2,1,0:T(8,128)S(1)} %get-tuple-element.31.rates_ref, bf16[4,512,256]{2,1,0:T(8,128)(2,1)S(1)} %get-tuple-element.32.query_ref, f32[4,512,256]{2,1,0:T(8,128)S(1)} %get-tuple-element.35.local_ref, ...), custom_call_target="tpu_custom_call" | custom-call | tf_op jit(solution)/shard_map/carried/pallas_call | solution.py:287
  29.2 0.0 collective-permute-start.9
  29.2 1.6 %collective-permute-start.8 = (f32[1,512]{1,0:T(1,128)S(1)}, f32[1,512]{1,0:T(1,128)S(1)}, u32[]{:S(2)}, u32[]{:S(2)}) collective-permute-start(f32[1,512]{1,0:T(1,128)S(1)} %get-tuple-element.52.refs_0_), channel_id=1, source_target_pairs={{0,2},{1,3},{2,0},{3,1},{4,6},{5,7},{6,4},{7,5},{8,10},{9,11},{10,... | collective-permute-start | bytes 6152 | tf_op jit(solution)/shard_map/ppermute | solution.py:299
  30.8 0.3 collective-permute-start.7
  31.1 1.1 %collective-permute-done.9.refs_3_ = f32[1,512]{1,0:T(1,128)S(1)} collective-permute-done((f32[1,512]{1,0:T(1,128)S(1)}, f32[1,512]{1,0:T(1,128)S(1)}, u32[]{:S(2)}, u32[]{:S(2)}) %collective-permute-start.9) | collective-permute-done | bytes 2080 | tf_op jit(solution)/shard_map/ppermute | solution.py:299
  32.2 0.6 %collective-permute-done.8.refs_2_ = f32[1,512]{1,0:T(1,128)S(1)} collective-permute-done((f32[1,512]{1,0:T(1,128)S(1)}, f32[1,512]{1,0:T(1,128)S(1)}, u32[]{:S(2)}, u32[]{:S(2)}) %collective-permute-start.8) | collective-permute-done | bytes 2080 | tf_op jit(solution)/shard_map/ppermute | solution.py:299
  32.9 0.0 collective-permute-done.7.refs_1_
  32.9 0.0 copy-done
  32.9 1.3 %norm.1 = bf16[512,1024]{1,0:T(8,128)(2,1)} custom-call(f32[1,512]{1,0:T(1,128)S(1)} %get-tuple-element.52.refs_0_, f32[1,512]{1,0:T(1,128)S(1)} %collective-permute-done.7.refs_1_, f32[1,512]{1,0:T(1,128)S(1)} %collective-permute-done.8.refs_2_, f32[1,512]{1,0:T(1,128)S(1)} %collective-permute-done.9.refs_3_, f32[1,1024]{1,0:T(1,128)S(1)} %bitcast.1, ...), custom_call_target="tpu_custom_call" | custom-call | tf_op jit(solution)/shard_map/norm/pallas_call | solution.py:303
Async XLA Ops:
  2.3 9.0 %collective-permute-start.1 = (f32[256,128]{1,0:T(8,128)S(1)}, f32[256,128]{1,0:T(8,128)S(1)}, u32[]{:S(2)}, u32[]{:S(2)}) collective-permute-start(f32[256,128]{1,0:T(8,128)S(1)} %get-tuple-element.40), channel_id=1, source_target_pairs={{0,8},{4,12},{8,0},{12,4},{16,24},{20,28},{24,16},{28,20},{1,9},{5... | collective-permute-start | bytes 393224 | tf_op jit(solution)/shard_map/ppermute | solution.py:248
  5.7 7.8 %collective-permute-start = (f32[256,128]{1,0:T(8,128)S(1)}, f32[256,128]{1,0:T(8,128)S(1)}, u32[]{:S(2)}, u32[]{:S(2)}) collective-permute-start(f32[256,128]{1,0:T(8,128)S(1)} %get-tuple-element.39), channel_id=1, source_target_pairs={{0,4},{4,0},{8,12},{12,8},{16,20},{20,16},{24,28},{28,24},{1,5},{5... | collective-permute-start | bytes 393224 | tf_op jit(solution)/shard_map/ppermute | solution.py:248
  7.5 6.0 %collective-permute-start.2 = (f32[256,128]{1,0:T(8,128)S(1)}, f32[256,128]{1,0:T(8,128)S(1)}, u32[]{:S(2)}, u32[]{:S(2)}) collective-permute-start(f32[256,128]{1,0:T(8,128)S(1)} %get-tuple-element.41), channel_id=1, source_target_pairs={{0,12},{4,8},{8,4},{12,0},{16,28},{20,24},{24,20},{28,16},{1,13},{... | collective-permute-start | bytes 393224 | tf_op jit(solution)/shard_map/ppermute | solution.py:248
  13.6 6.9 %collective-permute-start.3 = (f32[256,128]{1,0:T(8,128)S(1)}, f32[256,128]{1,0:T(8,128)S(1)}, u32[]{:S(2)}, u32[]{:S(2)}) collective-permute-start(f32[256,128]{1,0:T(8,128)S(1)} %group_total.1), channel_id=1, source_target_pairs={{0,24},{8,16},{16,8},{24,0},{1,25},{9,17},{17,9},{25,1},{2,26},{10... | collective-permute-start | bytes 393224 | tf_op jit(solution)/shard_map/ppermute | solution.py:269
  20.7 5.3 %collective-permute-start.6 = (f32[256,128]{1,0:T(8,128)S(1)}, f32[256,128]{1,0:T(8,128)S(1)}, u32[]{:S(2)}, u32[]{:S(2)}) collective-permute-start(f32[256,128]{1,0:T(8,128)S(1)} %get-tuple-element.46), channel_id=1, source_target_pairs={{0,8},{4,12},{8,0},{12,4},{16,24},{20,28},{24,16},{28,20},{1,9},{5... | collective-permute-start | bytes 393224 | tf_op jit(solution)/shard_map/ppermute | solution.py:248
  22.0 5.0 %collective-permute-start.5 = (f32[256,128]{1,0:T(8,128)S(1)}, f32[256,128]{1,0:T(8,128)S(1)}, u32[]{:S(2)}, u32[]{:S(2)}) collective-permute-start(f32[256,128]{1,0:T(8,128)S(1)} %get-tuple-element.44), channel_id=1, source_target_pairs={{0,4},{4,0},{8,12},{12,8},{16,20},{20,16},{24,28},{28,24},{1,5},{5... | collective-permute-start | bytes 393224 | tf_op jit(solution)/shard_map/ppermute | solution.py:248
  22.9 5.9 %collective-permute-start.4 = (f32[256,128]{1,0:T(8,128)S(1)}, f32[256,128]{1,0:T(8,128)S(1)}, u32[]{:S(2)}, u32[]{:S(2)}) collective-permute-start(f32[256,128]{1,0:T(8,128)S(1)} %get-tuple-element.42), channel_id=1, source_target_pairs={{0,12},{4,8},{8,4},{12,0},{16,28},{20,24},{24,20},{28,16},{1,13},{... | collective-permute-start | bytes 393224 | tf_op jit(solution)/shard_map/ppermute | solution.py:248
  28.8 4.1 %copy-start = (f32[1024]{0:T(1024)S(1)}, f32[1024]{0:T(1024)}, u32[]{:S(2)}) copy-start(f32[1024]{0:T(1024)} %param.9) | copy-start | bytes 12292
  29.2 3.0 %collective-permute-start.9 = (f32[1,512]{1,0:T(1,128)S(1)}, f32[1,512]{1,0:T(1,128)S(1)}, u32[]{:S(2)}, u32[]{:S(2)}) collective-permute-start(f32[1,512]{1,0:T(1,128)S(1)} %get-tuple-element.52.refs_0_), channel_id=1, source_target_pairs={{0,3},{1,2},{2,1},{3,0},{4,7},{5,6},{6,5},{7,4},{8,11},{9,10},{10,... | collective-permute-start | bytes 6152 | tf_op jit(solution)/shard_map/ppermute | solution.py:299
  29.2 3.7 %collective-permute-start.8 = (f32[1,512]{1,0:T(1,128)S(1)}, f32[1,512]{1,0:T(1,128)S(1)}, u32[]{:S(2)}, u32[]{:S(2)}) collective-permute-start(f32[1,512]{1,0:T(1,128)S(1)} %get-tuple-element.52.refs_0_), channel_id=1, source_target_pairs={{0,2},{1,3},{2,0},{3,1},{4,6},{5,7},{6,4},{7,5},{8,10},{9,11},{10,... | collective-permute-start | bytes 6152 | tf_op jit(solution)/shard_map/ppermute | solution.py:299
  30.8 2.1 %collective-permute-start.7 = (f32[1,512]{1,0:T(1,128)S(1)}, f32[1,512]{1,0:T(1,128)S(1)}, u32[]{:S(2)}, u32[]{:S(2)}) collective-permute-start(f32[1,512]{1,0:T(1,128)S(1)} %get-tuple-element.52.refs_0_), channel_id=1, source_target_pairs={{0,1},{1,0},{2,3},{3,2},{4,5},{5,4},{6,7},{7,6},{8,9},{9,8},{10,11... | collective-permute-start | bytes 6152 | tf_op jit(solution)/shard_map/ppermute | solution.py:299

commit v5 on v4

--- a/solution.py
+++ b/solution.py
@@ -24,13 +24,6 @@
     return slice(h * HEAD_DIM, (h + 1) * HEAD_DIM)
 
 
-def split_bf16(value):
-    high = value.astype(BF16)
-    rest = value - high.astype(F32)
-    middle = rest.astype(BF16)
-    return high, middle, (rest - middle.astype(F32)).astype(BF16)
-
-
 def member(zp, ne):
     return (lax.axis_index("ctx") % zp) * ne + lax.axis_index("exp")
 
@@ -40,31 +33,11 @@
     return me ^ (lax.axis_index("ctx") // zp % 2 * ne) if mirror else me
 
 
-def load_kernel(rate_hbm, query_hbm, key_hbm, value_hbm, rates_ref, query_ref, key_ref, value_ref, rate_smem, sems, *, zp, ne, mirror, heads, order):
-    me = owned(zp, ne, mirror)
-    part = heads * HEAD_DIM
-    copies = []
-    for n, (source, held) in enumerate(((key_hbm, key_ref), (value_hbm, value_ref), (query_hbm, query_ref))):
-        for d in order:
-            cols = pl.ds(pl.multiple_of((me ^ d) * part, part), part)
-            copies.append(pltpu.make_async_copy(source.at[:, cols], held.at[d], sems.at[n, d]))
-    rate_copy = pltpu.make_async_copy(rate_hbm, rate_smem, sems.at[3, 0])
-    rate_copy.start()
-    for copy in copies:
-        copy.start()
-    rate_copy.wait()
-    for d in order:
-        for h in range(heads):
-            rates_ref[d, h] = jnp.full((8, HEAD_DIM), rate_smem[(me ^ d) * heads + h], F32)
-    for copy in copies:
-        copy.wait()
-
-
-def spread_kernel(rates_ref, key_ref, value_ref, state_ref, terms_ref, *, d, blocks, heads):
+def spread(d, rate_of, key_ref, value_ref, state_ref, terms_ref, blocks, heads):
     left = (BLK - lax.broadcasted_iota(jnp.int32, (BLK, HEAD_DIM), 0)).astype(F32)
     for h in range(heads):
         here = head_rows(h)
-        rate = rates_ref[d, h][:1, :]
+        rate = rate_of(h)
         tail = jnp.exp(-rate * left)
         block_decay = jnp.exp(-rate * BLK)
         own = None
@@ -76,6 +49,41 @@
                 terms_ref[b, here, :] = term
             own = term if own is None else block_decay * own + term
         state_ref[here, :] = own
+
+
+def load_kernel(rate_hbm, query_hbm, key_hbm, value_hbm, *refs, zp, ne, mirror, heads, blocks, order, early):
+    rates_ref, query_ref, key_ref, value_ref = refs[:4]
+    states, terms, (rate_smem, sems) = refs[4 : 4 + early], refs[4 + early : 4 + 2 * early], refs[4 + 2 * early :]
+    me = owned(zp, ne, mirror)
+    part = heads * HEAD_DIM
+
+    def copy_of(n, d):
+        source, held = ((key_hbm, key_ref), (value_hbm, value_ref), (query_hbm, query_ref))[n]
+        cols = pl.ds(pl.multiple_of((me ^ d) * part, part), part)
+        return pltpu.make_async_copy(source.at[:, cols], held.at[d], sems.at[n, d])
+
+    rate_copy = pltpu.make_async_copy(rate_hbm, rate_smem, sems.at[3, 0])
+    rate_copy.start()
+    for d in order:
+        copy_of(0, d).start()
+        copy_of(1, d).start()
+    for d in order:
+        copy_of(2, d).start()
+    rate_copy.wait()
+    for d in order:
+        for h in range(heads):
+            rates_ref[d, h] = jnp.full((8, HEAD_DIM), rate_smem[(me ^ d) * heads + h], F32)
+    for i, d in enumerate(order):
+        copy_of(0, d).wait()
+        copy_of(1, d).wait()
+        if i < early:
+            spread(d, lambda h: rates_ref[d, h][:1, :], key_ref, value_ref, states[i], terms[i], blocks, heads)
+    for d in order:
+        copy_of(2, d).wait()
+
+
+def spread_kernel(rates_ref, key_ref, value_ref, state_ref, terms_ref, *, d, blocks, heads):
+    spread(d, lambda h: rates_ref[d, h][:1, :], key_ref, value_ref, state_ref, terms_ref, blocks, heads)
 
 
 def local_kernel(rates_ref, query_ref, key_ref, value_ref, out_ref, inner_ref, *, blocks, heads, group):
@@ -161,34 +169,27 @@
         rows = slice(b * BLK, (b + 1) * BLK)
         square = sums[b] if first else sums[b] + earlier_ref[rows, :]
         if last:
-            ones = jnp.ones((8, HEAD_DIM), BF16)
-            total = None
-            for piece in split_bf16(square)[:2]:
-                add = dot(ones, piece, ((1,), (1,)))
-                total = add if total is None else total + add
-            acc_ref[:, rows] = total[:1, :]
+            for at in range(0, BLK, HEAD_DIM):
+                turned = jnp.transpose(square[at : at + HEAD_DIM, :])
+                acc_ref[:, b * BLK + at : b * BLK + at + HEAD_DIM] = jnp.sum(turned, axis=0, keepdims=True)
         else:
             acc_ref[rows, :] = square
 
 
 def norm_kernel(*refs, features, count, steps, ring, zp, ne, mirror, heads):
     squares, gain_ref, refs = refs[:count], refs[count], refs[count + 1 :]
-    atts, (out_hbm, out_ref, column_ref, sems) = refs[: len(ring)], refs[len(ring) :]
+    atts, (out_hbm, out_ref, sems) = refs[: len(ring)], refs[len(ring) :]
     me = owned(zp, ne, mirror)
     total = squares[0][...]
     for other in squares[1:]:
         total = total + other[...]
     inverse = lax.rsqrt(total / features + 1e-06)
-    row = lax.broadcasted_iota(jnp.int32, (16, inverse.shape[1]), 0)
-    pieces = jnp.zeros(row.shape, F32)
-    for i, piece in enumerate(split_bf16(inverse)):
-        pieces = jnp.where(row == i, piece.astype(F32), pieces)
-    column_ref[...] = dot(pieces.astype(BF16), jnp.ones((16, HEAD_DIM), BF16), ((0,), (0,)))
     height = out_ref.shape[0] // steps
     copies = []
     for step in range(steps):
         rows = slice(step * height, (step + 1) * height)
-        column = column_ref[rows, :]
+        tiles = [inverse[:, at : at + HEAD_DIM] for at in range(step * height, (step + 1) * height, HEAD_DIM)]
+        column = jnp.concatenate([jnp.transpose(jnp.broadcast_to(tile, (HEAD_DIM, HEAD_DIM))) for tile in tiles], axis=0)
         for att, d in zip(atts, ring):
             for h in range(heads):
                 cols = pl.ds(pl.multiple_of(((me ^ d) * heads + h) * HEAD_DIM, HEAD_DIM), HEAD_DIM)
@@ -211,8 +212,8 @@
     vmem = pl.BlockSpec(memory_space=pltpu.VMEM)
     hbm = pl.BlockSpec(memory_space=pltpu.HBM)
     anywhere = pl.BlockSpec(memory_space=pl.ANY)
-    ring = (0, 1, 2, 3) if group == 4 else tuple(range(group))
-    ring3 = (0, 2, 1, 3) if group == 4 else tuple(range(group))
+    ring = (0, 2, 1, 3) if group == 4 else tuple(range(group))
+    ring3 = (0, 3, 2, 1) if group == 4 else tuple(range(group))
     state_type = jax.ShapeDtypeStruct((part, HEAD_DIM), F32)
     term_type = jax.ShapeDtypeStruct((max(blocks - 1, 1), part, HEAD_DIM), F32)
     held_type = jax.ShapeDtypeStruct((group, rows, part), BF16)
@@ -224,20 +225,23 @@
         return pl.pallas_call(kernel, compiler_params=params(), **more)
 
     pinned = [pltpu.with_memory_space_constraint(a, pltpu.HBM) for a in (decay_rate, queries, key_vectors, value_vectors)]
-    order = ring[1:] + ring[:1]
-    rates, query, key, value = call(
-        functools.partial(load_kernel, heads=heads, order=order, mirror=mirror, **where),
+    order = (3, 2, 1, 0) if group == 4 else ring[1:] + ring[:1]
+    early = min(3, group)
+    rates, query, key, value, *rest = call(
+        functools.partial(load_kernel, heads=heads, blocks=blocks, order=order, mirror=mirror, early=early, **where),
         4,
-        [jax.ShapeDtypeStruct((group, heads, 8, HEAD_DIM), F32), held_type, held_type, held_type],
+        [jax.ShapeDtypeStruct((group, heads, 8, HEAD_DIM), F32), held_type, held_type, held_type]
+        + [state_type] * early
+        + [term_type] * early,
         "load",
         in_specs=[hbm] * 4,
         scratch_shapes=[pltpu.SMEM((heads_all,), F32), pltpu.SemaphoreType.DMA((4, group))],
     )(*pinned)
 
-    slots, terms = {}, {}
-    for d in order:
-        spread = functools.partial(spread_kernel, d=d, blocks=blocks, heads=heads)
-        slots[d], terms[d] = call(spread, 3, [state_type, term_type], "spread")(rates, key, value)
+    slots, terms = dict(zip(order, rest[:early])), dict(zip(order, rest[early:]))
+    for d in order[early:]:
+        kernel = functools.partial(spread_kernel, d=d, blocks=blocks, heads=heads)
+        slots[d], terms[d] = call(kernel, 3, [state_type, term_type], "spread")(rates, key, value)
 
     def swap(value, d):
         pairs = []
@@ -308,7 +312,6 @@
         out_specs=[hbm],
         scratch_shapes=[
             pltpu.VMEM((rows, width), BF16),
-            pltpu.VMEM((rows, HEAD_DIM), F32),
             pltpu.SemaphoreType.DMA((steps,)),
         ],
     )(*row_sums, norm_gain[None, :], *attended)

time: 34.4 us -> 33.5 us (0.974)
  Pallas kernels: 9.2 us -> 8.17 us
    pallas_call x5 -> x2, Pallas kernels: 3.16 us -> 2.34 us  [the longest x1 2.05 us: local(): call(functools.partial(load_kernel, heads=heads, blocks=blocks, order=ord...]
    ppermute x1, starting transfers between devices: 2.91 us -> 3.27 us  [local(): lax.ppermute(total, 'ctx', [(zz, nc - 1 - zz if mirror else (zz + zp) % n...]
    ppermute x1, waiting for transfers between devices: 4.02 us -> 3.67 us  [local(): lax.ppermute(total, 'ctx', [(zz, nc - 1 - zz if mirror else (zz + zp) % n...]
  transfers between devices with their start and end apart: 10 -> 10, of which waited for: 7 -> 7; matrix products, arithmetic and copies ran while one was open for 0% -> 0% of each run, Pallas kernels for 14% -> 13%
where the time goes in v5:
time: 33.5 us; the launch traced here: 33.4 us
  starting transfers between devices  13.4 us (40%)
  waiting for transfers between devices  11.7 us (35%)
  Pallas kernels  8.17 us (24%)
    ppermute x6, starting transfers between devices, swap(): return lax.ppermute(value, ('ctx', 'exp'), pairs)  8.18 us
    ppermute x6, waiting for transfers between devices, swap(): return lax.ppermute(value, ('ctx', 'exp'), pairs)  6.27 us
    ppermute x1, waiting for transfers between devices, local(): lax.ppermute(total, 'ctx', [(zz, nc - 1 - zz if mirror else (zz + zp) % n...  3.67 us
    pallas_call x1, Pallas kernels, local(): call(functools.partial(local_kernel, blocks=blocks, heads=heads, group=gr...  3.36 us
    ppermute x1, starting transfers between devices, local(): lax.ppermute(total, 'ctx', [(zz, nc - 1 - zz if mirror else (zz + zp) % n...  3.27 us
    pallas_call x1, Pallas kernels, local(): call(functools.partial(load_kernel, heads=heads, blocks=blocks, order=ord...  2.05 us
    ppermute x3, starting transfers between devices, local(): lax.ppermute(row_sum, 'tp', pairs)  1.92 us
    ppermute x3, waiting for transfers between devices, local(): lax.ppermute(row_sum, 'tp', pairs)  1.8 us
  transfers between devices with their start and end apart: 10, of which 7 were waited for; matrix products, arithmetic and copies ran while one was open for 0% of the time, Pallas kernels for 13%

profile of v5, /device:TPU:0, one launch (start us, length us, event | category | flops | bytes accessed | tf_op | source)
XLA Modules:
  0.0 33.4 jit_solution(15325367646391892835)
XLA Ops:
  0.0 2.1 %load.1 = (f32[4,2,8,128]{3,2,1,0:T(8,128)S(1)}, bf16[4,512,256]{2,1,0:T(8,128)(2,1)S(1)}, bf16[4,512,256]{2,1,0:T(8,128)(2,1)S(1)}, bf16[4,512,256]{2,1,0:T(8,1...) custom-call(f32[8]{0:T(128)} %rate_hbm.1, ...), custom_call_target="tpu_custom_call" | custom-call | tf_op jit(solution)/shard_map/load/pallas_call | solution.py:230
  2.1 3.1 %collective-permute-start = (f32[256,128]{1,0:T(8,128)S(1)}, f32[256,128]{1,0:T(8,128)S(1)}, u32[]{:S(2)}, u32[]{:S(2)}) collective-permute-start(f32[256,128]{1,0:T(8,128)S(1)} %get-tuple-element.39), channel_id=1, source_target_pairs={{0,8},{4,12},{8,0},{12,4},{16,24},{20,28},{24,16},{28,20},{1,9},{5... | collective-permute-start | bytes 393224 | tf_op jit(solution)/shard_map/ppermute | solution.py:252
  5.2 1.5 %collective-permute-start.1 = (f32[256,128]{1,0:T(8,128)S(1)}, f32[256,128]{1,0:T(8,128)S(1)}, u32[]{:S(2)}, u32[]{:S(2)}) collective-permute-start(f32[256,128]{1,0:T(8,128)S(1)} %get-tuple-element.40), channel_id=1, source_target_pairs={{0,4},{4,0},{8,12},{12,8},{16,20},{20,16},{24,28},{28,24},{1,5},{5... | collective-permute-start | bytes 393224 | tf_op jit(solution)/shard_map/ppermute | solution.py:252
  6.6 0.1 collective-permute-start.2
  6.7 0.3 spread.1
  7.0 3.4 %local_part.1 = (f32[4,512,256]{2,1,0:T(8,128)S(1)}, f32[4,2,256,128]{3,2,1,0:T(8,128)S(1)}) custom-call(f32[4,2,8,128]{3,2,1,0:T(8,128)S(1)} %get-tuple-element.31.rates_ref, bf16[4,512,256]{2,1,0:T(8,128)(2,1)S(1)} %get-tuple-element.32.query_ref, bf16[4,512,256]{2,1,0:T(8,128)(2,1)S(1)} %get-tuple-element.33.key_ref, ...), custom_call_target="tpu_custom_call" | custom-call | flops 536870912 | bytes 5242880 | tf_op jit(solution)/shard_map/local_part/pallas_call | solution.py:256
  10.4 0.0 collective-permute-done.refs_1_
  10.4 2.6 %collective-permute-done.1.refs_2_ = f32[256,128]{1,0:T(8,128)S(1)} collective-permute-done((f32[256,128]{1,0:T(8,128)S(1)}, f32[256,128]{1,0:T(8,128)S(1)}, u32[]{:S(2)}, u32[]{:S(2)}) %collective-permute-start.1) | collective-permute-done | bytes 131104 | tf_op jit(solution)/shard_map/ppermute | solution.py:252
  12.9 0.0 collective-permute-done.2.refs_3_
  12.9 0.1 group_total.1
  13.0 3.3 %collective-permute-start.3 = (f32[256,128]{1,0:T(8,128)S(1)}, f32[256,128]{1,0:T(8,128)S(1)}, u32[]{:S(2)}, u32[]{:S(2)}) collective-permute-start(f32[256,128]{1,0:T(8,128)S(1)} %group_total.1), channel_id=1, source_target_pairs={{0,24},{8,16},{16,8},{24,0},{1,25},{9,17},{17,9},{25,1},{2,26},{10... | collective-permute-start | bytes 393224 | tf_op jit(solution)/shard_map/ppermute | solution.py:273
  16.3 3.7 %collective-permute-done.3.before_ref = f32[256,128]{1,0:T(8,128)S(1)} collective-permute-done((f32[256,128]{1,0:T(8,128)S(1)}, f32[256,128]{1,0:T(8,128)S(1)}, u32[]{:S(2)}, u32[]{:S(2)}) %collective-permute-start.3) | collective-permute-done | bytes 131104 | tf_op jit(solution)/shard_map/ppermute | solution.py:273
  19.9 0.2 carry.1
  20.1 1.6 %collective-permute-start.6 = (f32[256,128]{1,0:T(8,128)S(1)}, f32[256,128]{1,0:T(8,128)S(1)}, u32[]{:S(2)}, u32[]{:S(2)}) collective-permute-start(f32[256,128]{1,0:T(8,128)S(1)} %get-tuple-element.46), channel_id=1, source_target_pairs={{0,12},{4,8},{8,4},{12,0},{16,28},{20,24},{24,20},{28,16},{1,13},{... | collective-permute-start | bytes 393224 | tf_op jit(solution)/shard_map/ppermute | solution.py:252
  21.7 1.4 %collective-permute-start.5 = (f32[256,128]{1,0:T(8,128)S(1)}, f32[256,128]{1,0:T(8,128)S(1)}, u32[]{:S(2)}, u32[]{:S(2)}) collective-permute-start(f32[256,128]{1,0:T(8,128)S(1)} %get-tuple-element.44), channel_id=1, source_target_pairs={{0,8},{4,12},{8,0},{12,4},{16,24},{20,28},{24,16},{28,20},{1,9},{5... | collective-permute-start | bytes 393224 | tf_op jit(solution)/shard_map/ppermute | solution.py:252
  23.1 0.5 %collective-permute-start.4 = (f32[256,128]{1,0:T(8,128)S(1)}, f32[256,128]{1,0:T(8,128)S(1)}, u32[]{:S(2)}, u32[]{:S(2)}) collective-permute-start(f32[256,128]{1,0:T(8,128)S(1)} %get-tuple-element.42), channel_id=1, source_target_pairs={{0,4},{4,0},{8,12},{12,8},{16,20},{20,16},{24,28},{28,24},{1,5},{5... | collective-permute-start | bytes 393224 | tf_op jit(solution)/shard_map/ppermute | solution.py:252
  23.7 0.2 carried.4
  23.9 2.1 %collective-permute-done.6.carry_ref = f32[256,128]{1,0:T(8,128)S(1)} collective-permute-done((f32[256,128]{1,0:T(8,128)S(1)}, f32[256,128]{1,0:T(8,128)S(1)}, u32[]{:S(2)}, u32[]{:S(2)}) %collective-permute-start.6) | collective-permute-done | bytes 131104 | tf_op jit(solution)/shard_map/ppermute | solution.py:252
  26.1 0.2 carried.5
  26.3 1.2 %collective-permute-done.5.carry_ref = f32[256,128]{1,0:T(8,128)S(1)} collective-permute-done((f32[256,128]{1,0:T(8,128)S(1)}, f32[256,128]{1,0:T(8,128)S(1)}, u32[]{:S(2)}, u32[]{:S(2)}) %collective-permute-start.5) | collective-permute-done | bytes 131104 | tf_op jit(solution)/shard_map/ppermute | solution.py:252
  27.5 0.2 carried.6
  27.7 0.4 %collective-permute-done.4.carry_ref = f32[256,128]{1,0:T(8,128)S(1)} collective-permute-done((f32[256,128]{1,0:T(8,128)S(1)}, f32[256,128]{1,0:T(8,128)S(1)}, u32[]{:S(2)}, u32[]{:S(2)}) %collective-permute-start.4) | collective-permute-done | bytes 131104 | tf_op jit(solution)/shard_map/ppermute | solution.py:252
  28.1 0.0 copy-start
  28.1 0.3 %carried.7 = (f32[512,256]{1,0:T(8,128)S(1)}, f32[1,512]{1,0:T(1,128)S(1)}) custom-call(f32[4,2,8,128]{3,2,1,0:T(8,128)S(1)} %get-tuple-element.31.rates_ref, bf16[4,512,256]{2,1,0:T(8,128)(2,1)S(1)} %get-tuple-element.32.query_ref, f32[4,512,256]{2,1,0:T(8,128)S(1)} %get-tuple-element.35.local_ref, ...), custom_call_target="tpu_custom_call" | custom-call | tf_op jit(solution)/shard_map/carried/pallas_call | solution.py:291
  28.4 0.1 collective-permute-start.9
  28.5 1.6 %collective-permute-start.8 = (f32[1,512]{1,0:T(1,128)S(1)}, f32[1,512]{1,0:T(1,128)S(1)}, u32[]{:S(2)}, u32[]{:S(2)}) collective-permute-start(f32[1,512]{1,0:T(1,128)S(1)} %get-tuple-element.52.refs_0_), channel_id=1, source_target_pairs={{0,2},{1,3},{2,0},{3,1},{4,6},{5,7},{6,4},{7,5},{8,10},{9,11},{10,... | collective-permute-start | bytes 6152 | tf_op jit(solution)/shard_map/ppermute | solution.py:303
  30.1 0.3 collective-permute-start.7
  30.4 1.1 %collective-permute-done.9.refs_3_ = f32[1,512]{1,0:T(1,128)S(1)} collective-permute-done((f32[1,512]{1,0:T(1,128)S(1)}, f32[1,512]{1,0:T(1,128)S(1)}, u32[]{:S(2)}, u32[]{:S(2)}) %collective-permute-start.9) | collective-permute-done | bytes 2080 | tf_op jit(solution)/shard_map/ppermute | solution.py:303
  31.5 0.7 %collective-permute-done.8.refs_2_ = f32[1,512]{1,0:T(1,128)S(1)} collective-permute-done((f32[1,512]{1,0:T(1,128)S(1)}, f32[1,512]{1,0:T(1,128)S(1)}, u32[]{:S(2)}, u32[]{:S(2)}) %collective-permute-start.8) | collective-permute-done | bytes 2080 | tf_op jit(solution)/shard_map/ppermute | solution.py:303
  32.2 0.0 collective-permute-done.7.refs_1_
  32.2 0.0 copy-done
  32.2 1.2 %norm.1 = bf16[512,1024]{1,0:T(8,128)(2,1)} custom-call(f32[1,512]{1,0:T(1,128)S(1)} %get-tuple-element.52.refs_0_, f32[1,512]{1,0:T(1,128)S(1)} %collective-permute-done.7.refs_1_, f32[1,512]{1,0:T(1,128)S(1)} %collective-permute-done.8.refs_2_, f32[1,512]{1,0:T(1,128)S(1)} %collective-permute-done.9.refs_3_, f32[1,1024]{1,0:T(1,128)S(1)} %bitcast.1, ...), custom_call_target="tpu_custom_call" | custom-call | tf_op jit(solution)/shard_map/norm/pallas_call | solution.py:307
Async XLA Ops:
  2.1 8.3 %collective-permute-start = (f32[256,128]{1,0:T(8,128)S(1)}, f32[256,128]{1,0:T(8,128)S(1)}, u32[]{:S(2)}, u32[]{:S(2)}) collective-permute-start(f32[256,128]{1,0:T(8,128)S(1)} %get-tuple-element.39), channel_id=1, source_target_pairs={{0,8},{4,12},{8,0},{12,4},{16,24},{20,28},{24,16},{28,20},{1,9},{5... | collective-permute-start | bytes 393224 | tf_op jit(solution)/shard_map/ppermute | solution.py:252
  5.2 7.8 %collective-permute-start.1 = (f32[256,128]{1,0:T(8,128)S(1)}, f32[256,128]{1,0:T(8,128)S(1)}, u32[]{:S(2)}, u32[]{:S(2)}) collective-permute-start(f32[256,128]{1,0:T(8,128)S(1)} %get-tuple-element.40), channel_id=1, source_target_pairs={{0,4},{4,0},{8,12},{12,8},{16,20},{20,16},{24,28},{28,24},{1,5},{5... | collective-permute-start | bytes 393224 | tf_op jit(solution)/shard_map/ppermute | solution.py:252
  6.6 6.3 %collective-permute-start.2 = (f32[256,128]{1,0:T(8,128)S(1)}, f32[256,128]{1,0:T(8,128)S(1)}, u32[]{:S(2)}, u32[]{:S(2)}) collective-permute-start(f32[256,128]{1,0:T(8,128)S(1)} %get-tuple-element.41), channel_id=1, source_target_pairs={{0,12},{4,8},{8,4},{12,0},{16,28},{20,24},{24,20},{28,16},{1,13},{... | collective-permute-start | bytes 393224 | tf_op jit(solution)/shard_map/ppermute | solution.py:252
  13.0 6.9 %collective-permute-start.3 = (f32[256,128]{1,0:T(8,128)S(1)}, f32[256,128]{1,0:T(8,128)S(1)}, u32[]{:S(2)}, u32[]{:S(2)}) collective-permute-start(f32[256,128]{1,0:T(8,128)S(1)} %group_total.1), channel_id=1, source_target_pairs={{0,24},{8,16},{16,8},{24,0},{1,25},{9,17},{17,9},{25,1},{2,26},{10... | collective-permute-start | bytes 393224 | tf_op jit(solution)/shard_map/ppermute | solution.py:273
  20.1 5.9 %collective-permute-start.6 = (f32[256,128]{1,0:T(8,128)S(1)}, f32[256,128]{1,0:T(8,128)S(1)}, u32[]{:S(2)}, u32[]{:S(2)}) collective-permute-start(f32[256,128]{1,0:T(8,128)S(1)} %get-tuple-element.46), channel_id=1, source_target_pairs={{0,12},{4,8},{8,4},{12,0},{16,28},{20,24},{24,20},{28,16},{1,13},{... | collective-permute-start | bytes 393224 | tf_op jit(solution)/shard_map/ppermute | solution.py:252
  21.7 5.7 %collective-permute-start.5 = (f32[256,128]{1,0:T(8,128)S(1)}, f32[256,128]{1,0:T(8,128)S(1)}, u32[]{:S(2)}, u32[]{:S(2)}) collective-permute-start(f32[256,128]{1,0:T(8,128)S(1)} %get-tuple-element.44), channel_id=1, source_target_pairs={{0,8},{4,12},{8,0},{12,4},{16,24},{20,28},{24,16},{28,20},{1,9},{5... | collective-permute-start | bytes 393224 | tf_op jit(solution)/shard_map/ppermute | solution.py:252
  23.1 5.0 %collective-permute-start.4 = (f32[256,128]{1,0:T(8,128)S(1)}, f32[256,128]{1,0:T(8,128)S(1)}, u32[]{:S(2)}, u32[]{:S(2)}) collective-permute-start(f32[256,128]{1,0:T(8,128)S(1)} %get-tuple-element.42), channel_id=1, source_target_pairs={{0,4},{4,0},{8,12},{12,8},{16,20},{20,16},{24,28},{28,24},{1,5},{5... | collective-permute-start | bytes 393224 | tf_op jit(solution)/shard_map/ppermute | solution.py:252
  28.1 4.1 %copy-start = (f32[1024]{0:T(1024)S(1)}, f32[1024]{0:T(1024)}, u32[]{:S(2)}) copy-start(f32[1024]{0:T(1024)} %param.9) | copy-start | bytes 12292
  28.4 3.1 %collective-permute-start.9 = (f32[1,512]{1,0:T(1,128)S(1)}, f32[1,512]{1,0:T(1,128)S(1)}, u32[]{:S(2)}, u32[]{:S(2)}) collective-permute-start(f32[1,512]{1,0:T(1,128)S(1)} %get-tuple-element.52.refs_0_), channel_id=1, source_target_pairs={{0,3},{1,2},{2,1},{3,0},{4,7},{5,6},{6,5},{7,4},{8,11},{9,10},{10,... | collective-permute-start | bytes 6152 | tf_op jit(solution)/shard_map/ppermute | solution.py:303
  28.5 3.7 %collective-permute-start.8 = (f32[1,512]{1,0:T(1,128)S(1)}, f32[1,512]{1,0:T(1,128)S(1)}, u32[]{:S(2)}, u32[]{:S(2)}) collective-permute-start(f32[1,512]{1,0:T(1,128)S(1)} %get-tuple-element.52.refs_0_), channel_id=1, source_target_pairs={{0,2},{1,3},{2,0},{3,1},{4,6},{5,7},{6,4},{7,5},{8,10},{9,11},{10,... | collective-permute-start | bytes 6152 | tf_op jit(solution)/shard_map/ppermute | solution.py:303
  30.1 2.1 %collective-permute-start.7 = (f32[1,512]{1,0:T(1,128)S(1)}, f32[1,512]{1,0:T(1,128)S(1)}, u32[]{:S(2)}, u32[]{:S(2)}) collective-permute-start(f32[1,512]{1,0:T(1,128)S(1)} %get-tuple-element.52.refs_0_), channel_id=1, source_target_pairs={{0,1},{1,0},{2,3},{3,2},{4,5},{5,4},{6,7},{7,6},{8,9},{9,8},{10,11... | collective-permute-start | bytes 6152 | tf_op jit(solution)/shard_map/ppermute | solution.py:303

commit v6 on v5

--- a/solution.py
+++ b/solution.py
@@ -26,6 +26,11 @@
 
 def member(zp, ne):
     return (lax.axis_index("ctx") % zp) * ne + lax.axis_index("exp")
+
+
+def away(way):
+    even, odd = way
+    return even if even == odd else jnp.where(lax.axis_index("tp") % 2 == 0, even, odd)
 
 
 def owned(zp, ne, mirror):
@@ -51,7 +56,7 @@
         state_ref[here, :] = own
 
 
-def load_kernel(rate_hbm, query_hbm, key_hbm, value_hbm, *refs, zp, ne, mirror, heads, blocks, order, early):
+def load_kernel(rate_hbm, query_hbm, key_hbm, value_hbm, *refs, zp, ne, mirror, heads, blocks, order, early, ways):
     rates_ref, query_ref, key_ref, value_ref = refs[:4]
     states, terms, (rate_smem, sems) = refs[4 : 4 + early], refs[4 + early : 4 + 2 * early], refs[4 + 2 * early :]
     me = owned(zp, ne, mirror)
@@ -59,7 +64,7 @@
 
     def copy_of(n, d):
         source, held = ((key_hbm, key_ref), (value_hbm, value_ref), (query_hbm, query_ref))[n]
-        cols = pl.ds(pl.multiple_of((me ^ d) * part, part), part)
+        cols = pl.ds(pl.multiple_of((me ^ away(ways[d])) * part, part), part)
         return pltpu.make_async_copy(source.at[:, cols], held.at[d], sems.at[n, d])
 
     rate_copy = pltpu.make_async_copy(rate_hbm, rate_smem, sems.at[3, 0])
@@ -72,7 +77,7 @@
     rate_copy.wait()
     for d in order:
         for h in range(heads):
-            rates_ref[d, h] = jnp.full((8, HEAD_DIM), rate_smem[(me ^ d) * heads + h], F32)
+            rates_ref[d, h] = jnp.full((8, HEAD_DIM), rate_smem[(me ^ away(ways[d])) * heads + h], F32)
     for i, d in enumerate(order):
         copy_of(0, d).wait()
         copy_of(1, d).wait()
@@ -114,7 +119,7 @@
     return jnp.where(gap >= 0, jnp.exp(-rate * (jnp.maximum(gap, 0).astype(F32) * span)), 0.0)
 
 
-def total_kernel(rates_ref, after_ref, *refs, ring, heads, span, zp, ne):
+def total_kernel(rates_ref, after_ref, *refs, ring, heads, span, zp, ne, ways):
     group = len(ring)
     slots, out = refs[:group], refs[group]
     me = member(zp, ne)
@@ -122,12 +127,12 @@
         rate = rates_ref[0, h][:1, :]
         total = None
         for e, slot in zip(ring, slots):
-            part = span_weight(rate, group - 1 - (me ^ e), span) * slot[head_rows(h), :]
+            part = span_weight(rate, group - 1 - (me ^ away(ways[e])), span) * slot[head_rows(h), :]
             total = part if total is None else total + part
         out[head_rows(h), :] = total
 
 
-def carry_kernel(rates_ref, before_ref, *refs, ring, ring_out, heads, span, zp, ne):
+def carry_kernel(rates_ref, before_ref, *refs, ring, ring_out, heads, span, zp, ne, ways):
     group = len(ring)
     slots, outs = refs[:group], refs[group:]
     me = member(zp, ne)
@@ -137,10 +142,11 @@
         parts = [slot[head_rows(h), :] for slot in slots]
         before = jnp.where(has_before, before_ref[head_rows(h), :], 0.0)
         for d, out in zip(ring_out, outs):
-            carry = span_weight(rate, me ^ d, span) * before
+            at = me ^ away(ways[d])
+            carry = span_weight(rate, at, span) * before
             for e, part in zip(ring, parts):
                 if e != d:
-                    carry = carry + span_weight(rate, (me ^ d) - (me ^ e) - 1, span) * part
+                    carry = carry + span_weight(rate, at - (me ^ away(ways[e])) - 1, span) * part
             out[head_rows(h), :] = carry
 
 
@@ -176,7 +182,7 @@
             acc_ref[rows, :] = square
 
 
-def norm_kernel(*refs, features, count, steps, ring, zp, ne, mirror, heads):
+def norm_kernel(*refs, features, count, steps, ring, zp, ne, mirror, heads, ways):
     squares, gain_ref, refs = refs[:count], refs[count], refs[count + 1 :]
     atts, (out_hbm, out_ref, sems) = refs[: len(ring)], refs[len(ring) :]
     me = owned(zp, ne, mirror)
@@ -192,7 +198,7 @@
         column = jnp.concatenate([jnp.transpose(jnp.broadcast_to(tile, (HEAD_DIM, HEAD_DIM))) for tile in tiles], axis=0)
         for att, d in zip(atts, ring):
             for h in range(heads):
-                cols = pl.ds(pl.multiple_of(((me ^ d) * heads + h) * HEAD_DIM, HEAD_DIM), HEAD_DIM)
+                cols = pl.ds(pl.multiple_of(((me ^ away(ways[d])) * heads + h) * HEAD_DIM, HEAD_DIM), HEAD_DIM)
                 out_ref[rows, cols] = (att[rows, head_rows(h)] * column * gain_ref[:, cols]).astype(BF16)
         copies.append(pltpu.make_async_copy(out_ref.at[rows, :], out_hbm.at[rows, :], sems.at[step]))
         copies[-1].start()
@@ -212,8 +218,11 @@
     vmem = pl.BlockSpec(memory_space=pltpu.VMEM)
     hbm = pl.BlockSpec(memory_space=pltpu.HBM)
     anywhere = pl.BlockSpec(memory_space=pl.ANY)
-    ring = (0, 2, 1, 3) if group == 4 else tuple(range(group))
-    ring3 = (0, 3, 2, 1) if group == 4 else tuple(range(group))
+    if group == 4:
+        ways, ring, ring3, order = ((0, 0), (1, 3), (2, 1), (3, 2)), (0, 1, 2, 3), (0, 1, 3, 2), (3, 2, 1, 0)
+    else:
+        ways, ring = tuple((d, d) for d in range(group)), tuple(range(group))
+        ring3, order = ring, ring[1:] + ring[:1]
     state_type = jax.ShapeDtypeStruct((part, HEAD_DIM), F32)
     term_type = jax.ShapeDtypeStruct((max(blocks - 1, 1), part, HEAD_DIM), F32)
     held_type = jax.ShapeDtypeStruct((group, rows, part), BF16)
@@ -225,10 +234,9 @@
         return pl.pallas_call(kernel, compiler_params=params(), **more)
 
     pinned = [pltpu.with_memory_space_constraint(a, pltpu.HBM) for a in (decay_rate, queries, key_vectors, value_vectors)]
-    order = (3, 2, 1, 0) if group == 4 else ring[1:] + ring[:1]
     early = min(3, group)
     rates, query, key, value, *rest = call(
-        functools.partial(load_kernel, heads=heads, blocks=blocks, order=order, mirror=mirror, early=early, **where),
+        functools.partial(load_kernel, heads=heads, blocks=blocks, order=order, mirror=mirror, early=early, ways=ways, **where),
         4,
         [jax.ShapeDtypeStruct((group, heads, 8, HEAD_DIM), F32), held_type, held_type, held_type]
         + [state_type] * early
@@ -247,9 +255,11 @@
         pairs = []
         for zz in range(nc):
             for xx in range(ne):
-                m = ((zz % zp) * ne + xx) ^ d
-                pairs.append((zz * ne + xx, (zz // zp * zp + m // ne) * ne + m % ne))
-        return lax.ppermute(value, ("ctx", "exp"), pairs)
+                for tt in range(nt):
+                    m = ((zz % zp) * ne + xx) ^ ways[d][tt % 2]
+                    to = (zz // zp * zp + m // ne) * ne + m % ne
+                    pairs.append(((zz * ne + xx) * nt + tt, to * nt + tt))
+        return lax.ppermute(value, ("ctx", "exp", "tp"), pairs)
 
     slots = [slots[0]] + [swap(slots[d], d) for d in ring[1:]]
 
@@ -262,7 +272,7 @@
     )(rates, query, key, value)
 
     (total,) = call(
-        functools.partial(total_kernel, ring=ring, heads=heads, span=span, **where),
+        functools.partial(total_kernel, ring=ring, ways=ways, heads=heads, span=span, **where),
         group + 2,
         [state_type],
         "group_total",
@@ -281,7 +291,7 @@
         step *= 2
 
     carries = call(
-        functools.partial(carry_kernel, ring=ring, ring_out=ring3, heads=heads, span=span, **where), group + 2, [state_type] * group, "carry"
+        functools.partial(carry_kernel, ring=ring, ways=ways, ring_out=ring3, heads=heads, span=span, **where), group + 2, [state_type] * group, "carry"
     )(rates, before, *slots)
     carries = [carries[0]] + [swap(carry, d) for carry, d in zip(carries[1:], ring3[1:])]
 
@@ -303,7 +313,7 @@
     row_sums = [row_sum] + [lax.ppermute(row_sum, "tp", pairs) for pairs in swaps]
 
     steps = 4
-    norm = functools.partial(norm_kernel, features=float(width * nt), count=nt, steps=steps, ring=ring3, heads=heads, mirror=mirror, **where)
+    norm = functools.partial(norm_kernel, features=float(width * nt), count=nt, steps=steps, ring=ring3, heads=heads, mirror=mirror, ways=ways, **where)
     (out,) = call(
         norm,
         nt + 1 + group,

time: 33.5 us -> 33.3 us (level)
  waiting for transfers between devices: 11.7 us -> 11.1 us
    ppermute x1, waiting for transfers between devices: 3.67 us -> 3.26 us  [local(): lax.ppermute(total, 'ctx', [(zz, nc - 1 - zz if mirror else (zz + zp) % n...]
    ppermute x1, starting transfers between devices: 3.27 us -> 3.68 us  [local(): lax.ppermute(total, 'ctx', [(zz, nc - 1 - zz if mirror else (zz + zp) % n...]
  transfers between devices with their start and end apart: 10 -> 10, of which waited for: 7 -> 9; matrix products, arithmetic and copies ran while one was open for 0% -> 0% of each run, Pallas kernels for 13% -> 13%
where the time goes in v6:
time: 33.3 us; the launch traced here: 33.1 us
  starting transfers between devices  13.7 us (41%)
  waiting for transfers between devices  11.1 us (33%)
  Pallas kernels  8.17 us (25%)
    ppermute x6, starting transfers between devices, swap(): return lax.ppermute(value, ('ctx', 'exp', 'tp'), pairs)  8.14 us
    ppermute x6, waiting for transfers between devices, swap(): return lax.ppermute(value, ('ctx', 'exp', 'tp'), pairs)  6.08 us
    ppermute x1, starting transfers between devices, local(): lax.ppermute(total, 'ctx', [(zz, nc - 1 - zz if mirror else (zz + zp) % n...  3.68 us
    pallas_call x1, Pallas kernels, local(): call(functools.partial(local_kernel, blocks=blocks, heads=heads, group=gr...  3.36 us
    ppermute x1, waiting for transfers between devices, local(): lax.ppermute(total, 'ctx', [(zz, nc - 1 - zz if mirror else (zz + zp) % n...  3.26 us
    pallas_call x1, Pallas kernels, local(): call(functools.partial(load_kernel, heads=heads, blocks=blocks, order=ord...  2.05 us
    ppermute x3, starting transfers between devices, local(): lax.ppermute(row_sum, 'tp', pairs)  1.92 us
    ppermute x3, waiting for transfers between devices, local(): lax.ppermute(row_sum, 'tp', pairs)  1.8 us
  transfers between devices with their start and end apart: 10, of which 9 were waited for; matrix products, arithmetic and copies ran while one was open for 0% of the time, Pallas kernels for 13%

profile of v6, /device:TPU:0, one launch (start us, length us, event | category | flops | bytes accessed | tf_op | source)
XLA Modules:
  0.0 33.1 jit_solution(2241893000423667389)
XLA Ops:
  0.0 2.1 %load.1 = (f32[4,2,8,128]{3,2,1,0:T(8,128)S(1)}, bf16[4,512,256]{2,1,0:T(8,128)(2,1)S(1)}, bf16[4,512,256]{2,1,0:T(8,128)(2,1)S(1)}, bf16[4,512,256]{2,1,0:T(8,1...) custom-call(f32[8]{0:T(128)} %rate_hbm.1, ...), custom_call_target="tpu_custom_call" | custom-call | tf_op jit(solution)/shard_map/load/pallas_call | solution.py:238
  2.1 3.0 %collective-permute-start = (f32[256,128]{1,0:T(8,128)S(1)}, f32[256,128]{1,0:T(8,128)S(1)}, u32[]{:S(2)}, u32[]{:S(2)}) collective-permute-start(f32[256,128]{1,0:T(8,128)S(1)} %get-tuple-element.39), channel_id=1, source_target_pairs={{0,4},{1,13},{2,6},{3,15},{4,0},{5,9},{6,2},{7,11},{8,12},{9,5},{1... | collective-permute-start | bytes 393224 | tf_op jit(solution)/shard_map/ppermute | solution.py:262
  5.1 1.6 %collective-permute-start.1 = (f32[256,128]{1,0:T(8,128)S(1)}, f32[256,128]{1,0:T(8,128)S(1)}, u32[]{:S(2)}, u32[]{:S(2)}) collective-permute-start(f32[256,128]{1,0:T(8,128)S(1)} %get-tuple-element.40), channel_id=1, source_target_pairs={{0,8},{1,5},{2,10},{3,7},{4,12},{5,1},{6,14},{7,3},{8,0},{9,13},{1... | collective-permute-start | bytes 393224 | tf_op jit(solution)/shard_map/ppermute | solution.py:262
  6.6 0.0 collective-permute-start.2
  6.6 0.3 spread.1
  6.9 3.4 %local_part.1 = (f32[4,512,256]{2,1,0:T(8,128)S(1)}, f32[4,2,256,128]{3,2,1,0:T(8,128)S(1)}) custom-call(f32[4,2,8,128]{3,2,1,0:T(8,128)S(1)} %get-tuple-element.31.rates_ref, bf16[4,512,256]{2,1,0:T(8,128)(2,1)S(1)} %get-tuple-element.32.query_ref, bf16[4,512,256]{2,1,0:T(8,128)(2,1)S(1)} %get-tuple-element.33.key_ref, ...), custom_call_target="tpu_custom_call" | custom-call | flops 536870912 | bytes 5242880 | tf_op jit(solution)/shard_map/local_part/pallas_call | solution.py:266
  10.3 0.3 collective-permute-done.refs_1_
  10.6 0.7 %collective-permute-done.1.refs_2_ = f32[256,128]{1,0:T(8,128)S(1)} collective-permute-done((f32[256,128]{1,0:T(8,128)S(1)}, f32[256,128]{1,0:T(8,128)S(1)}, u32[]{:S(2)}, u32[]{:S(2)}) %collective-permute-start.1) | collective-permute-done | bytes 131104 | tf_op jit(solution)/shard_map/ppermute | solution.py:262
  11.3 1.2 %collective-permute-done.2.refs_3_ = f32[256,128]{1,0:T(8,128)S(1)} collective-permute-done((f32[256,128]{1,0:T(8,128)S(1)}, f32[256,128]{1,0:T(8,128)S(1)}, u32[]{:S(2)}, u32[]{:S(2)}) %collective-permute-start.2) | collective-permute-done | bytes 131104 | tf_op jit(solution)/shard_map/ppermute | solution.py:262
  12.5 0.1 group_total.1
  12.6 3.7 %collective-permute-start.3 = (f32[256,128]{1,0:T(8,128)S(1)}, f32[256,128]{1,0:T(8,128)S(1)}, u32[]{:S(2)}, u32[]{:S(2)}) collective-permute-start(f32[256,128]{1,0:T(8,128)S(1)} %group_total.1), channel_id=1, source_target_pairs={{0,24},{8,16},{16,8},{24,0},{1,25},{9,17},{17,9},{25,1},{2,26},{10... | collective-permute-start | bytes 393224 | tf_op jit(solution)/shard_map/ppermute | solution.py:283
  16.2 3.3 %collective-permute-done.3.before_ref = f32[256,128]{1,0:T(8,128)S(1)} collective-permute-done((f32[256,128]{1,0:T(8,128)S(1)}, f32[256,128]{1,0:T(8,128)S(1)}, u32[]{:S(2)}, u32[]{:S(2)}) %collective-permute-start.3) | collective-permute-done | bytes 131104 | tf_op jit(solution)/shard_map/ppermute | solution.py:283
  19.5 0.2 carry.1
  19.7 1.7 %collective-permute-start.6 = (f32[256,128]{1,0:T(8,128)S(1)}, f32[256,128]{1,0:T(8,128)S(1)}, u32[]{:S(2)}, u32[]{:S(2)}) collective-permute-start(f32[256,128]{1,0:T(8,128)S(1)} %get-tuple-element.46), channel_id=1, source_target_pairs={{0,4},{1,13},{2,6},{3,15},{4,0},{5,9},{6,2},{7,11},{8,12},{9,5},{1... | collective-permute-start | bytes 393224 | tf_op jit(solution)/shard_map/ppermute | solution.py:262
  21.4 1.5 %collective-permute-start.5 = (f32[256,128]{1,0:T(8,128)S(1)}, f32[256,128]{1,0:T(8,128)S(1)}, u32[]{:S(2)}, u32[]{:S(2)}) collective-permute-start(f32[256,128]{1,0:T(8,128)S(1)} %get-tuple-element.44), channel_id=1, source_target_pairs={{0,12},{1,9},{2,14},{3,11},{4,8},{5,13},{6,10},{7,15},{8,4},{9,1},... | collective-permute-start | bytes 393224 | tf_op jit(solution)/shard_map/ppermute | solution.py:262
  22.9 0.4 %collective-permute-start.4 = (f32[256,128]{1,0:T(8,128)S(1)}, f32[256,128]{1,0:T(8,128)S(1)}, u32[]{:S(2)}, u32[]{:S(2)}) collective-permute-start(f32[256,128]{1,0:T(8,128)S(1)} %get-tuple-element.42), channel_id=1, source_target_pairs={{0,8},{1,5},{2,10},{3,7},{4,12},{5,1},{6,14},{7,3},{8,0},{9,13},{1... | collective-permute-start | bytes 393224 | tf_op jit(solution)/shard_map/ppermute | solution.py:262
  23.2 0.2 carried.4
  23.5 2.5 %collective-permute-done.6.carry_ref = f32[256,128]{1,0:T(8,128)S(1)} collective-permute-done((f32[256,128]{1,0:T(8,128)S(1)}, f32[256,128]{1,0:T(8,128)S(1)}, u32[]{:S(2)}, u32[]{:S(2)}) %collective-permute-start.6) | collective-permute-done | bytes 131104 | tf_op jit(solution)/shard_map/ppermute | solution.py:262
  26.0 0.2 carried.5
  26.3 1.0 %collective-permute-done.5.carry_ref = f32[256,128]{1,0:T(8,128)S(1)} collective-permute-done((f32[256,128]{1,0:T(8,128)S(1)}, f32[256,128]{1,0:T(8,128)S(1)}, u32[]{:S(2)}, u32[]{:S(2)}) %collective-permute-start.5) | collective-permute-done | bytes 131104 | tf_op jit(solution)/shard_map/ppermute | solution.py:262
  27.3 0.2 carried.6
  27.5 0.3 %collective-permute-done.4.carry_ref = f32[256,128]{1,0:T(8,128)S(1)} collective-permute-done((f32[256,128]{1,0:T(8,128)S(1)}, f32[256,128]{1,0:T(8,128)S(1)}, u32[]{:S(2)}, u32[]{:S(2)}) %collective-permute-start.4) | collective-permute-done | bytes 131104 | tf_op jit(solution)/shard_map/ppermute | solution.py:262
  27.8 0.0 copy-start
  27.8 0.3 %carried.7 = (f32[512,256]{1,0:T(8,128)S(1)}, f32[1,512]{1,0:T(1,128)S(1)}) custom-call(f32[4,2,8,128]{3,2,1,0:T(8,128)S(1)} %get-tuple-element.31.rates_ref, bf16[4,512,256]{2,1,0:T(8,128)(2,1)S(1)} %get-tuple-element.32.query_ref, f32[4,512,256]{2,1,0:T(8,128)S(1)} %get-tuple-element.35.local_ref, ...), custom_call_target="tpu_custom_call" | custom-call | tf_op jit(solution)/shard_map/carried/pallas_call | solution.py:301
  28.2 0.1 collective-permute-start.9
  28.3 1.6 %collective-permute-start.8 = (f32[1,512]{1,0:T(1,128)S(1)}, f32[1,512]{1,0:T(1,128)S(1)}, u32[]{:S(2)}, u32[]{:S(2)}) collective-permute-start(f32[1,512]{1,0:T(1,128)S(1)} %get-tuple-element.52.refs_0_), channel_id=1, source_target_pairs={{0,2},{1,3},{2,0},{3,1},{4,6},{5,7},{6,4},{7,5},{8,10},{9,11},{10,... | collective-permute-start | bytes 6152 | tf_op jit(solution)/shard_map/ppermute | solution.py:313
  29.9 0.2 collective-permute-start.7
  30.1 1.1 %collective-permute-done.9.refs_3_ = f32[1,512]{1,0:T(1,128)S(1)} collective-permute-done((f32[1,512]{1,0:T(1,128)S(1)}, f32[1,512]{1,0:T(1,128)S(1)}, u32[]{:S(2)}, u32[]{:S(2)}) %collective-permute-start.9) | collective-permute-done | bytes 2080 | tf_op jit(solution)/shard_map/ppermute | solution.py:313
  31.3 0.7 %collective-permute-done.8.refs_2_ = f32[1,512]{1,0:T(1,128)S(1)} collective-permute-done((f32[1,512]{1,0:T(1,128)S(1)}, f32[1,512]{1,0:T(1,128)S(1)}, u32[]{:S(2)}, u32[]{:S(2)}) %collective-permute-start.8) | collective-permute-done | bytes 2080 | tf_op jit(solution)/shard_map/ppermute | solution.py:313
  31.9 0.0 collective-permute-done.7.refs_1_
  31.9 0.0 copy-done
  31.9 1.2 %norm.1 = bf16[512,1024]{1,0:T(8,128)(2,1)} custom-call(f32[1,512]{1,0:T(1,128)S(1)} %get-tuple-element.52.refs_0_, f32[1,512]{1,0:T(1,128)S(1)} %collective-permute-done.7.refs_1_, f32[1,512]{1,0:T(1,128)S(1)} %collective-permute-done.8.refs_2_, f32[1,512]{1,0:T(1,128)S(1)} %collective-permute-done.9.refs_3_, f32[1,1024]{1,0:T(1,128)S(1)} %bitcast.1, ...), custom_call_target="tpu_custom_call" | custom-call | tf_op jit(solution)/shard_map/norm/pallas_call | solution.py:317
Async XLA Ops:
  2.1 8.5 %collective-permute-start = (f32[256,128]{1,0:T(8,128)S(1)}, f32[256,128]{1,0:T(8,128)S(1)}, u32[]{:S(2)}, u32[]{:S(2)}) collective-permute-start(f32[256,128]{1,0:T(8,128)S(1)} %get-tuple-element.39), channel_id=1, source_target_pairs={{0,4},{1,13},{2,6},{3,15},{4,0},{5,9},{6,2},{7,11},{8,12},{9,5},{1... | collective-permute-start | bytes 393224 | tf_op jit(solution)/shard_map/ppermute | solution.py:262
  5.1 6.2 %collective-permute-start.1 = (f32[256,128]{1,0:T(8,128)S(1)}, f32[256,128]{1,0:T(8,128)S(1)}, u32[]{:S(2)}, u32[]{:S(2)}) collective-permute-start(f32[256,128]{1,0:T(8,128)S(1)} %get-tuple-element.40), channel_id=1, source_target_pairs={{0,8},{1,5},{2,10},{3,7},{4,12},{5,1},{6,14},{7,3},{8,0},{9,13},{1... | collective-permute-start | bytes 393224 | tf_op jit(solution)/shard_map/ppermute | solution.py:262
  6.6 5.9 %collective-permute-start.2 = (f32[256,128]{1,0:T(8,128)S(1)}, f32[256,128]{1,0:T(8,128)S(1)}, u32[]{:S(2)}, u32[]{:S(2)}) collective-permute-start(f32[256,128]{1,0:T(8,128)S(1)} %get-tuple-element.41), channel_id=1, source_target_pairs={{0,12},{1,9},{2,14},{3,11},{4,8},{5,13},{6,10},{7,15},{8,4},{9,1},... | collective-permute-start | bytes 393224 | tf_op jit(solution)/shard_map/ppermute | solution.py:262
  12.6 6.9 %collective-permute-start.3 = (f32[256,128]{1,0:T(8,128)S(1)}, f32[256,128]{1,0:T(8,128)S(1)}, u32[]{:S(2)}, u32[]{:S(2)}) collective-permute-start(f32[256,128]{1,0:T(8,128)S(1)} %group_total.1), channel_id=1, source_target_pairs={{0,24},{8,16},{16,8},{24,0},{1,25},{9,17},{17,9},{25,1},{2,26},{10... | collective-permute-start | bytes 393224 | tf_op jit(solution)/shard_map/ppermute | solution.py:283
  19.7 6.3 %collective-permute-start.6 = (f32[256,128]{1,0:T(8,128)S(1)}, f32[256,128]{1,0:T(8,128)S(1)}, u32[]{:S(2)}, u32[]{:S(2)}) collective-permute-start(f32[256,128]{1,0:T(8,128)S(1)} %get-tuple-element.46), channel_id=1, source_target_pairs={{0,4},{1,13},{2,6},{3,15},{4,0},{5,9},{6,2},{7,11},{8,12},{9,5},{1... | collective-permute-start | bytes 393224 | tf_op jit(solution)/shard_map/ppermute | solution.py:262
  21.4 5.9 %collective-permute-start.5 = (f32[256,128]{1,0:T(8,128)S(1)}, f32[256,128]{1,0:T(8,128)S(1)}, u32[]{:S(2)}, u32[]{:S(2)}) collective-permute-start(f32[256,128]{1,0:T(8,128)S(1)} %get-tuple-element.44), channel_id=1, source_target_pairs={{0,12},{1,9},{2,14},{3,11},{4,8},{5,13},{6,10},{7,15},{8,4},{9,1},... | collective-permute-start | bytes 393224 | tf_op jit(solution)/shard_map/ppermute | solution.py:262
  22.9 5.0 %collective-permute-start.4 = (f32[256,128]{1,0:T(8,128)S(1)}, f32[256,128]{1,0:T(8,128)S(1)}, u32[]{:S(2)}, u32[]{:S(2)}) collective-permute-start(f32[256,128]{1,0:T(8,128)S(1)} %get-tuple-element.42), channel_id=1, source_target_pairs={{0,8},{1,5},{2,10},{3,7},{4,12},{5,1},{6,14},{7,3},{8,0},{9,13},{1... | collective-permute-start | bytes 393224 | tf_op jit(solution)/shard_map/ppermute | solution.py:262
  27.8 4.1 %copy-start = (f32[1024]{0:T(1024)S(1)}, f32[1024]{0:T(1024)}, u32[]{:S(2)}) copy-start(f32[1024]{0:T(1024)} %param.9) | copy-start | bytes 12292
  28.2 3.1 %collective-permute-start.9 = (f32[1,512]{1,0:T(1,128)S(1)}, f32[1,512]{1,0:T(1,128)S(1)}, u32[]{:S(2)}, u32[]{:S(2)}) collective-permute-start(f32[1,512]{1,0:T(1,128)S(1)} %get-tuple-element.52.refs_0_), channel_id=1, source_target_pairs={{0,3},{1,2},{2,1},{3,0},{4,7},{5,6},{6,5},{7,4},{8,11},{9,10},{10,... | collective-permute-start | bytes 6152 | tf_op jit(solution)/shard_map/ppermute | solution.py:313
  28.3 3.7 %collective-permute-start.8 = (f32[1,512]{1,0:T(1,128)S(1)}, f32[1,512]{1,0:T(1,128)S(1)}, u32[]{:S(2)}, u32[]{:S(2)}) collective-permute-start(f32[1,512]{1,0:T(1,128)S(1)} %get-tuple-element.52.refs_0_), channel_id=1, source_target_pairs={{0,2},{1,3},{2,0},{3,1},{4,6},{5,7},{6,4},{7,5},{8,10},{9,11},{10,... | collective-permute-start | bytes 6152 | tf_op jit(solution)/shard_map/ppermute | solution.py:313
  29.9 2.0 %collective-permute-start.7 = (f32[1,512]{1,0:T(1,128)S(1)}, f32[1,512]{1,0:T(1,128)S(1)}, u32[]{:S(2)}, u32[]{:S(2)}) collective-permute-start(f32[1,512]{1,0:T(1,128)S(1)} %get-tuple-element.52.refs_0_), channel_id=1, source_target_pairs={{0,1},{1,0},{2,3},{3,2},{4,5},{5,4},{6,7},{7,6},{8,9},{9,8},{10,11... | collective-permute-start | bytes 6152 | tf_op jit(solution)/shard_map/ppermute | solution.py:313
